TPU v7x, 256 devices: a whole 4x4x8 slice. The times are simulated.
256 devices in a mesh: row: 2 (over core), pitch: 32 (over z, y), rad: 4 (over x).
Axes of the slice: x: 4, y: 4, z: 8, core: 2. Of those that a mesh axis runs over, the one named last changes fastest.
Arguments:
- flow_field: float32 [2, 5, 8, 256, 4096], P('row', None, None, 'rad', 'pitch'), may hold values from -6 to 6
- inflow: float32 [2, 5, 256, 4096], P('row', None, 'rad', 'pitch'), may hold values from -6 to 6
- flux_jacobian: float32 [2, 3, 5, 5], P('row'), may hold values from -2.5 to 2.5
- sweep_jacobian: float32 [2, 2, 5, 5], P('row'), may hold values from -2.5 to 2.5
- mode_index: int32 [2, 4, 128], replicated, may hold values from -32 to 32
- destination: int32 [2, 512, 1], replicated, may hold values from 0 to 31; in each aligned block of 512 rows (0 to 511, 512 to 1023, ..., all dimensions but the last counted through in order) at most 48 rows name the same one
Outputs:
- next_flow: float32 [2, 5, 8, 256, 4096], P('row', None, None, 'rad', 'pitch')
- response: float32 [2, 32, 48, 2, 5, 256], P('row', 'pitch', None, None, None, 'rad')
Inputs may be any that keep to these rules, and one draw needn't show every extreme that they name: At most 48 of one blade row's modes name the same destination, and 48 is reached in every draw.
All inputs are finite; a program needn't handle non-finite values.
Results may differ from a plain program's by a relative error of at most 0.0003.
Values sent between devices are 32-bit elements; how exact they have to be, the bound alone decides.
No kernel may reach another device: no remote copies, remote signals or barrier semaphores. Data moves between devices by JAX's collectives and lax.ppermute only.
A program may use at most 64 MiB of HBM per device.

v0:
```python
import math

import jax
import jax.numpy as jnp
from jax import lax
from jax.sharding import PartitionSpec as P

FIELDS = 5
BLADES = 22
VANES = 54
PITCH_DEV = 128
RAD_DEV = 64
MODES = 512


PRECISE = lax.Precision.HIGHEST
FLUX_PITCH = 0.25
FLUX_RAD = 0.25
FLUX_AXIAL = 0.5
FLUX_DIFFUSE = 0.1
SWEEP_DIFFUSE = 0.5
CENTRE_WEIGHT = 2.0
RELAX = 0.7
OMEGA = 0.05
KAPPA = 2.0


def extended(block, sides, width, periodic):
    for axis, dim in sides:
        count = lax.axis_size(axis)
        forward = [(i, i + 1) for i in range(count - 1)]
        if periodic:
            forward.append((count - 1, 0))
        backward = [(target, source) for source, target in forward]
        low = lax.ppermute(
            lax.slice_in_dim(block, block.shape[dim] - width, None, axis=dim), axis, forward
        )
        high = lax.ppermute(lax.slice_in_dim(block, 0, width, axis=dim), axis, backward)
        block = jnp.concatenate([low, block, high], axis=dim)
    return block


def partner(value, axis, distance):
    mask = 2**distance
    pairs = [(source, source ^ mask) for source in range(lax.axis_size(axis))]
    return lax.ppermute(value, axis, pairs)


def flux_step(state_now, inflow_face, jacobian, pitch_plus, pitch_minus, rad_plus, rad_minus):
    behind = jnp.concatenate([inflow_face[:, None], state_now[:, :-1]], axis=1)
    laplace = pitch_plus + pitch_minus + rad_plus + rad_minus - 4.0 * state_now
    flux_sum = FLUX_PITCH * jnp.einsum(
        "gf,fzrp->gzrp", jacobian[0], pitch_plus - pitch_minus, precision=PRECISE
    )
    flux_sum = flux_sum + FLUX_RAD * jnp.einsum(
        "gf,fzrp->gzrp", jacobian[1], rad_plus - rad_minus, precision=PRECISE
    )
    flux_sum = flux_sum + FLUX_AXIAL * jnp.einsum(
        "gf,fzrp->gzrp", jacobian[2], state_now - behind, precision=PRECISE
    )
    return state_now - flux_sum + FLUX_DIFFUSE * laplace


def row_tables(mode_index, destination, row_id, slot_count, capacity):
    index_row = lax.dynamic_index_in_dim(mode_index, row_id, 0, keepdims=False)
    dest_row = lax.dynamic_index_in_dim(destination, row_id, 0, keepdims=False)[:, 0]
    passing = jnp.where(row_id == 0, BLADES, VANES).astype(jnp.int32)
    opposing = jnp.where(row_id == 0, VANES, BLADES).astype(jnp.int32)
    harmonic = jnp.arange(1, index_row.shape[0] + 1, dtype=jnp.int32)[:, None] * jnp.ones_like(
        index_row
    )
    orders = (harmonic * passing - index_row * opposing).reshape(-1)
    harmonic = harmonic.reshape(-1)
    mode_count = orders.shape[0]
    earlier = (
        jnp.arange(mode_count, dtype=jnp.int32)[None, :]
        < jnp.arange(mode_count, dtype=jnp.int32)[:, None]
    )
    same_dest = dest_row[None, :] == dest_row[:, None]
    rank_before = jnp.sum((earlier & same_dest).astype(jnp.int32), axis=1)
    target = dest_row * capacity + rank_before
    select = (target[None, :] == jnp.arange(slot_count, dtype=jnp.int32)[:, None]).astype(jnp.int32)
    slot_orders = jnp.sum(select * orders[None, :], axis=1)
    slot_harm = jnp.sum(select * harmonic[None, :], axis=1)
    filled = jnp.sum(select, axis=1)
    return (orders, harmonic, target, slot_orders, slot_harm, filled, select, passing)


def phase_table(orders, weights, positions, pitch_total):
    phase_index = jnp.mod(orders[:, None] * positions[None, :], pitch_total)
    angles = phase_index.astype(jnp.float32) * (2.0 * math.pi / pitch_total)
    scaling = weights.astype(jnp.float32) / math.sqrt(pitch_total)
    return (jnp.cos(angles) * scaling[:, None], -jnp.sin(angles) * scaling[:, None])


def transform(cosine, sine_part, exit_face):
    real_part = jnp.einsum("sp,cp->sc", cosine, exit_face, precision=PRECISE)
    imag_part = jnp.einsum("sp,cp->sc", sine_part, exit_face, precision=PRECISE)
    return jnp.stack([real_part, imag_part], axis=1)


def wrapped(orders, pitch_total):
    return jnp.mod(orders + pitch_total // 2, pitch_total) - pitch_total // 2


def operate(widened, freq_term, wave_term, twist_map, radial):
    centre = widened[..., 1:-1]
    outer_side = widened[..., 2:]
    inner_side = widened[..., :-2]
    turned_re = jnp.einsum("gf,sfr->sgr", twist_map, centre[:, 0], precision=PRECISE)
    turned_im = jnp.einsum("gf,sfr->sgr", twist_map, centre[:, 1], precision=PRECISE)
    grade_re = jnp.einsum(
        "gf,sfr->sgr", radial, outer_side[:, 0] - inner_side[:, 0], precision=PRECISE
    )
    grade_im = jnp.einsum(
        "gf,sfr->sgr", radial, outer_side[:, 1] - inner_side[:, 1], precision=PRECISE
    )
    sig_col = freq_term[:, None, None]
    wave_col = wave_term[:, None, None]
    out_re = (
        CENTRE_WEIGHT * centre[:, 0]
        - SWEEP_DIFFUSE * (outer_side[:, 0] + inner_side[:, 0])
        - sig_col * centre[:, 1]
        - wave_col * turned_im
        + 0.5 * grade_re
    )
    out_im = (
        CENTRE_WEIGHT * centre[:, 1]
        - SWEEP_DIFFUSE * (outer_side[:, 1] + inner_side[:, 1])
        + sig_col * centre[:, 0]
        + wave_col * turned_re
        + 0.5 * grade_im
    )
    return (out_re, out_im)


def relax_step(centre, target, applied, freq_term):
    resid_real = target[:, 0] - applied[0]
    resid_imag = target[:, 1] - applied[1]
    sig_col = freq_term[:, None, None]
    denominator = CENTRE_WEIGHT * CENTRE_WEIGHT + sig_col * sig_col
    new_re = (
        centre[:, 0] + RELAX * (CENTRE_WEIGHT * resid_real + sig_col * resid_imag) / denominator
    )
    new_im = (
        centre[:, 1] + RELAX * (CENTRE_WEIGHT * resid_imag - sig_col * resid_real) / denominator
    )
    return jnp.stack([new_re, new_im], axis=1)


def sweeps(amplitude, freq_term, wave_term, twist_map, radial):
    current = amplitude
    for repeat_no in range(2):
        widened = extended(current, (("rad", 3),), 1, False)
        current = relax_step(
            current, amplitude, operate(widened, freq_term, wave_term, twist_map, radial), freq_term
        )
    return current


def on_device(flow_field, inflow, flux_jacobian, sweep_jacobian, mode_index, destination):
    pitch_count = lax.axis_size("pitch")
    capacity = 3 * MODES // pitch_count
    slot_count = pitch_count * capacity
    pitch_total = PITCH_DEV * pitch_count
    row_id = lax.axis_index("row")
    pitch_id = lax.axis_index("pitch")
    state_now = flow_field[0]
    side_halo = extended(state_now, (("pitch", 3),), 1, True)
    rad_halo = extended(state_now, (("rad", 2),), 1, False)
    next_state = flux_step(
        state_now,
        inflow[0],
        flux_jacobian[0],
        side_halo[..., 2:],
        side_halo[..., :-2],
        rad_halo[:, :, 2:],
        rad_halo[:, :, :-2],
    )
    exit_face = next_state[:, -1].reshape(FIELDS * RAD_DEV, PITCH_DEV)
    own_tables = row_tables(mode_index, destination, row_id, slot_count, capacity)
    other_tables = row_tables(mode_index, destination, 1 - row_id, slot_count, capacity)
    positions = pitch_id * PITCH_DEV + jnp.arange(PITCH_DEV, dtype=jnp.int32)
    orders = own_tables[3]
    weights = own_tables[5]
    cosine, sine_part = phase_table(orders, weights, positions, pitch_total)
    spectrum = lax.psum_scatter(
        transform(cosine, sine_part, exit_face), "pitch", scatter_dimension=0, tiled=True
    )
    received = partner(spectrum, "row", 0)
    amplitude = received.reshape(received.shape[0], 2, FIELDS, RAD_DEV)
    orders_in = lax.dynamic_slice_in_dim(other_tables[3], pitch_id * capacity, capacity)
    harm_in = lax.dynamic_slice_in_dim(other_tables[4], pitch_id * capacity, capacity)
    freq_term = OMEGA * harm_in.astype(jnp.float32) * other_tables[7].astype(jnp.float32)
    wave_term = KAPPA * wrapped(orders_in, pitch_total).astype(jnp.float32) / pitch_total
    result = sweeps(amplitude, freq_term, wave_term, sweep_jacobian[0, 0], sweep_jacobian[0, 1])
    response = result.reshape(1, 1, capacity, 2, FIELDS, RAD_DEV)
    return (next_state[None], response)


def solution(mesh):
    placed = (
        P("row", None, None, "rad", "pitch"),
        P("row", None, "rad", "pitch"),
        P("row", None, None, None),
        P("row", None, None, None),
        P(),
        P(),
    )
    return jax.shard_map(
        on_device,
        mesh=mesh,
        in_specs=placed,
        out_specs=(
            P("row", None, None, "rad", "pitch"),
            P("row", "pitch", None, None, None, "rad"),
        ),
        check_vma=False,
    )
```

profile of v0, /device:TPU:4, one launch (start us, length us, event | category | flops | bytes accessed | tf_op | source)
XLA Modules:
  0.0 290.7 jit_solution(1154162816710734578)
XLA Ops:
  7.2 2.1 copy.126
  9.3 3.1 %collective-permute-start.3 = (f32[5,8,1,128]{3,0,2,1:T(8,128)S(1)}, f32[5,8,1,128]{3,0,2,1:T(8,128)S(1)}, u32[]{:S(2)}, u32[]{:S(2)}) collective-permute-start(f32[5,8,1,128]{3,0,2,1:T(8,128)S(1)} %get-tuple-element.20), channel_id=1, source_target_pairs={{0,1},{1,2},{2,3},{4,5},{5,6},{6,7},{8,9},{9,10},{10,11},{12,13},{... | collective-permute-start | bytes 61448 | tf_op jit(solution)/shard_map/ppermute | solution.py:35
  12.4 2.7 collective-permute-start.2
  15.2 2.6 fusion.83
  17.8 2.6 copy.76
  20.4 8.3 %collective-permute-start = (f32[5,8,64,1]{2,1,3,0:T(8,128)}, f32[5,8,64,1]{2,1,3,0:T(8,128)}, u32[]{:S(2)}, u32[]{:S(2)}) collective-permute-start(f32[5,8,64,1]{2,1,3,0:T(8,128)} %copy.76), channel_id=1, source_target_pairs={{4,0},{8,4},{12,8},{16,12},{20,16},{24,20},{28,24},{32,28},{36,32}... | collective-permute-start | bytes 30728 | tf_op jit(solution)/shard_map/ppermute | solution.py:38
  28.8 2.6 copy.78
  31.4 1.3 slice_bitcast_fusion
  35.2 0.8 bitcast_subtract_fusion.5
  36.0 2.6 select_reduce_fusion.1
  39.2 1.7 copy.127
  40.9 5.5 %fusion.1 = f32[8,64,128,5]{2,3,1,0:T(8,128)} fusion(f32[1,5,8,64,128]{4,3,2,1,0:T(8,128)S(1)} %copy-done.4, f32[1,5,7,64,128]{4,1,3,2,0:T(8,128)} %slice_bitcast_fusion, f32[1,5,1,64,128]{4,1,3,2,0:T(8,128)} %bitcast.211, f32[1,1,5,5]{3,0,2,1:T(1,128)S(1)} %get-tuple-element.36), kind=kOutput, calls=%fused_computation.12 | convolution fusion | flops 20316160 | bytes 3932260 | tf_op jit(solution)/shard_map/gf,fzrp->gzrp/dot_general | solution.py:58
  46.4 2.7 copy.79
  49.1 2.7 copy.77
  51.9 2.0 fusion.7
  54.1 6.3 %fusion.6 = f32[5,8,64,128]{3,0,2,1:T(8,128)S(1)} fusion(f32[5,8,64,128]{3,0,2,1:T(8,128)S(1)} %bitcast.205, f32[8,64,128,5]{2,3,1,0:T(8,128)} %fusion.1, f32[8,64,128,5]{2,3,1,0:T(8,128)S(1)} %fusion.7, f32[5,8,64,1]{3,0,2,1:T(8,128)S(1)} %copy-done.1, f32[5,8,64,1]{3,0,2,1:T(8,128)S(1)} %copy-done, f32[5,8,1,128]{3,0,2,1:T(8,128)S(1)} %collective-permute-done.2, ...), kind=kOutput, calls=%fused_computation.21 | convolution fusion | flops 25886720 | bytes 5304420 | tf_op jit(solution)/shard_map/gf,fzrp->gzrp/dot_general | solution.py:52
  60.5 4.7 %convolution_bitcast_fusion = f32[1536,1,320]{0,2,1:T(8,128)S(1)} fusion(f32[320,128]{1,0:T(8,128)S(1)} %bitcast.212, f32[1536]{0:T(1024)S(1)} %copy-done.5, s32[128]{0:T(128)S(1)} %iota_add_fusion, s32[1536]{0:T(1024)S(1)} %copy-done.6), kind=kOutput, calls=%fused_computation.7 | convolution fusion | flops 758120448 | bytes 2142720 | tf_op jit(solution)/shard_map/sp,cp->sc/dot_general | solution.py:98
  65.2 4.7 %convolution_bitcast_fusion.1 = f32[1536,1,320]{0,2,1:T(8,128)S(1)} fusion(f32[320,128]{1,0:T(8,128)S(1)} %bitcast.213, f32[1536]{0:T(1024)S(1)} %copy-done.5, s32[128]{0:T(128)S(1)} %iota_add_fusion, s32[1536]{0:T(1024)S(1)} %copy-done.6), kind=kOutput, calls=%fused_computation.8 | convolution fusion | flops 757923840 | bytes 2142720 | tf_op jit(solution)/shard_map/sp,cp->sc/dot_general | solution.py:97
  69.8 2.2 pad_maximum_fusion
  72.0 7.8 %copy.86 = f32[1536,2,320]{2,1,0:T(2,128)} copy(f32[1536,2,320]{0,2,1:T(8,128)} %pad_maximum_fusion) | data formatting | bytes 7864320 | tf_op jit(solution)/shard_map/stack | solution.py:99
  81.7 164.1 %all-reduce.3.cloned.1.call-done = f32[1536,2,320]{2,1,0:T(2,128)} async-done(((f32[1536,2,320]{2,1,0:T(2,128)}), f32[1536,2,320]{2,1,0:T(2,128)}) %all-reduce.3.cloned.1.call-update) | async-done | bytes 3932176
  245.8 0.9 constant_dynamic-slice_fusion.2
  248.8 3.1 %collective-permute-start.6 = (f32[48,2,5,1]{3,2,0,1:T(8,128)S(1)}, f32[48,2,5,1]{3,2,0,1:T(8,128)S(1)}, u32[]{:S(2)}, u32[]{:S(2)}) collective-permute-start(f32[48,2,5,1]{3,2,0,1:T(8,128)S(1)} %get-tuple-element.32), channel_id=1, source_target_pairs={{0,1},{1,2},{2,3},{4,5},{5,6},{6,7},{8,9},{9,10},{10,11},{12,13},{... | collective-permute-start | bytes 5768 | tf_op jit(solution)/shard_map/ppermute | solution.py:35
  251.9 2.8 collective-permute-start.5
  255.4 6.4 %collective-permute-done.6 = f32[48,2,5,1]{3,2,0,1:T(8,128)S(1)} collective-permute-done((f32[48,2,5,1]{3,2,0,1:T(8,128)S(1)}, f32[48,2,5,1]{3,2,0,1:T(8,128)S(1)}, u32[]{:S(2)}, u32[]{:S(2)}) %collective-permute-start.6) | collective-permute-done | bytes 1952 | tf_op jit(solution)/shard_map/ppermute | solution.py:35
  261.8 2.8 collective-permute-done.5
  266.7 2.8 collective-permute-start.7
  269.4 3.1 %collective-permute-start.8 = (f32[48,2,5,1]{3,2,0,1:T(8,128)S(1)}, f32[48,2,5,1]{3,2,0,1:T(8,128)S(1)}, u32[]{:S(2)}, u32[]{:S(2)}) collective-permute-start(f32[48,2,5,1]{3,2,0,1:T(8,128)S(1)} %get-tuple-element.29), channel_id=1, source_target_pairs={{0,1},{1,2},{2,3},{4,5},{5,6},{6,7},{8,9},{9,10},{10,11},{12,13},{... | collective-permute-start | bytes 5768 | tf_op jit(solution)/shard_map/ppermute | solution.py:35
  272.6 1.3 copy.90
  273.9 4.7 %collective-permute-done.7 = f32[48,2,5,1]{3,2,0,1:T(8,128)S(1)} collective-permute-done((f32[48,2,5,1]{3,2,0,1:T(8,128)S(1)}, f32[48,2,5,1]{3,2,0,1:T(8,128)S(1)}, u32[]{:S(2)}, u32[]{:S(2)}) %collective-permute-start.7) | collective-permute-done | bytes 1952 | tf_op jit(solution)/shard_map/ppermute | solution.py:38
  278.6 2.5 collective-permute-done.8
  283.0 0.9 copy.91
  (63 shorter events, 11.2 us)
Async XLA Ops:
  7.2 238.6 %all-reduce.3.cloned.1.call-start = ((), (), s32[]{:S(2)}) async-start(), calls=%async_computation | async-start | bytes 9437184
  9.3 42.5 %collective-permute-start.3 = (f32[5,8,1,128]{3,0,2,1:T(8,128)S(1)}, f32[5,8,1,128]{3,0,2,1:T(8,128)S(1)}, u32[]{:S(2)}, u32[]{:S(2)}) collective-permute-start(f32[5,8,1,128]{3,0,2,1:T(8,128)S(1)} %get-tuple-element.20), channel_id=1, source_target_pairs={{0,1},{1,2},{2,3},{4,5},{5,6},{6,7},{8,9},{9,10},{10,11},{12,13},{... | collective-permute-start | bytes 61448 | tf_op jit(solution)/shard_map/ppermute | solution.py:35
  12.4 39.4 %collective-permute-start.2 = (f32[5,8,1,128]{3,0,2,1:T(8,128)S(1)}, f32[5,8,1,128]{3,0,2,1:T(8,128)S(1)}, u32[]{:S(2)}, u32[]{:S(2)}) collective-permute-start(f32[5,8,1,128]{3,0,2,1:T(8,128)S(1)} %get-tuple-element.21), channel_id=1, source_target_pairs={{1,0},{2,1},{3,2},{5,4},{6,5},{7,6},{9,8},{10,9},{11,10},{13,12},{... | collective-permute-start | bytes 61448 | tf_op jit(solution)/shard_map/ppermute | solution.py:38
  20.4 28.7 %collective-permute-start = (f32[5,8,64,1]{2,1,3,0:T(8,128)}, f32[5,8,64,1]{2,1,3,0:T(8,128)}, u32[]{:S(2)}, u32[]{:S(2)}) collective-permute-start(f32[5,8,64,1]{2,1,3,0:T(8,128)} %copy.76), channel_id=1, source_target_pairs={{4,0},{8,4},{12,8},{16,12},{20,16},{24,20},{28,24},{32,28},{36,32}... | collective-permute-start | bytes 30728 | tf_op jit(solution)/shard_map/ppermute | solution.py:38
  31.4 2.5 copy-start.8
  31.4 15.0 %collective-permute-start.1 = (f32[5,8,64,1]{2,1,3,0:T(8,128)}, f32[5,8,64,1]{2,1,3,0:T(8,128)}, u32[]{:S(2)}, u32[]{:S(2)}) collective-permute-start(f32[5,8,64,1]{2,1,3,0:T(8,128)} %copy.78), channel_id=1, source_target_pairs={{0,4},{4,8},{8,12},{12,16},{16,20},{20,24},{24,28},{28,32},{32,36}... | collective-permute-start | bytes 30728 | tf_op jit(solution)/shard_map/ppermute | solution.py:35
  31.4 9.5 %copy-start.4 = (f32[1,5,8,64,128]{4,3,2,1,0:T(8,128)S(1)}, f32[1,5,8,64,128]{4,3,2,1,0:T(8,128)}, u32[]{:S(2)}) copy-start(f32[1,5,8,64,128]{4,3,2,1,0:T(8,128)} %param.6) | copy-start | bytes 3932164
  51.8 2.0 copy-start
  51.9 2.2 copy-start.1
  54.1 6.4 %copy-start.5 = (f32[1536]{0:T(1024)S(1)}, f32[1536]{0:T(1024)}, u32[]{:S(2)}) copy-start(f32[1536]{0:T(1024)} %convert_multiply_fusion) | copy-start | bytes 18436
  54.1 6.4 %copy-start.6 = (s32[1536]{0:T(1024)S(1)}, s32[1536]{0:T(1024)}, u32[]{:S(2)}) copy-start(s32[1536]{0:T(1024)} %get-tuple-element.44) | copy-start | bytes 18436
  60.4 4.8 %copy-start.2 = (f32[5,8,64,128]{3,0,2,1:T(8,128)}, f32[5,8,64,128]{3,0,2,1:T(8,128)S(1)}, u32[]{:S(2)}) copy-start(f32[5,8,64,128]{3,0,2,1:T(8,128)S(1)} %fusion.6) | copy-start | bytes 3932164
  79.8 0.7 copy-start.9
  79.8 167.3 %copy-start.7 = (f32[1,2,5,5]{3,1,2,0:T(2,128)S(1)}, f32[1,2,5,5]{3,1,2,0:T(2,128)}, u32[]{:S(2)}) copy-start(f32[1,2,5,5]{3,1,2,0:T(2,128)} %param.9) | copy-start | bytes 604
  246.7 1.7 collective-permute-start.4
  248.8 13.1 %collective-permute-start.6 = (f32[48,2,5,1]{3,2,0,1:T(8,128)S(1)}, f32[48,2,5,1]{3,2,0,1:T(8,128)S(1)}, u32[]{:S(2)}, u32[]{:S(2)}) collective-permute-start(f32[48,2,5,1]{3,2,0,1:T(8,128)S(1)} %get-tuple-element.32), channel_id=1, source_target_pairs={{0,1},{1,2},{2,3},{4,5},{5,6},{6,7},{8,9},{9,10},{10,11},{12,13},{... | collective-permute-start | bytes 5768 | tf_op jit(solution)/shard_map/ppermute | solution.py:35
  251.9 12.8 %collective-permute-start.5 = (f32[48,2,5,1]{3,2,0,1:T(8,128)S(1)}, f32[48,2,5,1]{3,2,0,1:T(8,128)S(1)}, u32[]{:S(2)}, u32[]{:S(2)}) collective-permute-start(f32[48,2,5,1]{3,2,0,1:T(8,128)S(1)} %get-tuple-element.33), channel_id=1, source_target_pairs={{1,0},{2,1},{3,2},{5,4},{6,5},{7,6},{9,8},{10,9},{11,10},{13,12},{... | collective-permute-start | bytes 5768 | tf_op jit(solution)/shard_map/ppermute | solution.py:38
  265.6 7.0 %copy-start.3 = (f32[5,8,64,128]{3,0,2,1:T(8,128)S(1)}, f32[5,8,64,128]{3,0,2,1:T(8,128)}, u32[]{:S(2)}) copy-start(f32[5,8,64,128]{3,0,2,1:T(8,128)} %copy-done.2) | copy-start | bytes 3932164
  266.7 11.9 %collective-permute-start.7 = (f32[48,2,5,1]{3,2,0,1:T(8,128)S(1)}, f32[48,2,5,1]{3,2,0,1:T(8,128)S(1)}, u32[]{:S(2)}, u32[]{:S(2)}) collective-permute-start(f32[48,2,5,1]{3,2,0,1:T(8,128)S(1)} %get-tuple-element.28), channel_id=1, source_target_pairs={{1,0},{2,1},{3,2},{5,4},{6,5},{7,6},{9,8},{10,9},{11,10},{13,12},{... | collective-permute-start | bytes 5768 | tf_op jit(solution)/shard_map/ppermute | solution.py:38
  269.4 11.6 %collective-permute-start.8 = (f32[48,2,5,1]{3,2,0,1:T(8,128)S(1)}, f32[48,2,5,1]{3,2,0,1:T(8,128)S(1)}, u32[]{:S(2)}, u32[]{:S(2)}) collective-permute-start(f32[48,2,5,1]{3,2,0,1:T(8,128)S(1)} %get-tuple-element.29), channel_id=1, source_target_pairs={{0,1},{1,2},{2,3},{4,5},{5,6},{6,7},{8,9},{9,10},{10,11},{12,13},{... | collective-permute-start | bytes 5768 | tf_op jit(solution)/shard_map/ppermute | solution.py:35
Sparse Core Ops, SparseCore 0:
  80.0 165.7 all-reduce.2
where the time goes:
time: 292 us; the launch traced here: 291 us
  waiting for transfers between devices  181 us (62%)
  local copies, waits for them, and re-layouts  32 us (11%)
  matrix products  26.3 us (9%)
  starting transfers between devices  26.2 us (9%)
  between operations  15 us (5%)
  other arithmetic  10.1 us (3%)
    unnamed x2, waiting for transfers between devices  164 us
    ppermute x4, starting transfers between devices, extended(): lax.ppermute(lax.slice_in_dim(block, 0, width, axis=dim), axis, backward)  16.5 us
    ppermute x4, starting transfers between devices, extended(): lax.ppermute(lax.slice_in_dim(block, block.shape[dim] - width, None, axis...  9.31 us
    ppermute x4, waiting for transfers between devices, extended(): lax.ppermute(lax.slice_in_dim(block, block.shape[dim] - width, None, axis...  8.9 us
    unnamed x26, local copies, waits for them, and re-layouts  8.38 us
    another operation x1, local copies, waits for them, and re-layouts, transform(): return jnp.stack([real_part, imag_part], axis=1)  7.77 us
    ppermute x4, waiting for transfers between devices, extended(): lax.ppermute(lax.slice_in_dim(block, 0, width, axis=dim), axis, backward)  7.55 us
    dot_general x1, matrix products, flux_step(): jnp.einsum('gf,fzrp->gzrp', jacobian[0], pitch_plus - pitch_minus, precis...  6.27 us
  transfers between devices with their start and end apart: 10, of which 6 were waited for; matrix products, arithmetic and copies ran while one was open for 11% of the time, Pallas kernels for 0%

commit v1 on v0

v1 whole, which is shorter than its diff:
```python
import math

import jax
import jax.numpy as jnp
import ml_dtypes
import numpy as np
from jax import lax
from jax.experimental import pallas as pl
from jax.experimental.pallas import tpu as pltpu
from jax.sharding import PartitionSpec as P

F = 5
BLADES = 22
VANES = 54
AXIAL = 8
HARMONICS = 4
MODES_PER = 128
MODES = 512
PITCH = 4096
K_MAX = 32
CAPACITY = 48
N_PITCH = 32
N_RAD = 4
RAD = 64
LANES = 128
GROUPS = 3
TABLE = GROUPS * LANES
SLOT_LANES = 64
PACKED = N_PITCH * SLOT_LANES

FLUX_PITCH = 0.25
FLUX_RAD = 0.25
FLUX_AXIAL = 0.5
FLUX_DIFFUSE = 0.1
RELAX = 0.7
OMEGA = 0.05
KAPPA = 2.0

f32 = jnp.float32
bf16 = jnp.bfloat16
SMEM = pl.BlockSpec(memory_space=pltpu.SMEM)
VMEM = pl.BlockSpec(memory_space=pltpu.VMEM)


def iota(shape, dim):
    return lax.broadcasted_iota(jnp.int32, shape, dim)


def fourier_tables():
    weights = np.zeros((2, GROUPS, 3 * 2 * LANES, 2 * LANES), np.float64)
    codes = np.full((2, 8, TABLE), -1, np.int32)
    j = np.arange(LANES)
    for b, (own, other) in enumerate(((BLADES, VANES), (VANES, BLADES))):
        used = [0] * GROUPS
        for n in range(1, HARMONICS + 1):
            for k in range(-K_MAX, K_MAX + 1):
                q = (n * own - k * other) // 2
                t = q % 16
                part = min(t, 16 - t)
                sign = 1.0 if t <= 8 else -1.0
                group, member = divmod(part, 3)
                lane = used[group]
                used[group] += 1
                angle = 2.0 * np.pi * ((q * j) % 2048) / 2048.0
                cos, sin = np.cos(angle) / 64.0, np.sin(angle) / 64.0
                rows = weights[b, group, member * 256 : member * 256 + 256]
                rows[:LANES, lane] = cos
                rows[LANES:, lane] = sign * sin
                rows[:LANES, LANES + lane] = -sin
                rows[LANES:, LANES + lane] = sign * cos
                codes[b, :, group * LANES + lane] = n * 128 + k + K_MAX
    high = weights.astype(ml_dtypes.bfloat16)
    low = (weights - high.astype(np.float64)).astype(ml_dtypes.bfloat16)
    return np.stack([high, low], axis=1), codes


def mix(jac, k, g, parts):
    total = jac[0, k, g, 0] * parts[0]
    for f in range(1, F):
        total = total + jac[0, k, g, f] * parts[f]
    return total


def exit_kernel(jac, flow, out):
    now = [flow[0, f, 1] for f in range(F)]
    behind = [flow[0, f, 0] for f in range(F)]
    lane = iota((RAD, LANES), 1)
    row = iota((RAD, LANES), 0)
    change = [now[f] - behind[f] for f in range(F)]
    edges = jnp.zeros((RAD, LANES), f32)
    out[...] = jnp.zeros(out.shape, f32)
    for g in range(F):
        pitch = FLUX_PITCH * mix(jac, 0, g, now)
        radial = FLUX_RAD * mix(jac, 1, g, now)
        soft = FLUX_DIFFUSE * now[g]
        to_low, to_high = soft - pitch, soft + pitch
        inward, outward = soft - radial, soft + radial
        value = now[g] - FLUX_AXIAL * mix(jac, 2, g, change) - 4.0 * soft
        value = value + jnp.where(lane == LANES - 1, 0.0, pltpu.roll(to_low, LANES - 1, 1))
        value = value + jnp.where(lane == 0, 0.0, pltpu.roll(to_high, 1, 1))
        value = value + jnp.where(row == RAD - 1, 0.0, pltpu.roll(inward, RAD - 1, 0))
        value = value + jnp.where(row == 0, 0.0, pltpu.roll(outward, 1, 0))
        out[:, g, :] = value
        edges = jnp.where(lane == g, pltpu.roll(to_low, g, 1) if g else to_low, edges)
        edges = jnp.where(lane == 8 + g, pltpu.roll(to_high, 9 + g, 1), edges)
        out[g, 6:7, :] = inward[0:1]
        out[F + g, 6:7, :] = outward[RAD - 1 : RAD]
    out[:, 5, :] = edges


def halo_kernel(flow, to_low, to_high, first, last):
    lane = iota((RAD, LANES), 1)
    low = jnp.zeros((RAD, LANES), f32)
    high = jnp.zeros((RAD, LANES), f32)
    for f in range(F):
        for z in range(AXIAL):
            k = f * AXIAL + z
            block = flow[0, f, z]
            low = jnp.where(lane == k, pltpu.roll(block, k, 1) if k else block, low)
            high = jnp.where(lane == k, pltpu.roll(block, k + 1, 1), high)
            first[f, z : z + 1, :] = block[0:1]
            last[f, z : z + 1, :] = block[RAD - 1 : RAD]
    to_low[...] = low
    to_high[...] = high


def flux_kernel(jac, flow, inflow, next_column, last_column, next_row, last_row, out, previous):
    z = pl.program_id(0)
    lane = iota((RAD, LANES), 1)
    row = iota((RAD, LANES), 0)

    @pl.when(z == 0)
    def _():
        previous[...] = inflow[0]

    now, pitch, radial, change, laplace = [], [], [], [], []
    for f in range(F):
        block = flow[0, f, 0]
        k = f * AXIAL + z
        right = pltpu.roll(next_column[...], LANES - 1 - k, 1)
        left = pltpu.roll(last_column[...], lax.bitwise_and(LANES - k, LANES - 1), 1)
        right = jnp.where(lane == LANES - 1, right, pltpu.roll(block, LANES - 1, 1))
        left = jnp.where(lane == 0, left, pltpu.roll(block, 1, 1))
        above = jnp.where(row == RAD - 1, next_row[f, pl.ds(z, 1), :], pltpu.roll(block, RAD - 1, 0))
        below = jnp.where(row == 0, last_row[f, pl.ds(z, 1), :], pltpu.roll(block, 1, 0))
        now.append(block)
        pitch.append(FLUX_PITCH * (right - left))
        radial.append(FLUX_RAD * (above - below))
        change.append(FLUX_AXIAL * (block - previous[f]))
        laplace.append(FLUX_DIFFUSE * (right + left + above + below - 4.0 * block))
    for g in range(F):
        flux = mix(jac, 0, g, pitch) + mix(jac, 1, g, radial) + mix(jac, 2, g, change)
        out[0, g, 0] = now[g] - flux + laplace[g]
    for f in range(F):
        previous[f] = now[f]


def table_kernel(ids, dest, modes, codes, place, terms):
    source = 1 - ids[0]
    own = jnp.where(source == 0, BLADES, VANES)
    other = jnp.where(source == 0, VANES, BLADES)
    dest_row = dest[pl.ds(source, 1), :]
    listed = modes[source]
    code_row = jnp.concatenate(
        [listed[h : h + 1] + (K_MAX + 128 * (h + 1)) for h in range(HARMONICS)], axis=1
    )

    def column(row, block):
        part = row[:, block * LANES : (block + 1) * LANES]
        return jnp.transpose(jnp.broadcast_to(part, (LANES, LANES)))

    here = iota((LANES, LANES), 0)
    there = iota((LANES, LANES), 1)
    spread = iota((LANES, PACKED), 1)
    target = ids[1] * SLOT_LANES + lax.bitwise_and(there, SLOT_LANES - 1)
    slot_code = jnp.zeros((1, LANES), jnp.int32)
    hits = []
    for block in range(MODES // LANES):
        dest_col = column(dest_row, block)
        before = jnp.zeros((LANES, LANES), f32)
        for past in range(block + 1):
            same = dest_col == dest_row[:, past * LANES : (past + 1) * LANES]
            if past == block:
                same = same & (there < here)
            before = before + same.astype(f32)
        rank = jnp.sum(before, axis=1, keepdims=True).astype(jnp.int32)
        slot = dest_col * SLOT_LANES + rank
        hits.append((slot[:, :1] == spread).astype(f32).astype(bf16))
        mine = jnp.where(slot == target, column(code_row, block), 0)
        slot_code = slot_code + jnp.sum(mine, axis=0, keepdims=True)
    hit = jnp.concatenate(hits, axis=0)
    code_table = codes[source]
    lane_code = jnp.concatenate([column(code_table[0:1], g) for g in range(GROUPS)], axis=0)
    listed_at = (lane_code[:, :1] == code_row).astype(f32).astype(bf16)
    place[...] = jnp.dot(listed_at, hit, preferred_element_type=f32).astype(bf16)
    n = lax.shift_right_logical(slot_code, 7)
    m = n * own - (lax.bitwise_and(slot_code, 127) - K_MAX) * other
    m = jnp.where(n > 0, m, 0)
    wave = lax.bitwise_and(m + PITCH // 2, PITCH - 1) - PITCH // 2
    sigma = OMEGA * n.astype(f32) * own.astype(f32)
    kappa = KAPPA * wave.astype(f32) / PITCH
    lane = iota((1, LANES), 1)
    sign = jnp.where(lane < SLOT_LANES, -1.0, 1.0)
    terms[...] = jnp.zeros(terms.shape, f32)
    terms[0:1] = sign * sigma
    terms[1:2] = sign * kappa
    terms[2:3] = RELAX / (4.0 + sigma * sigma)


def transform_kernel(cells, weights, out):
    lane = iota((8, LANES), 1)
    sub = iota((8, LANES), 0)
    parts = []
    for half in range(2):
        x = [cells[2 * p + half] for p in range(N_PITCH)]
        z = [x[p] + x[p + 16] for p in range(16)]
        even = [None] + [z[p] + z[16 - p] for p in range(1, 8)]
        odd = [None] + [z[p] - z[16 - p] for p in range(1, 8)]
        columns = []
        for t in range(9):
            re = z[0] + z[8] if t % 2 == 0 else z[0] - z[8]
            im = jnp.zeros((8, LANES), f32)
            for p in range(1, 8):
                re = re + math.cos(2.0 * math.pi * ((t * p) % 16) / 16) * even[p]
                if t % 8:
                    im = im - math.sin(2.0 * math.pi * ((t * p) % 16) / 16) * odd[p]

            def edge(value, offset):
                spread = jnp.broadcast_to(value[5:6, :], (8, LANES))
                return jnp.sum(jnp.where(lane == sub + offset, spread, 0.0), axis=1, keepdims=True)

            cos, sin = math.cos(2.0 * math.pi * t / 16), math.sin(2.0 * math.pi * t / 16)
            low_re, high_re = edge(re, 0), edge(re, 8)
            low_im, high_im = (edge(im, 0), edge(im, 8)) if t % 8 else (0.0, 0.0)
            re = re + jnp.where(lane == LANES - 1, cos * low_re - sin * low_im, 0.0)
            re = re + jnp.where(lane == 0, cos * high_re + sin * high_im, 0.0)
            im = im + jnp.where(lane == LANES - 1, cos * low_im + sin * low_re, 0.0)
            im = im + jnp.where(lane == 0, cos * high_im - sin * high_re, 0.0)
            columns += [re, im]
        parts.append(columns)
    for group in range(GROUPS):
        left = jnp.concatenate(
            [
                jnp.concatenate([parts[half][group * 6 + i] for i in range(6)], axis=1)
                for half in range(2)
            ],
            axis=0,
        )
        high = left.astype(bf16)
        low = (left - high.astype(f32)).astype(bf16)
        both = jnp.dot(
            jnp.concatenate([high, low], axis=0), weights[0, group], preferred_element_type=f32
        )
        value = both[:16] + both[16:]
        value = value + jnp.dot(high, weights[1, group], preferred_element_type=f32)
        out[0:16, group * LANES : (group + 1) * LANES] = value[:, :LANES]
        out[16:32, group * LANES : (group + 1) * LANES] = value[:, LANES:]


def place_kernel(values, place, out):
    x = values[...]
    high = x.astype(bf16)
    rest = x - high.astype(f32)
    mid = rest.astype(bf16)
    low = (rest - mid.astype(f32)).astype(bf16)
    split = jnp.concatenate([high, mid, low], axis=0)
    lane = iota((8, LANES), 1)
    for pair in range(N_PITCH // 2):
        picked = jnp.dot(
            split, place[:, pair * LANES : (pair + 1) * LANES], preferred_element_type=f32
        )
        picked = picked[0:32] + picked[32:64] + picked[64:96]
        for half in range(2):
            re, im = picked[half * 8 : half * 8 + 8], picked[16 + half * 8 : 24 + half * 8]
            out[4 * pair + half] = jnp.where(lane < SLOT_LANES, re, pltpu.roll(im, SLOT_LANES, 1))
            out[4 * pair + 2 + half] = jnp.where(
                lane < SLOT_LANES, pltpu.roll(re, SLOT_LANES, 1), im
            )


SPAN = RAD + 8


def sweep_kernel(ids, jac, modes, terms, main, low, high):
    rad = ids[0]
    radius = iota((SPAN, LANES), 0) - 4
    inside = jnp.where(
        ((radius < 0) & (rad == 0)) | ((radius >= RAD) & (rad == N_RAD - 1)), 0.0, 1.0
    )
    sigma, kappa, scale = terms[0:1], terms[1:2], terms[2:3]
    index = iota((8, LANES), 0)

    def turned(value):
        return pltpu.roll(value, SLOT_LANES, 1)

    start = []
    for f in range(F):
        before = jnp.where(index == 3, modes[f, 6:7, :], 0.0)
        after = jnp.where(index == 4, modes[F + f, 6:7, :], 0.0)
        body = jnp.concatenate([before[:4], modes[:, f, :], after[4:]], axis=0)
        start.append(body * inside)
    current = start
    for _ in range(2):
        above = [pltpu.roll(w, SPAN - 1, 0) for w in current]
        below = [pltpu.roll(w, 1, 0) for w in current]
        grade = [above[f] - below[f] for f in range(F)]
        update = []
        for g in range(F):
            w = current[g]
            applied = 2.0 * w - 0.5 * (above[g] + below[g]) + sigma * turned(w)
            applied = applied + kappa * turned(mix(jac, 0, g, current))
            applied = applied + 0.5 * mix(jac, 1, g, grade)
            rest = start[g] - applied
            update.append((w + scale * (2.0 * rest - sigma * turned(rest))) * inside)
        current = update
    for f in range(F):
        main[f] = current[f][4 : 4 + RAD]
        low[f] = current[f][:8]
        high[f] = current[f][SPAN - 8 :]


def finish_kernel(main, from_low, from_high, out):
    index = iota((8, LANES), 0)
    for f in range(F):
        first = main[f, 0:8] + jnp.where(index < 4, pltpu.roll(from_low[f], 4, 0), 0.0)
        last = main[f, RAD - 8 :] + jnp.where(index >= 4, pltpu.roll(from_high[f], 4, 0), 0.0)
        body = jnp.concatenate([first, main[f, 8 : RAD - 8], last], axis=0)
        turned = jnp.transpose(body)
        out[0, 0, :, 0, f, :] = turned[:CAPACITY]
        out[0, 0, :, 1, f, :] = turned[SLOT_LANES : SLOT_LANES + CAPACITY]


def shape(*dims, dtype=f32):
    return jax.ShapeDtypeStruct(dims, dtype)


def cost(flops, size):
    return pl.CostEstimate(flops=flops, bytes_accessed=size, transcendentals=0)


BIG = pltpu.CompilerParams(vmem_limit_bytes=40 * 1024 * 1024)


def on_device(flow, inflow, flux_jacobian, sweep_jacobian, mode_index, destination):
    weights, codes = fourier_tables()
    row = lax.axis_index("row")
    pitch = lax.axis_index("pitch")
    rad = lax.axis_index("rad")

    face = pl.pallas_call(
        exit_kernel,
        grid=(1,),
        out_shape=shape(RAD, 8, LANES),
        in_specs=[SMEM, pl.BlockSpec((1, F, 2, RAD, LANES), lambda i: (0, 0, 3, 0, 0))],
        out_specs=pl.BlockSpec((RAD, 8, LANES), lambda i: (0, 0, 0)),
        compiler_params=BIG,
        cost_estimate=cost(4_000_000, 600_000),
    )(flux_jacobian, flow)
    cells = lax.all_to_all(face, "pitch", 0, 0, tiled=True)

    ids = jnp.stack([row, pitch]).astype(jnp.int32)
    place, terms = pl.pallas_call(
        table_kernel,
        out_shape=(shape(TABLE, PACKED, dtype=bf16), shape(8, LANES)),
        in_specs=[SMEM, VMEM, VMEM, VMEM],
        out_specs=(VMEM, VMEM),
        compiler_params=BIG,
        cost_estimate=cost(2 * TABLE * MODES * PACKED, 2_000_000),
    )(ids, destination[:, :, 0], mode_index, codes)

    to_low, to_high, first, last = pl.pallas_call(
        halo_kernel,
        out_shape=(shape(RAD, LANES), shape(RAD, LANES), shape(F, AXIAL, LANES), shape(F, AXIAL, LANES)),
        in_specs=[VMEM],
        out_specs=(VMEM,) * 4,
        compiler_params=BIG,
        cost_estimate=cost(4_000_000, 1_400_000),
    )(flow)
    up = [(i, (i + 1) % N_PITCH) for i in range(N_PITCH)]
    down = [((i + 1) % N_PITCH, i) for i in range(N_PITCH)]
    outward = [(i, i + 1) for i in range(N_RAD - 1)]
    inward = [(i + 1, i) for i in range(N_RAD - 1)]
    next_column = lax.ppermute(to_low, "pitch", down)
    last_column = lax.ppermute(to_high, "pitch", up)
    next_row = lax.ppermute(first, "rad", inward)
    last_row = lax.ppermute(last, "rad", outward)

    next_flow = pl.pallas_call(
        flux_kernel,
        grid=(AXIAL,),
        out_shape=shape(1, F, AXIAL, RAD, LANES),
        in_specs=[
            SMEM,
            pl.BlockSpec((1, F, 1, RAD, LANES), lambda z: (0, 0, z, 0, 0)),
            pl.BlockSpec((1, F, RAD, LANES), lambda z: (0, 0, 0, 0)),
            pl.BlockSpec((RAD, LANES), lambda z: (0, 0)),
            pl.BlockSpec((RAD, LANES), lambda z: (0, 0)),
            pl.BlockSpec((F, AXIAL, LANES), lambda z: (0, 0, 0)),
            pl.BlockSpec((F, AXIAL, LANES), lambda z: (0, 0, 0)),
        ],
        out_specs=pl.BlockSpec((1, F, 1, RAD, LANES), lambda z: (0, 0, z, 0, 0)),
        scratch_shapes=[pltpu.VMEM((F, RAD, LANES), f32)],
        compiler_params=BIG,
        cost_estimate=cost(20_000_000, 3_000_000),
    )(flux_jacobian, flow, inflow, next_column, last_column, next_row, last_row)

    own_weights = lax.dynamic_index_in_dim(jnp.asarray(weights), row, 0, keepdims=False)
    modes = pl.pallas_call(
        transform_kernel,
        out_shape=shape(32, TABLE),
        in_specs=[VMEM, VMEM],
        out_specs=VMEM,
        compiler_params=BIG,
        cost_estimate=cost(60_000_000, 3_000_000),
    )(cells, own_weights)
    modes = lax.ppermute(modes, "row", [(0, 1), (1, 0)])
    placed = pl.pallas_call(
        place_kernel,
        out_shape=shape(RAD, 8, LANES),
        in_specs=[VMEM, VMEM],
        out_specs=VMEM,
        compiler_params=BIG,
        cost_estimate=cost(150_000_000, 2_000_000),
    )(modes, place)
    amplitude = lax.all_to_all(placed, "pitch", 0, 0, tiled=True)
    main, low, high = pl.pallas_call(
        sweep_kernel,
        out_shape=(shape(F, RAD, LANES), shape(F, 8, LANES), shape(F, 8, LANES)),
        in_specs=[SMEM, SMEM, VMEM, VMEM],
        out_specs=(VMEM,) * 3,
        compiler_params=BIG,
        cost_estimate=cost(8_000_000, 500_000),
    )(rad.astype(jnp.int32).reshape(1), sweep_jacobian, amplitude, terms)
    from_high = lax.ppermute(low, "rad", inward)
    from_low = lax.ppermute(high, "rad", outward)
    response = pl.pallas_call(
        finish_kernel,
        out_shape=shape(1, 1, CAPACITY, 2, F, RAD),
        in_specs=[VMEM] * 3,
        out_specs=VMEM,
        compiler_params=BIG,
        cost_estimate=cost(1_000_000, 800_000),
    )(main, from_low, from_high)
    return next_flow, response


def solution(mesh):
    placed = (
        P("row", None, None, "rad", "pitch"),
        P("row", None, "rad", "pitch"),
        P("row", None, None, None),
        P("row", None, None, None),
        P(),
        P(),
    )
    return jax.shard_map(
        on_device,
        mesh=mesh,
        in_specs=placed,
        out_specs=(
            P("row", None, None, "rad", "pitch"),
            P("row", "pitch", None, None, None, "rad"),
        ),
        check_vma=False,
    )
```

time: 292 us -> 64.7 us (0.22)
  waiting for transfers between devices: 181 us -> 11.9 us
  local copies, waits for them, and re-layouts: 32 us -> 5.38 us
  matrix products: 26.3 us -> 0 us
  between operations: 15 us -> 0.84 us
  Pallas kernels: 0 us -> 13.5 us
  other arithmetic: 10.1 us -> 0.07 us
  starting transfers between devices: 26.2 us -> 32.5 us
    unnamed x2 -> x0, waiting for transfers between devices: 164 us -> none
    dot_general x13 -> x0, matrix products: 26.3 us -> none  [the longest x1 6.27 us: flux_step(): jnp.einsum('gf,fzrp->gzrp', jacobian[0], pitch_plus - pitch_minus, precis...]
    ppermute x9 -> x7, waiting for transfers between devices: 17 us -> 0.02 us  [the longest x1 0.01 us: on_device(): modes = lax.ppermute(modes, 'row', [(0, 1), (1, 0)])]
    all_to_all x0 -> x2, starting transfers between devices: none -> 15.6 us  [the longest x1 11.5 us: on_device(): cells = lax.all_to_all(face, 'pitch', 0, 0, tiled=True)]
    pallas_call x0 -> x8, Pallas kernels: none -> 13.5 us  [the longest x1 5.35 us: on_device(): pl.pallas_call(flux_kernel, grid=(AXIAL,), out_shape=shape(1, F, AXIAL, R...]
    all_to_all x0 -> x2, waiting for transfers between devices: none -> 11.8 us  [the longest x1 10.1 us: on_device(): cells = lax.all_to_all(face, 'pitch', 0, 0, tiled=True)]
    ppermute x9 -> x7, starting transfers between devices: 26.2 us -> 17 us  [the longest x1 5.28 us: on_device(): next_column = lax.ppermute(to_low, 'pitch', down)]
    slice x9 -> x0, local copies, waits for them, and re-layouts: 8.86 us -> none  [the longest x4 5.44 us: extended(): lax.slice_in_dim(block, block.shape[dim] - width, None, axis=dim)]
  transfers between devices with their start and end apart: 10 -> 9, of which waited for: 6 -> 2; matrix products, arithmetic and copies ran while one was open for 11% -> 4% of each run, Pallas kernels for 0% -> 15%
where the time goes in v1:
time: 64.7 us; the launch traced here: 64.2 us
  starting transfers between devices  32.5 us (50%)
  Pallas kernels  13.5 us (21%)
  waiting for transfers between devices  11.9 us (18%)
  local copies, waits for them, and re-layouts  5.38 us (8%)
  between operations  0.84 us (1%)
    all_to_all x1, starting transfers between devices, on_device(): cells = lax.all_to_all(face, 'pitch', 0, 0, tiled=True)  11.5 us
    all_to_all x1, waiting for transfers between devices, on_device(): cells = lax.all_to_all(face, 'pitch', 0, 0, tiled=True)  10.1 us
    pallas_call x1, Pallas kernels, on_device(): pl.pallas_call(flux_kernel, grid=(AXIAL,), out_shape=shape(1, F, AXIAL, R...  5.35 us
    ppermute x1, starting transfers between devices, on_device(): next_column = lax.ppermute(to_low, 'pitch', down)  5.28 us
    all_to_all x1, starting transfers between devices, on_device(): amplitude = lax.all_to_all(placed, 'pitch', 0, 0, tiled=True)  4.1 us
    unnamed x16, local copies, waits for them, and re-layouts  3.57 us
    ppermute x1, starting transfers between devices, on_device(): last_row = lax.ppermute(last, 'rad', outward)  3.39 us
    ppermute x1, starting transfers between devices, on_device(): from_low = lax.ppermute(high, 'rad', outward)  3.11 us
  transfers between devices with their start and end apart: 9, of which 2 were waited for; matrix products, arithmetic and copies ran while one was open for 4% of the time, Pallas kernels for 15%

profile of v1, /device:TPU:4, one launch (start us, length us, event | category | flops | bytes accessed | tf_op | source)
XLA Modules:
  0.0 64.2 jit_solution(17661978687936641423)
XLA Ops:
  0.6 0.7 %copy.10.jac = f32[1,3,5,5]{3,2,1,0:T(8,128)S(1)} copy(f32[1,3,5,5]{3,0,2,1:T(1,128)} %param.10) | data formatting | bytes 600 | tf_op args[2]
  1.3 1.3 %copy-done = f32[1,5,8,64,128]{4,3,2,1,0:T(8,128)S(1)} copy-done((f32[1,5,8,64,128]{4,3,2,1,0:T(8,128)S(1)}, f32[1,5,8,64,128]{4,3,2,1,0:T(8,128)}, u32[]{:S(2)}) %copy-start) | copy-done | bytes 1310744
  2.6 1.9 %shard_map.97 = f32[64,8,128]{2,1,0:T(8,128)} custom-call(f32[1,3,5,5]{3,2,1,0:T(8,128)S(1)} %copy.10.jac, f32[1,5,8,64,128]{4,3,2,1,0:T(8,128)S(1)} %copy-done), custom_call_target="tpu_custom_call" | custom-call | flops 4000000 | bytes 600000 | tf_op jit(solution)/shard_map/pallas_call | solution.py:350
  4.5 11.5 %all-to-all-start = ((f32[64,8,128]{2,1,0:T(8,128)}), f32[64,8,128]{2,1,0:T(8,128)S(1)}, u32[]{:S(2)}, u32[]{:S(2)}) async-start(f32[64,8,128]{2,1,0:T(8,128)} %shard_map.97), calls=%async_computation | async-start | bytes 524288 | tf_op jit(solution)/shard_map/all_to_all | solution.py:359
  16.0 0.7 %copy.16 = s32[2,512,1]{1,0,2:T(2,128)S(1)} copy(s32[2,512,1]{1,2,0:T(1,128)} %param.13) | data formatting | bytes 8192
  16.7 0.1 pad_add_fusion.ids
  16.8 1.8 %dynamic-slice_bitcast_fusion.weights = bf16[2,3,768,256]{3,2,1,0:T(8,128)(2,1)S(1)} fusion(bf16[2,2,3,768,256]{4,3,2,1,0:T(8,128)(2,1)} %constant.26.clone, s32[]{:T(128)S(6)} %select_n.4), kind=kLoop, calls=%fused_computation | loop fusion | bytes 4718596 | tf_op jit(solution)/shard_map/jit(dynamic_index_in_dim)/squeeze | solution.py:407
  18.6 0.0 copy-start.3
  18.6 0.0 copy-start.4
  18.6 10.1 %all-to-all-done.cells = f32[64,8,128]{2,1,0:T(8,128)S(1)} async-done(((f32[64,8,128]{2,1,0:T(8,128)}), f32[64,8,128]{2,1,0:T(8,128)S(1)}, u32[]{:S(2)}, u32[]{:S(2)}) %all-to-all-start) | async-done | bytes 262176 | tf_op jit(solution)/shard_map/all_to_all | solution.py:359
  28.7 0.5 shard_map.98
  29.2 0.0 collective-permute-start.4
  29.2 0.0 copy-start.1
  29.2 2.1 %shard_map.99 = (bf16[384,2048]{1,0:T(8,128)(2,1)S(1)}, f32[8,128]{1,0:T(8,128)S(1)}) custom-call(s32[2]{0:T(128)S(1)} %pad_add_fusion.ids, s32[2,512]{1,0:T(2,128)S(1)} %bitcast.8, s32[2,4,128]{2,1,0:T(4,128)S(1)} %copy-done.3, s32[2,8,384]{2,1,0:T(8,128)S(1)} %copy-done.4), custom_call_target="tpu_custom_call" | custom-call | flops 805306368 | bytes 2000000 | tf_op jit(solution)/shard_map/pallas_call | solution.py:362
  31.3 0.0 copy-start.5
  31.4 0.0 copy-start.2
  31.4 0.0 collective-permute-done.4.values
  31.4 1.3 %shard_map.100 = f32[64,8,128]{2,1,0:T(8,128)} custom-call(f32[32,384]{1,0:T(8,128)S(1)} %collective-permute-done.4.values, bf16[384,2048]{1,0:T(8,128)(2,1)S(1)} %get-tuple-element.15.place), custom_call_target="tpu_custom_call" | custom-call | flops 150000000 | bytes 2000000 | tf_op jit(solution)/shard_map/pallas_call | solution.py:417
  32.7 4.1 %all-to-all-start.1 = ((f32[64,8,128]{2,1,0:T(8,128)}), f32[64,8,128]{2,1,0:T(8,128)S(1)}, u32[]{:S(2)}, u32[]{:S(2)}) async-start(f32[64,8,128]{2,1,0:T(8,128)} %shard_map.100), calls=%async_computation.1 | async-start | bytes 524288 | tf_op jit(solution)/shard_map/all_to_all | solution.py:425
  36.8 0.7 %shard_map.95 = (f32[64,128]{1,0:T(8,128)S(1)}, f32[64,128]{1,0:T(8,128)S(1)}, f32[5,8,128]{2,1,0:T(8,128)S(1)}, f32[5,8,128]{2,1,0:T(8,128)S(1)}) custom-call(f32[1,5,8,64,128]{4,3,2,1,0:T(8,128)S(1)} %copy-done.1), custom_call_target="tpu_custom_call" | custom-call | flops 4000000 | bytes 1400000 | tf_op jit(solution)/shard_map/pallas_call | solution.py:371
  37.5 2.4 %collective-permute-start.2 = (f32[5,8,128]{2,1,0:T(8,128)S(1)}, f32[5,8,128]{2,1,0:T(8,128)S(1)}, u32[]{:S(2)}, u32[]{:S(2)}) collective-permute-start(f32[5,8,128]{2,1,0:T(8,128)S(1)} %get-tuple-element.13), channel_id=1, source_target_pairs={{1,0},{2,1},{3,2},{5,4},{6,5},{7,6},{9,8},{10,9},{11,10},{13,12},{... | collective-permute-start | bytes 61448 | tf_op jit(solution)/shard_map/ppermute | solution.py:385
  40.0 5.3 %collective-permute-start = (f32[64,128]{1,0:T(8,128)S(1)}, f32[64,128]{1,0:T(8,128)S(1)}, u32[]{:S(2)}, u32[]{:S(2)}) collective-permute-start(f32[64,128]{1,0:T(8,128)S(1)} %get-tuple-element.11), channel_id=1, source_target_pairs={{4,0},{8,4},{12,8},{16,12},{20,16},{24,20},{28,24},{32,28},{36,32}... | collective-permute-start | bytes 98312 | tf_op jit(solution)/shard_map/ppermute | solution.py:383
  45.3 3.4 %collective-permute-start.3 = (f32[5,8,128]{2,1,0:T(8,128)S(1)}, f32[5,8,128]{2,1,0:T(8,128)S(1)}, u32[]{:S(2)}, u32[]{:S(2)}) collective-permute-start(f32[5,8,128]{2,1,0:T(8,128)S(1)} %get-tuple-element.14), channel_id=1, source_target_pairs={{0,1},{1,2},{2,3},{4,5},{5,6},{6,7},{8,9},{9,10},{10,11},{12,13},{... | collective-permute-start | bytes 61448 | tf_op jit(solution)/shard_map/ppermute | solution.py:386
  48.7 1.8 %all-to-all-done.1.modes = f32[64,8,128]{2,1,0:T(8,128)S(1)} async-done(((f32[64,8,128]{2,1,0:T(8,128)}), f32[64,8,128]{2,1,0:T(8,128)S(1)}, u32[]{:S(2)}, u32[]{:S(2)}) %all-to-all-start.1) | async-done | bytes 262176 | tf_op jit(solution)/shard_map/all_to_all | solution.py:425
  50.5 1.4 %shard_map.101 = (f32[5,64,128]{2,1,0:T(8,128)S(1)}, f32[5,8,128]{2,1,0:T(8,128)S(1)}, f32[5,8,128]{2,1,0:T(8,128)S(1)}) custom-call(s32[1]{0:T(128)} %bitcast.ids, f32[1,2,5,5]{3,2,1,0:T(8,128)S(1)} %copy.12.jac, f32[64,8,128]{2,1,0:T(8,128)S(1)} %all-to-all-done.1.modes, f32[8,128]{1,0:T(8,128)S(1)} %get-tuple-element.16.terms), custom_call_target="tpu_custom_call" | custom-call | flops 8000000 | bytes 500000 | tf_op jit(solution)/shard_map/pallas_call | solution.py:426
  51.9 3.1 %collective-permute-start.5 = (f32[5,8,128]{2,1,0:T(8,128)S(1)}, f32[5,8,128]{2,1,0:T(8,128)S(1)}, u32[]{:S(2)}, u32[]{:S(2)}) collective-permute-start(f32[5,8,128]{2,1,0:T(8,128)S(1)} %get-tuple-element.18), channel_id=1, source_target_pairs={{0,1},{1,2},{2,3},{4,5},{5,6},{6,7},{8,9},{9,10},{10,11},{12,13},{... | collective-permute-start | bytes 61448 | tf_op jit(solution)/shard_map/ppermute | solution.py:435
  55.0 0.0 collective-permute-done.2.next_row
  55.0 2.7 %collective-permute-start.6 = (f32[5,8,128]{2,1,0:T(8,128)S(1)}, f32[5,8,128]{2,1,0:T(8,128)S(1)}, u32[]{:S(2)}, u32[]{:S(2)}) collective-permute-start(f32[5,8,128]{2,1,0:T(8,128)S(1)} %get-tuple-element.19), channel_id=1, source_target_pairs={{1,0},{2,1},{3,2},{5,4},{6,5},{7,6},{9,8},{10,9},{11,10},{13,12},{... | collective-permute-start | bytes 61448 | tf_op jit(solution)/shard_map/ppermute | solution.py:434
  57.8 0.0 collective-permute-done.3.last_row
  57.8 5.4 %shard_map.96 = f32[1,5,8,64,128]{4,3,2,1,0:T(8,128)} custom-call(f32[1,3,5,5]{3,2,1,0:T(8,128)S(1)} %copy.10.jac, f32[1,5,8,64,128]{4,3,2,1,0:T(8,128)S(1)} %copy-done.1, f32[1,5,64,128]{3,2,1,0:T(8,128)S(1)} %copy-done.2, f32[64,128]{1,0:T(8,128)S(1)} %collective-permute-done.next_column, f32[64,128]{1,0:T(8,128)S(1)} %collective-permute-done.1.last_column, ...), custom_call_target="tpu_custom_call" | custom-call | flops 20000000 | bytes 3000000 | tf_op jit(solution)/shard_map/pallas_call | solution.py:388
  63.2 0.2 shard_map.102
  63.4 0.8 %copy.13 = f32[1,1,48,2,5,64]{5,3,4,2,1,0:T(2,128)} copy(f32[1,1,48,2,5,64]{5,4,3,2,1,0:T(8,128)S(1)} %shard_map.102) | data formatting | bytes 245760
  (12 shorter events, 0.0 us)
Async XLA Ops:
  1.3 1.3 %copy-start = (f32[1,5,8,64,128]{4,3,2,1,0:T(8,128)S(1)}, f32[1,5,8,64,128]{4,3,2,1,0:T(8,128)}, u32[]{:S(2)}) copy-start(f32[1,5,8,64,128]{4,3,2,1,0:T(8,128)} %flow.5) | copy-start | bytes 3932164
  4.5 24.2 %all-to-all-start = ((f32[64,8,128]{2,1,0:T(8,128)}), f32[64,8,128]{2,1,0:T(8,128)S(1)}, u32[]{:S(2)}, u32[]{:S(2)}) async-start(f32[64,8,128]{2,1,0:T(8,128)} %shard_map.97), calls=%async_computation | async-start | bytes 524288 | tf_op jit(solution)/shard_map/all_to_all | solution.py:359
  18.6 10.6 %copy-start.3 = (s32[2,4,128]{2,1,0:T(4,128)S(1)}, s32[2,4,128]{2,1,0:T(4,128)}, u32[]{:S(2)}) copy-start(s32[2,4,128]{2,1,0:T(4,128)} %modes.1) | copy-start | bytes 12292
  18.6 10.6 %copy-start.4 = (s32[2,8,384]{2,1,0:T(8,128)S(1)}, s32[2,8,384]{2,1,0:T(8,128)}, u32[]{:S(2)}) copy-start(s32[2,8,384]{2,1,0:T(8,128)} %constant.25.clone.codes) | copy-start | bytes 73732
  29.2 2.1 %collective-permute-start.4 = (f32[32,384]{1,0:T(8,128)S(1)}, f32[32,384]{1,0:T(8,128)S(1)}, u32[]{:S(2)}, u32[]{:S(2)}) collective-permute-start(f32[32,384]{1,0:T(8,128)S(1)} %shard_map.98), channel_id=1, source_target_pairs={{0,128},{128,0},{1,129},{129,1},{2,130},{130,2},{3,131},{131,3},{4... | collective-permute-start | bytes 147464 | tf_op jit(solution)/shard_map/ppermute | solution.py:416
  29.2 7.5 %copy-start.1 = (f32[1,5,8,64,128]{4,3,2,1,0:T(8,128)S(1)}, f32[1,5,8,64,128]{4,3,2,1,0:T(8,128)}, u32[]{:S(2)}) copy-start(f32[1,5,8,64,128]{4,3,2,1,0:T(8,128)} %flow.5) | copy-start | bytes 3932164
  31.3 17.3 %copy-start.5 = (f32[1,2,5,5]{3,1,2,0:T(2,128)S(1)}, f32[1,2,5,5]{3,1,2,0:T(2,128)}, u32[]{:S(2)}) copy-start(f32[1,2,5,5]{3,1,2,0:T(2,128)} %param.11) | copy-start | bytes 604
  31.4 26.4 %copy-start.2 = (f32[1,5,64,128]{3,2,1,0:T(8,128)S(1)}, f32[1,5,64,128]{3,2,1,0:T(8,128)}, u32[]{:S(2)}) copy-start(f32[1,5,64,128]{3,2,1,0:T(8,128)} %inflow.1) | copy-start | bytes 491524
  32.7 17.8 %all-to-all-start.1 = ((f32[64,8,128]{2,1,0:T(8,128)}), f32[64,8,128]{2,1,0:T(8,128)S(1)}, u32[]{:S(2)}, u32[]{:S(2)}) async-start(f32[64,8,128]{2,1,0:T(8,128)} %shard_map.100), calls=%async_computation.1 | async-start | bytes 524288 | tf_op jit(solution)/shard_map/all_to_all | solution.py:425
  37.5 17.5 %collective-permute-start.2 = (f32[5,8,128]{2,1,0:T(8,128)S(1)}, f32[5,8,128]{2,1,0:T(8,128)S(1)}, u32[]{:S(2)}, u32[]{:S(2)}) collective-permute-start(f32[5,8,128]{2,1,0:T(8,128)S(1)} %get-tuple-element.13), channel_id=1, source_target_pairs={{1,0},{2,1},{3,2},{5,4},{6,5},{7,6},{9,8},{10,9},{11,10},{13,12},{... | collective-permute-start | bytes 61448 | tf_op jit(solution)/shard_map/ppermute | solution.py:385
  40.0 17.8 %collective-permute-start = (f32[64,128]{1,0:T(8,128)S(1)}, f32[64,128]{1,0:T(8,128)S(1)}, u32[]{:S(2)}, u32[]{:S(2)}) collective-permute-start(f32[64,128]{1,0:T(8,128)S(1)} %get-tuple-element.11), channel_id=1, source_target_pairs={{4,0},{8,4},{12,8},{16,12},{20,16},{24,20},{28,24},{32,28},{36,32}... | collective-permute-start | bytes 98312 | tf_op jit(solution)/shard_map/ppermute | solution.py:383
  45.3 12.5 %collective-permute-start.1 = (f32[64,128]{1,0:T(8,128)S(1)}, f32[64,128]{1,0:T(8,128)S(1)}, u32[]{:S(2)}, u32[]{:S(2)}) collective-permute-start(f32[64,128]{1,0:T(8,128)S(1)} %get-tuple-element.12), channel_id=1, source_target_pairs={{0,4},{4,8},{8,12},{12,16},{16,20},{20,24},{24,28},{28,32},{32,36}... | collective-permute-start | bytes 98312 | tf_op jit(solution)/shard_map/ppermute | solution.py:384
  45.3 12.5 %collective-permute-start.3 = (f32[5,8,128]{2,1,0:T(8,128)S(1)}, f32[5,8,128]{2,1,0:T(8,128)S(1)}, u32[]{:S(2)}, u32[]{:S(2)}) collective-permute-start(f32[5,8,128]{2,1,0:T(8,128)S(1)} %get-tuple-element.14), channel_id=1, source_target_pairs={{0,1},{1,2},{2,3},{4,5},{5,6},{6,7},{8,9},{9,10},{10,11},{12,13},{... | collective-permute-start | bytes 61448 | tf_op jit(solution)/shard_map/ppermute | solution.py:386
  51.9 11.3 %collective-permute-start.5 = (f32[5,8,128]{2,1,0:T(8,128)S(1)}, f32[5,8,128]{2,1,0:T(8,128)S(1)}, u32[]{:S(2)}, u32[]{:S(2)}) collective-permute-start(f32[5,8,128]{2,1,0:T(8,128)S(1)} %get-tuple-element.18), channel_id=1, source_target_pairs={{0,1},{1,2},{2,3},{4,5},{5,6},{6,7},{8,9},{9,10},{10,11},{12,13},{... | collective-permute-start | bytes 61448 | tf_op jit(solution)/shard_map/ppermute | solution.py:435
  55.0 8.1 %collective-permute-start.6 = (f32[5,8,128]{2,1,0:T(8,128)S(1)}, f32[5,8,128]{2,1,0:T(8,128)S(1)}, u32[]{:S(2)}, u32[]{:S(2)}) collective-permute-start(f32[5,8,128]{2,1,0:T(8,128)S(1)} %get-tuple-element.19), channel_id=1, source_target_pairs={{1,0},{2,1},{3,2},{5,4},{6,5},{7,6},{9,8},{10,9},{11,10},{13,12},{... | collective-permute-start | bytes 61448 | tf_op jit(solution)/shard_map/ppermute | solution.py:434

commit v2 on v1

v2 whole, which is shorter than its diff:
```python
import math

import jax
import jax.numpy as jnp
import ml_dtypes
import numpy as np
from jax import lax
from jax.experimental import pallas as pl
from jax.experimental.pallas import tpu as pltpu
from jax.sharding import PartitionSpec as P

F = 5
BLADES = 22
VANES = 54
AXIAL = 8
HARMONICS = 4
MODES_PER = 128
MODES = 512
PITCH = 4096
K_MAX = 32
CAPACITY = 48
N_PITCH = 32
N_RAD = 4
RAD = 64
LANES = 128
GROUPS = 3
TABLE = GROUPS * LANES
SLOT_LANES = 64
PACKED = N_PITCH * SLOT_LANES

FLUX_PITCH = 0.25
FLUX_RAD = 0.25
FLUX_AXIAL = 0.5
FLUX_DIFFUSE = 0.1
RELAX = 0.7
OMEGA = 0.05
KAPPA = 2.0

f32 = jnp.float32
bf16 = jnp.bfloat16
SMEM = pl.BlockSpec(memory_space=pltpu.SMEM)
VMEM = pl.BlockSpec(memory_space=pltpu.VMEM)


def iota(shape, dim):
    return lax.broadcasted_iota(jnp.int32, shape, dim)


CLASS_LANES = 43
HALF_CLASS = 22


def fourier_tables():
    weights = np.zeros((2, 2, 9, LANES, LANES), np.float64)
    codes = np.full((2, 8, TABLE), -1, np.int32)
    j = np.arange(LANES)
    for b, (own, other) in enumerate(((BLADES, VANES), (VANES, BLADES))):
        used = np.zeros((9, 2), int)
        for n in range(1, HARMONICS + 1):
            for k in range(-K_MAX, K_MAX + 1):
                q = (n * own - k * other) // 2
                t = q % 16
                part, side = (t, 0) if t <= 8 else (16 - t, 1)
                lane = side * HALF_CLASS + used[part, side]
                used[part, side] += 1
                angle = 2.0 * np.pi * ((q * j) % 2048) / 2048.0
                weights[b, 0, part, :, lane] = np.cos(angle) / 64.0
                weights[b, 0, part, :, SLOT_LANES + lane] = np.sin(angle) / 64.0
                group, member = divmod(part, 3)
                codes[b, :, group * LANES + member * CLASS_LANES + lane] = n * 128 + k + K_MAX
        assert used.max() <= HALF_CLASS - 1
    high = weights[:, 0].astype(ml_dtypes.bfloat16)
    low = (weights[:, 0] - high.astype(np.float64)).astype(ml_dtypes.bfloat16)
    return np.stack([high, low], axis=1), codes


def mix(coefficients, parts):
    total = coefficients[0] * parts[0]
    for f in range(1, F):
        total = total + coefficients[f] * parts[f]
    return total


def flux_row(jac, k, g):
    return [jac[k, g, 0, f] for f in range(F)]


def sweep_row(jac, k, g):
    return [jac[0, g, k, f] for f in range(F)]


def exit_kernel(jacobian, flow, out, planes, jac, arrived):
    copies = [
        pltpu.make_async_copy(flow.at[0, f, pl.ds(AXIAL - 2, 2)], planes.at[f], arrived.at[f])
        for f in range(F)
    ]
    copies.append(pltpu.make_async_copy(jacobian, jac, arrived.at[F]))
    for copy in copies:
        copy.start()
    for copy in copies:
        copy.wait()
    now = [planes[f, 1] for f in range(F)]
    behind = [planes[f, 0] for f in range(F)]
    lane = iota((RAD, LANES), 1)
    row = iota((RAD, LANES), 0)
    change = [now[f] - behind[f] for f in range(F)]
    edges = jnp.zeros((RAD, LANES), f32)
    out[...] = jnp.zeros(out.shape, f32)
    for g in range(F):
        pitch = mix([FLUX_PITCH * c for c in flux_row(jac, 0, g)], now)
        radial = mix([FLUX_RAD * c for c in flux_row(jac, 1, g)], now)
        soft = FLUX_DIFFUSE * now[g]
        to_low, to_high = soft - pitch, soft + pitch
        inward, outward = soft - radial, soft + radial
        value = now[g] - mix([FLUX_AXIAL * c for c in flux_row(jac, 2, g)], change) - 4.0 * soft
        value = value + jnp.where(lane == LANES - 1, 0.0, pltpu.roll(to_low, LANES - 1, 1))
        value = value + jnp.where(lane == 0, 0.0, pltpu.roll(to_high, 1, 1))
        value = value + jnp.where(row == RAD - 1, 0.0, pltpu.roll(inward, RAD - 1, 0))
        value = value + jnp.where(row == 0, 0.0, pltpu.roll(outward, 1, 0))
        out[:, g, :] = value
        edges = jnp.where(lane == g, pltpu.roll(to_low, g, 1) if g else to_low, edges)
        edges = jnp.where(lane == 8 + g, pltpu.roll(to_high, 9 + g, 1), edges)
        out[g, 6:7, :] = inward[0:1]
        out[F + g, 6:7, :] = outward[RAD - 1 : RAD]
    out[:, 5, :] = edges


def halo_kernel(flow, pitch_near, pitch_far, rad_near, rad_far):
    lane = iota((RAD, LANES), 1)
    low = jnp.zeros((RAD, LANES), f32)
    high = jnp.zeros((RAD, LANES), f32)
    pitch_even = lax.rem(lax.axis_index("pitch"), 2) == 0
    rad_even = lax.rem(lax.axis_index("rad"), 2) == 0
    for f in range(F):
        for z in range(AXIAL):
            k = f * AXIAL + z
            block = flow[0, f, z]
            low = jnp.where(lane == k, pltpu.roll(block, k, 1) if k else block, low)
            high = jnp.where(lane == k, pltpu.roll(block, k + 1, 1), high)
            first, last = block[0:1], block[RAD - 1 : RAD]
            rad_near[f, z : z + 1, :] = jnp.where(rad_even, last, first)
            rad_far[f, z : z + 1, :] = jnp.where(rad_even, first, last)
    pitch_near[...] = jnp.where(pitch_even, high, low)
    pitch_far[...] = jnp.where(pitch_even, low, high)


DEPTH = 4
ROWS = 16


def flux_kernel(jac, flow, inflow, pitch_near, pitch_far, rad_near, rad_far, after, out, done, previous):
    step = pl.program_id(0)
    lane = iota((ROWS, LANES), 1)
    row = iota((ROWS, LANES), 0)
    pitch_even = lax.rem(lax.axis_index("pitch"), 2) == 0
    rad_even = lax.rem(lax.axis_index("rad"), 2) == 0

    @pl.when(step == 0)
    def _():
        previous[...] = inflow[0]

    pitch_jac = [[FLUX_PITCH * c for c in flux_row(jac, 0, g)] for g in range(F)]
    rad_jac = [[FLUX_RAD * c for c in flux_row(jac, 1, g)] for g in range(F)]
    axial_jac = [[FLUX_AXIAL * c for c in flux_row(jac, 2, g)] for g in range(F)]
    for z in range(DEPTH):
        axial = step * DEPTH + z
        for start in range(0, RAD, ROWS):
            rows = slice(start, start + ROWS)
            near, far = pitch_near[rows], pitch_far[rows]
            next_column = jnp.where(pitch_even, near, far)
            last_column = jnp.where(pitch_even, far, near)
            now, pitch, radial, change, total = [], [], [], [], []
            for f in range(F):
                block = flow[0, f, z, rows]
                k = f * AXIAL + axial
                right = pltpu.roll(next_column, LANES - 1 - k, 1)
                left = pltpu.roll(last_column, lax.bitwise_and(LANES - k, LANES - 1), 1)
                right = jnp.where(lane == LANES - 1, right, pltpu.roll(block, LANES - 1, 1))
                left = jnp.where(lane == 0, left, pltpu.roll(block, 1, 1))
                if start + ROWS < RAD:
                    above = flow[0, f, z, start + 1 : start + ROWS + 1]
                else:
                    edge_near, edge_far = rad_near[f, pl.ds(axial, 1), :], rad_far[f, pl.ds(axial, 1), :]
                    edge = jnp.where(rad_even, edge_near, edge_far)
                    above = jnp.where(row == ROWS - 1, edge, pltpu.roll(block, ROWS - 1, 0))
                if start:
                    below = flow[0, f, z, start - 1 : start + ROWS - 1]
                else:
                    edge_near, edge_far = rad_near[f, pl.ds(axial, 1), :], rad_far[f, pl.ds(axial, 1), :]
                    edge = jnp.where(rad_even, edge_far, edge_near)
                    below = jnp.where(row == 0, edge, pltpu.roll(block, 1, 0))
                behind = flow[0, f, z - 1, rows] if z else previous[f, rows]
                now.append(block)
                pitch.append(right - left)
                radial.append(above - below)
                change.append(block - behind)
                total.append((right + left) + (above + below))
            for g in range(F):
                flux = mix(pitch_jac[g], pitch) + mix(rad_jac[g], radial) + mix(axial_jac[g], change)
                soft = (1.0 - 4.0 * FLUX_DIFFUSE) * now[g] + FLUX_DIFFUSE * total[g]
                out[0, g, z, rows] = soft - flux
    for f in range(F):
        previous[f] = flow[0, f, DEPTH - 1]
    done[...] = jnp.zeros(done.shape, f32)


def table_kernel(dest, modes, codes, place, terms):
    source = 1 - lax.axis_index("row")
    own = jnp.where(source == 0, BLADES, VANES)
    other = jnp.where(source == 0, VANES, BLADES)
    dest_row = dest[source]
    listed = modes[source]
    code_row = jnp.concatenate(
        [listed[h : h + 1] + (K_MAX + 128 * (h + 1)) for h in range(HARMONICS)], axis=1
    )

    def column(row, block):
        part = row[:, block * LANES : (block + 1) * LANES]
        return jnp.transpose(jnp.broadcast_to(part, (LANES, LANES)))

    here = iota((LANES, LANES), 0)
    there = iota((LANES, LANES), 1)
    spread = iota((LANES, PACKED), 1)
    target = lax.axis_index("pitch") * SLOT_LANES + lax.bitwise_and(there, SLOT_LANES - 1)
    slot_code = jnp.zeros((1, LANES), jnp.int32)
    hits = []
    for block in range(MODES // LANES):
        dest_col = column(dest_row, block)
        before = jnp.zeros((LANES, LANES), f32)
        for past in range(block + 1):
            same = dest_col == dest_row[:, past * LANES : (past + 1) * LANES]
            if past == block:
                same = same & (there < here)
            before = before + same.astype(f32)
        rank = jnp.sum(before, axis=1, keepdims=True).astype(jnp.int32)
        slot = dest_col * SLOT_LANES + rank
        hits.append((slot[:, :1] == spread).astype(f32).astype(bf16))
        mine = jnp.where(slot == target, column(code_row, block), 0)
        slot_code = slot_code + jnp.sum(mine, axis=0, keepdims=True)
    hit = jnp.concatenate(hits, axis=0)
    code_table = codes[source]
    lane_code = jnp.concatenate([column(code_table[0:1], g) for g in range(GROUPS)], axis=0)
    listed_at = (lane_code[:, :1] == code_row).astype(f32).astype(bf16)
    place[...] = jnp.dot(listed_at, hit, preferred_element_type=f32).astype(bf16)
    n = lax.shift_right_logical(slot_code, 7)
    m = n * own - (lax.bitwise_and(slot_code, 127) - K_MAX) * other
    m = jnp.where(n > 0, m, 0)
    wave = lax.bitwise_and(m + PITCH // 2, PITCH - 1) - PITCH // 2
    sigma = OMEGA * n.astype(f32) * own.astype(f32)
    kappa = KAPPA * wave.astype(f32) / PITCH
    lane = iota((1, LANES), 1)
    sign = jnp.where(lane < SLOT_LANES, -1.0, 1.0)
    terms[...] = jnp.zeros(terms.shape, f32)
    terms[0:1] = sign * sigma
    terms[1:2] = sign * kappa
    terms[2:3] = RELAX / (4.0 + sigma * sigma)


def transform_kernel(cells, tables, *rest):
    out, weights, arrived = rest[-3:]
    mine = lax.axis_index("row")
    fetches = [
        pltpu.make_async_copy(tables.at[mine, part], weights.at[part], arrived.at[part])
        for part in range(2)
    ]
    for fetch in fetches:
        fetch.start()
    lane = iota((8, LANES), 1)
    sub = iota((8, LANES), 0)
    parts = []
    for half in range(2):
        x = [cells[2 * p + half] for p in range(N_PITCH)]
        z = [x[p] + x[p + 16] for p in range(16)]
        even = [None] + [z[p] + z[16 - p] for p in range(1, 8)]
        odd = [None] + [z[p] - z[16 - p] for p in range(1, 8)]
        columns = []
        for t in range(9):
            re = z[0] + z[8] if t % 2 == 0 else z[0] - z[8]
            im = jnp.zeros((8, LANES), f32)
            for p in range(1, 8):
                re = re + math.cos(2.0 * math.pi * ((t * p) % 16) / 16) * even[p]
                if t % 8:
                    im = im - math.sin(2.0 * math.pi * ((t * p) % 16) / 16) * odd[p]

            def edge(value, offset):
                spread = jnp.broadcast_to(value[5:6, :], (8, LANES))
                return jnp.sum(jnp.where(lane == sub + offset, spread, 0.0), axis=1, keepdims=True)

            cos, sin = math.cos(2.0 * math.pi * t / 16), math.sin(2.0 * math.pi * t / 16)
            low_re, high_re = edge(re, 0), edge(re, 8)
            low_im, high_im = (edge(im, 0), edge(im, 8)) if t % 8 else (0.0, 0.0)
            re = re + jnp.where(lane == LANES - 1, cos * low_re - sin * low_im, 0.0)
            re = re + jnp.where(lane == 0, cos * high_re + sin * high_im, 0.0)
            im = im + jnp.where(lane == LANES - 1, cos * low_im + sin * low_re, 0.0)
            im = im + jnp.where(lane == 0, cos * high_im - sin * high_re, 0.0)
            columns += [re, im]
        parts.append(columns)
    for fetch in fetches:
        fetch.wait()
    wide = iota((16, LANES), 1)
    spot = lax.bitwise_and(wide, SLOT_LANES - 1)
    side = jnp.where(spot < HALF_CLASS, 1.0, -1.0)
    for group in range(GROUPS):
        re_lanes = jnp.zeros((16, LANES), f32)
        im_lanes = jnp.zeros((16, LANES), f32)
        for member in range(3):
            t = group * 3 + member
            left = jnp.concatenate(
                [parts[0][2 * t], parts[1][2 * t], parts[0][2 * t + 1], parts[1][2 * t + 1]], axis=0
            )
            high = left.astype(bf16)
            low = (left - high.astype(f32)).astype(bf16)
            both = jnp.dot(
                jnp.concatenate([high, low], axis=0), weights[0, t], preferred_element_type=f32
            )
            value = both[:32] + both[32:]
            value = value + jnp.dot(high, weights[1, t], preferred_element_type=f32)
            of_re, of_im = value[:16], pltpu.roll(value[16:], SLOT_LANES, 1)
            re = jnp.where(wide < SLOT_LANES, of_re, -of_re) + side * of_im
            im = pltpu.roll(re, SLOT_LANES, 1)
            first = member * CLASS_LANES
            if first:
                re, im = pltpu.roll(re, first, 1), pltpu.roll(im, first, 1)
            own = (wide >= first) & (wide < first + CLASS_LANES)
            re_lanes = jnp.where(own, re, re_lanes)
            im_lanes = jnp.where(own, im, im_lanes)
        out[0:16, group * LANES : (group + 1) * LANES] = re_lanes
        out[16:32, group * LANES : (group + 1) * LANES] = im_lanes


def place_kernel(values, place, out):
    x = values[...]
    high = x.astype(bf16)
    low = (x - high.astype(f32)).astype(bf16)
    split = jnp.concatenate([high, low], axis=0)
    lane = iota((8, LANES), 1)
    for block in range(N_PITCH // 4):
        picked = jnp.dot(
            split, place[:, 2 * block * LANES : 2 * (block + 1) * LANES], preferred_element_type=f32
        )
        picked = picked[0:32] + picked[32:64]
        for pair in range(2):
            here = picked[:, pair * LANES : (pair + 1) * LANES]
            at = 8 * block + 4 * pair
            for half in range(2):
                re, im = here[half * 8 : half * 8 + 8], here[16 + half * 8 : 24 + half * 8]
                out[at + half] = jnp.where(lane < SLOT_LANES, re, pltpu.roll(im, SLOT_LANES, 1))
                out[at + 2 + half] = jnp.where(lane < SLOT_LANES, pltpu.roll(re, SLOT_LANES, 1), im)


SPAN = RAD + 8


def turned(value):
    return pltpu.roll(value, SLOT_LANES, 1)


def swept(start, inside, jac, terms):
    length = start[0].shape[0]
    sigma, kappa, scale = terms[0:1], terms[1:2], terms[2:3]
    start = [w * inside for w in start]
    current = start
    for _ in range(2):
        above = [pltpu.roll(w, length - 1, 0) for w in current]
        below = [pltpu.roll(w, 1, 0) for w in current]
        grade = [above[f] - below[f] for f in range(F)]
        update = []
        for g in range(F):
            w = current[g]
            applied = 2.0 * w - 0.5 * (above[g] + below[g]) + sigma * turned(w)
            applied = applied + kappa * turned(mix(sweep_row(jac, 0, g), current))
            applied = applied + 0.5 * mix(sweep_row(jac, 1, g), grade)
            rest = start[g] - applied
            update.append((w + scale * (2.0 * rest - sigma * turned(rest))) * inside)
        current = update
    return current


def domain(radius):
    rad = lax.axis_index("rad")
    outside = ((radius < 0) & (rad == 0)) | ((radius >= RAD) & (rad == N_RAD - 1))
    return jnp.where(outside, 0.0, 1.0)


def beyond(modes, f):
    index = iota((8, LANES), 0)
    before = jnp.where(index == 7, modes[f, 6:7, :], 0.0)
    after = jnp.where(index == 0, modes[F + f, 6:7, :], 0.0)
    return before, after


def edge_kernel(jac, modes, terms, after, near, far):
    index = iota((32, LANES), 0)
    inside = domain(jnp.where(index < 16, index - 8, index + RAD - 24))
    start = []
    for f in range(F):
        low, high = beyond(modes, f)
        start.append(jnp.concatenate([low, modes[0:8, f, :], modes[RAD - 8 :, f, :], high], axis=0))
    rad_even = lax.rem(lax.axis_index("rad"), 2) == 0
    for f, w in enumerate(swept(start, inside, jac, terms)):
        near[f] = jnp.where(rad_even, w[24:], w[:8])
        far[f] = jnp.where(rad_even, w[:8], w[24:])


def sweep_kernel(jac, modes, terms, main):
    inside = domain(iota((RAD + 16, LANES), 0) - 8)
    start = []
    for f in range(F):
        low, high = beyond(modes, f)
        start.append(jnp.concatenate([low, modes[:, f, :], high], axis=0))
    for f, w in enumerate(swept(start, inside, jac, terms)):
        main[f] = w[8 : 8 + RAD]


def finish_kernel(main, near, far, out):
    index = iota((8, LANES), 0)
    rad_even = lax.rem(lax.axis_index("rad"), 2) == 0
    for f in range(F):
        from_low = jnp.where(rad_even, far[f], near[f])
        from_high = jnp.where(rad_even, near[f], far[f])
        first = main[f, 0:8] + jnp.where(index < 3, from_low, 0.0)
        last = main[f, RAD - 8 :] + jnp.where(index > 4, from_high, 0.0)
        body = jnp.concatenate([first, main[f, 8 : RAD - 8], last], axis=0)
        turned = jnp.transpose(body)
        out[pl.ds(2 * f, CAPACITY, 2 * F), :] = turned[:CAPACITY]
        out[pl.ds(2 * f + 1, CAPACITY, 2 * F), :] = turned[SLOT_LANES : SLOT_LANES + CAPACITY]


def shape(*dims, dtype=f32):
    return jax.ShapeDtypeStruct(dims, dtype)


def cost(flops, size):
    return pl.CostEstimate(flops=flops, bytes_accessed=size, transcendentals=0)


BIG = pltpu.CompilerParams(vmem_limit_bytes=20 * 1024 * 1024)


ANY = pl.BlockSpec(memory_space=pl.ANY)


def swap_pairs(count, first, periodic):
    pairs = []
    for i in range(first, count, 2):
        other = (i + 1) % count
        if other > i or periodic:
            pairs += [(i, other), (other, i)]
    return pairs


def on_device(flow, inflow, flux_jacobian, sweep_jacobian, mode_index, destination):
    weights, codes = fourier_tables()
    flux_jac = jnp.transpose(flux_jacobian, (1, 2, 0, 3))
    sweep_jac = jnp.transpose(sweep_jacobian, (0, 2, 1, 3))
    near_pitch, far_pitch = swap_pairs(N_PITCH, 0, True), swap_pairs(N_PITCH, 1, True)
    near_rad, far_rad = swap_pairs(N_RAD, 0, False), swap_pairs(N_RAD, 1, False)

    pinned = pltpu.with_memory_space_constraint(flow, pltpu.HBM)

    face = pl.pallas_call(
        exit_kernel,
        out_shape=shape(RAD, 8, LANES),
        in_specs=[ANY, ANY],
        out_specs=VMEM,
        scratch_shapes=[
            pltpu.VMEM((F, 2, RAD, LANES), f32),
            pltpu.SMEM((3, F, 1, F), f32),
            pltpu.SemaphoreType.DMA((F + 1,)),
        ],
        compiler_params=BIG,
        cost_estimate=cost(4_000_000, 600_000),
    )(pltpu.with_memory_space_constraint(flux_jac, pltpu.HBM), pinned)
    cells = lax.all_to_all(face, "pitch", 0, 0, tiled=True)

    faces = pl.pallas_call(
        halo_kernel,
        out_shape=(shape(RAD, LANES), shape(RAD, LANES), shape(F, AXIAL, LANES), shape(F, AXIAL, LANES)),
        in_specs=[VMEM],
        out_specs=(VMEM,) * 4,
        compiler_params=BIG,
        cost_estimate=cost(4_000_000, 1_400_000),
    )(flow)
    pitch_near = lax.ppermute(faces[0], "pitch", near_pitch)
    pitch_far = lax.ppermute(faces[1], "pitch", far_pitch)
    place, terms = pl.pallas_call(
        table_kernel,
        out_shape=(shape(TABLE, PACKED, dtype=bf16), shape(8, LANES)),
        in_specs=[VMEM, VMEM, VMEM],
        out_specs=(VMEM,) * 2,
        compiler_params=BIG,
        cost_estimate=cost(2 * TABLE * MODES * PACKED, 2_000_000),
    )(jnp.swapaxes(destination, 1, 2), mode_index, codes)

    modes = pl.pallas_call(
        transform_kernel,
        out_shape=shape(32, TABLE),
        in_specs=[VMEM, ANY, ANY, ANY, ANY],
        out_specs=VMEM,
        scratch_shapes=[
            pltpu.VMEM((2, 9, LANES, LANES), bf16),
            pltpu.SemaphoreType.DMA((2,)),
        ],
        compiler_params=BIG,
        cost_estimate=cost(60_000_000, 3_000_000),
    )(
        cells,
        pltpu.with_memory_space_constraint(jnp.asarray(weights), pltpu.HBM),
        place,
        pitch_near,
        pitch_far,
    )
    modes = lax.ppermute(modes, "row", [(0, 1), (1, 0)])
    placed = pl.pallas_call(
        place_kernel,
        out_shape=shape(RAD, 8, LANES),
        in_specs=[VMEM, VMEM],
        out_specs=VMEM,
        compiler_params=BIG,
        cost_estimate=cost(150_000_000, 2_000_000),
    )(modes, place)
    amplitude = lax.all_to_all(placed, "pitch", 0, 0, tiled=True)

    rows = lax.optimization_barrier((faces[2], faces[3], placed))[:2]
    rad_near = lax.ppermute(rows[0], "rad", near_rad)
    rad_far = lax.ppermute(rows[1], "rad", far_rad)
    next_flow, flux_done = pl.pallas_call(
        flux_kernel,
        grid=(AXIAL // DEPTH,),
        out_shape=(shape(1, F, AXIAL, RAD, LANES), shape(8, LANES)),
        in_specs=[
            SMEM,
            pl.BlockSpec((1, F, DEPTH, RAD, LANES), lambda z: (0, 0, z, 0, 0)),
            pl.BlockSpec((1, F, RAD, LANES), lambda z: (0, 0, 0, 0)),
            pl.BlockSpec((RAD, LANES), lambda z: (0, 0)),
            pl.BlockSpec((RAD, LANES), lambda z: (0, 0)),
            pl.BlockSpec((F, AXIAL, LANES), lambda z: (0, 0, 0)),
            pl.BlockSpec((F, AXIAL, LANES), lambda z: (0, 0, 0)),
            ANY,
        ],
        out_specs=(
            pl.BlockSpec((1, F, DEPTH, RAD, LANES), lambda z: (0, 0, z, 0, 0)),
            pl.BlockSpec((8, LANES), lambda z: (0, 0)),
        ),
        scratch_shapes=[pltpu.VMEM((F, RAD, LANES), f32)],
        compiler_params=BIG,
        cost_estimate=cost(20_000_000, 3_000_000),
    )(flux_jac, flow, inflow, pitch_near, pitch_far, rad_near, rad_far, placed)

    near, far = pl.pallas_call(
        edge_kernel,
        out_shape=(shape(F, 8, LANES), shape(F, 8, LANES)),
        in_specs=[SMEM, VMEM, VMEM, ANY],
        out_specs=(VMEM,) * 2,
        compiler_params=BIG,
        cost_estimate=cost(2_000_000, 300_000),
    )(sweep_jac, amplitude, terms, flux_done)
    near = lax.ppermute(near, "rad", near_rad)
    far = lax.ppermute(far, "rad", far_rad)
    main = pl.pallas_call(
        sweep_kernel,
        out_shape=shape(F, RAD, LANES),
        in_specs=[SMEM, VMEM, VMEM],
        out_specs=VMEM,
        compiler_params=BIG,
        cost_estimate=cost(8_000_000, 500_000),
    )(sweep_jac, amplitude, terms)
    response = pl.pallas_call(
        finish_kernel,
        out_shape=shape(CAPACITY * F * 2, RAD),
        in_specs=[VMEM] * 3,
        out_specs=VMEM,
        compiler_params=BIG,
        cost_estimate=cost(1_000_000, 800_000),
    )(main, near, far)
    response = response.reshape(1, 1, CAPACITY, F, 2, RAD)
    return next_flow, jnp.swapaxes(response, 3, 4)


def solution(mesh):
    placed = (
        P("row", None, None, "rad", "pitch"),
        P("row", None, "rad", "pitch"),
        P("row", None, None, None),
        P("row", None, None, None),
        P(),
        P(),
    )
    return jax.shard_map(
        on_device,
        mesh=mesh,
        in_specs=placed,
        out_specs=(
            P("row", None, None, "rad", "pitch"),
            P("row", "pitch", None, None, None, "rad"),
        ),
        check_vma=False,
    )
```

time: 64.7 us -> 59 us (0.912)
  local copies, waits for them, and re-layouts: 5.38 us -> 0.04 us
  starting transfers between devices: 32.5 us -> 28.2 us
  waiting for transfers between devices: 11.9 us -> 15.3 us
  Pallas kernels: 13.5 us -> 14.2 us
    ppermute x6, waiting for transfers between devices: 0.02 us -> 8.82 us  [the longest x1 3.09 us: on_device(): rad_far = lax.ppermute(rows[1], 'rad', far_rad)]
    all_to_all x1, waiting for transfers between devices: 10.1 us -> 2.4 us  [on_device(): cells = lax.all_to_all(face, 'pitch', 0, 0, tiled=True)]
    ppermute x6, starting transfers between devices: 17 us -> 12.5 us  [the longest x1 4.26 us: on_device(): pitch_far = lax.ppermute(faces[1], 'pitch', far_pitch)]
    unnamed x16 -> x14, local copies, waits for them, and re-layouts: 3.57 us -> 0.04 us
    squeeze x1 -> x0, local copies, waits for them, and re-layouts: 1.82 us -> none  [on_device(): lax.dynamic_index_in_dim(jnp.asarray(weights), row, 0, keepdims=False)]
    ppermute x1, waiting for transfers between devices: 0.01 us -> 1.22 us  [on_device(): modes = lax.ppermute(modes, 'row', [(0, 1), (1, 0)])]
    all_to_all x1, waiting for transfers between devices: 1.78 us -> 2.9 us  [on_device(): amplitude = lax.all_to_all(placed, 'pitch', 0, 0, tiled=True)]
    pallas_call x1, Pallas kernels: 0.52 us -> 1.59 us  [on_device(): pl.pallas_call(transform_kernel, out_shape=shape(32, TABLE), in_specs=[VM...]
  transfers between devices with their start and end apart: 9 -> 9, of which waited for: 2 -> 7; matrix products, arithmetic and copies ran while one was open for 4% -> 0% of each run, Pallas kernels for 15% -> 13%
where the time goes in v2:
time: 59 us; the launch traced here: 58.6 us
  starting transfers between devices  28.2 us (48%)
  waiting for transfers between devices  15.3 us (26%)
  Pallas kernels  14.2 us (24%)
  between operations  0.79 us (1%)
    all_to_all x1, starting transfers between devices, on_device(): cells = lax.all_to_all(face, 'pitch', 0, 0, tiled=True)  11.6 us
    ppermute x1, starting transfers between devices, on_device(): pitch_far = lax.ppermute(faces[1], 'pitch', far_pitch)  4.26 us
    all_to_all x1, starting transfers between devices, on_device(): amplitude = lax.all_to_all(placed, 'pitch', 0, 0, tiled=True)  4 us
    pallas_call x1, Pallas kernels, on_device(): pl.pallas_call(flux_kernel, grid=(AXIAL // DEPTH,), out_shape=(shape(1, F...  3.69 us
    ppermute x1, waiting for transfers between devices, on_device(): rad_far = lax.ppermute(rows[1], 'rad', far_rad)  3.09 us
    all_to_all x1, waiting for transfers between devices, on_device(): amplitude = lax.all_to_all(placed, 'pitch', 0, 0, tiled=True)  2.9 us
    ppermute x1, waiting for transfers between devices, on_device(): pitch_far = lax.ppermute(faces[1], 'pitch', far_pitch)  2.73 us
    all_to_all x1, waiting for transfers between devices, on_device(): cells = lax.all_to_all(face, 'pitch', 0, 0, tiled=True)  2.4 us
  transfers between devices with their start and end apart: 9, of which 7 were waited for; matrix products, arithmetic and copies ran while one was open for 0% of the time, Pallas kernels for 13%

profile of v2, /device:TPU:4, one launch (start us, length us, event | category | flops | bytes accessed | tf_op | source)
XLA Modules:
  0.0 58.6 jit_solution(6358844221600181517)
XLA Ops:
  0.6 2.2 %shard_map.96 = f32[64,8,128]{2,1,0:T(8,128)} custom-call(f32[3,5,1,5]{3,2,1,0:T(1,128)} %bitcast.6, f32[1,5,8,64,128]{4,3,2,1,0:T(8,128)} %flow.5), custom_call_target="tpu_custom_call" | custom-call | flops 4000000 | bytes 600000 | tf_op jit(solution)/shard_map/pallas_call | solution.py:461
  2.9 0.0 copy-start.4
  2.9 0.0 copy-start.5
  2.9 0.0 copy-start.6
  2.9 11.6 %all-to-all-start = ((f32[64,8,128]{2,1,0:T(8,128)}), f32[64,8,128]{2,1,0:T(8,128)S(1)}, u32[]{:S(2)}, u32[]{:S(2)}) async-start(f32[64,8,128]{2,1,0:T(8,128)} %shard_map.96), calls=%async_computation | async-start | bytes 524288 | tf_op jit(solution)/shard_map/all_to_all | solution.py:474
  14.6 0.7 %shard_map.95 = (f32[64,128]{1,0:T(8,128)S(1)}, f32[64,128]{1,0:T(8,128)S(1)}, f32[5,8,128]{2,1,0:T(8,128)S(1)}, f32[5,8,128]{2,1,0:T(8,128)S(1)}) custom-call(f32[1,5,8,64,128]{4,3,2,1,0:T(8,128)S(1)} %copy-done), custom_call_target="tpu_custom_call" | custom-call | flops 4000000 | bytes 1400000 | tf_op jit(solution)/shard_map/pallas_call | solution.py:476
  15.3 1.9 %collective-permute-start = (f32[64,128]{1,0:T(8,128)S(1)}, f32[64,128]{1,0:T(8,128)S(1)}, u32[]{:S(2)}, u32[]{:S(2)}) collective-permute-start(f32[64,128]{1,0:T(8,128)S(1)} %get-tuple-element.14), channel_id=1, source_target_pairs={{0,4},{4,0},{8,12},{12,8},{16,20},{20,16},{24,28},{28,24},{32,36},... | collective-permute-start | bytes 98312 | tf_op jit(solution)/shard_map/ppermute | solution.py:484
  17.2 4.3 %collective-permute-start.1 = (f32[64,128]{1,0:T(8,128)S(1)}, f32[64,128]{1,0:T(8,128)S(1)}, u32[]{:S(2)}, u32[]{:S(2)}) collective-permute-start(f32[64,128]{1,0:T(8,128)S(1)} %get-tuple-element.15), channel_id=1, source_target_pairs={{4,8},{8,4},{12,16},{16,12},{20,24},{24,20},{28,32},{32,28},{36,40... | collective-permute-start | bytes 98312 | tf_op jit(solution)/shard_map/ppermute | solution.py:485
  21.5 1.5 %shard_map.97 = (bf16[384,2048]{1,0:T(8,128)(2,1)S(1)}, f32[8,128]{1,0:T(8,128)S(1)}) custom-call(s32[2,1,512]{2,1,0:T(1,128)S(1)} %bitcast.10, s32[2,4,128]{2,1,0:T(4,128)S(1)} %copy-done.5, s32[2,8,384]{2,1,0:T(8,128)S(1)} %copy-done.6), custom_call_target="tpu_custom_call" | custom-call | flops 805306368 | bytes 2000000 | tf_op jit(solution)/shard_map/pallas_call | solution.py:486
  23.0 0.0 collective-permute-done.rest_1_.pitch_near
  23.0 2.7 %collective-permute-done.1.rest_2_.pitch_far = f32[64,128]{1,0:T(8,128)S(1)} collective-permute-done((f32[64,128]{1,0:T(8,128)S(1)}, f32[64,128]{1,0:T(8,128)S(1)}, u32[]{:S(2)}, u32[]{:S(2)}) %collective-permute-start.1) | collective-permute-done | bytes 32800 | tf_op jit(solution)/shard_map/ppermute | solution.py:485
  25.8 2.4 %all-to-all-done.cells = f32[64,8,128]{2,1,0:T(8,128)S(1)} async-done(((f32[64,8,128]{2,1,0:T(8,128)}), f32[64,8,128]{2,1,0:T(8,128)S(1)}, u32[]{:S(2)}, u32[]{:S(2)}) %all-to-all-start) | async-done | bytes 262176 | tf_op jit(solution)/shard_map/all_to_all | solution.py:474
  28.2 1.6 %shard_map.98 = f32[32,384]{1,0:T(8,128)S(1)} custom-call(f32[64,8,128]{2,1,0:T(8,128)S(1)} %all-to-all-done.cells, bf16[2,2,9,128,128]{4,3,2,1,0:T(8,128)(2,1)} %constant.5.clone.tables, bf16[384,2048]{1,0:T(8,128)(2,1)S(1)} %get-tuple-element.18.rest_0_.place, f32[64,128]{1,0:T(8,128)S(1)} %collective-permute-done.rest_1_.pitch_near, ...), custom_call_target="tpu_custom_call" | custom-call | flops 60000000 | bytes 3000000 | tf_op jit(solution)/shard_map/pallas_call | solution.py:495
  29.8 0.0 copy-start.1
  29.8 0.0 copy-start.2
  29.8 0.1 collective-permute-start.2
  29.9 1.2 %collective-permute-done.2.values = f32[32,384]{1,0:T(8,128)S(1)} collective-permute-done((f32[32,384]{1,0:T(8,128)S(1)}, f32[32,384]{1,0:T(8,128)S(1)}, u32[]{:S(2)}, u32[]{:S(2)}) %collective-permute-start.2) | collective-permute-done | bytes 49184 | tf_op jit(solution)/shard_map/ppermute | solution.py:513
  31.1 1.2 %shard_map.99.after = f32[64,8,128]{2,1,0:T(8,128)} custom-call(f32[32,384]{1,0:T(8,128)S(1)} %collective-permute-done.2.values, bf16[384,2048]{1,0:T(8,128)(2,1)S(1)} %get-tuple-element.18.rest_0_.place), custom_call_target="tpu_custom_call" | custom-call | flops 150000000 | bytes 2000000 | tf_op jit(solution)/shard_map/pallas_call | solution.py:514
  32.3 4.0 %all-to-all-start.1 = ((f32[64,8,128]{2,1,0:T(8,128)}), f32[64,8,128]{2,1,0:T(8,128)S(1)}, u32[]{:S(2)}, u32[]{:S(2)}) async-start(f32[64,8,128]{2,1,0:T(8,128)} %shard_map.99.after), calls=%async_computation.1 | async-start | bytes 524288 | tf_op jit(solution)/shard_map/all_to_all | solution.py:522
  36.3 1.3 %collective-permute-start.3 = (f32[5,8,128]{2,1,0:T(8,128)S(1)}, f32[5,8,128]{2,1,0:T(8,128)S(1)}, u32[]{:S(2)}, u32[]{:S(2)}) collective-permute-start(f32[5,8,128]{2,1,0:T(8,128)S(1)} %get-tuple-element.19), channel_id=1, source_target_pairs={{0,1},{1,0},{2,3},{3,2},{4,5},{5,4},{6,7},{7,6},{8,9},{9,8},{10,11... | collective-permute-start | bytes 61448 | tf_op jit(solution)/shard_map/ppermute | solution.py:525
  37.6 1.9 %collective-permute-start.4 = (f32[5,8,128]{2,1,0:T(8,128)S(1)}, f32[5,8,128]{2,1,0:T(8,128)S(1)}, u32[]{:S(2)}, u32[]{:S(2)}) collective-permute-start(f32[5,8,128]{2,1,0:T(8,128)S(1)} %get-tuple-element.20), channel_id=1, source_target_pairs={{1,2},{2,1},{5,6},{6,5},{9,10},{10,9},{13,14},{14,13},{17,18},{18,... | collective-permute-start | bytes 61448 | tf_op jit(solution)/shard_map/ppermute | solution.py:526
  39.5 0.7 %collective-permute-done.3.rad_near = f32[5,8,128]{2,1,0:T(8,128)S(1)} collective-permute-done((f32[5,8,128]{2,1,0:T(8,128)S(1)}, f32[5,8,128]{2,1,0:T(8,128)S(1)}, u32[]{:S(2)}, u32[]{:S(2)}) %collective-permute-start.3) | collective-permute-done | bytes 20512 | tf_op jit(solution)/shard_map/ppermute | solution.py:525
  40.2 3.1 %collective-permute-done.4.rad_far = f32[5,8,128]{2,1,0:T(8,128)S(1)} collective-permute-done((f32[5,8,128]{2,1,0:T(8,128)S(1)}, f32[5,8,128]{2,1,0:T(8,128)S(1)}, u32[]{:S(2)}, u32[]{:S(2)}) %collective-permute-start.4) | collective-permute-done | bytes 20512 | tf_op jit(solution)/shard_map/ppermute | solution.py:526
  43.3 3.7 %shard_map.100 = (f32[1,5,8,64,128]{4,3,2,1,0:T(8,128)}, f32[8,128]{1,0:T(8,128)S(1)}) custom-call(f32[3,5,1,5]{3,2,1,0:T(1,128)S(1)} %bitcast.7, f32[1,5,8,64,128]{4,3,2,1,0:T(8,128)S(1)} %copy-done, f32[1,5,64,128]{3,2,1,0:T(8,128)S(1)} %copy-done.1, f32[64,128]{1,0:T(8,128)S(1)} %collective-permute-done.rest_1_.pitch_near, ...), custom_call_target="tpu_custom_call" | custom-call | flops 20000000 | bytes 3000000 | tf_op jit(solution)/shard_map/pallas_call | solution.py:527
  46.9 2.9 %all-to-all-done.1.modes = f32[64,8,128]{2,1,0:T(8,128)S(1)} async-done(((f32[64,8,128]{2,1,0:T(8,128)}), f32[64,8,128]{2,1,0:T(8,128)S(1)}, u32[]{:S(2)}, u32[]{:S(2)}) %all-to-all-start.1) | async-done | bytes 262176 | tf_op jit(solution)/shard_map/all_to_all | solution.py:522
  49.8 0.9 %shard_map.102 = (f32[5,8,128]{2,1,0:T(8,128)S(1)}, f32[5,8,128]{2,1,0:T(8,128)S(1)}) custom-call(f32[1,5,2,5]{3,2,1,0:T(2,128)S(1)} %bitcast.8, f32[64,8,128]{2,1,0:T(8,128)S(1)} %all-to-all-done.1.modes, f32[8,128]{1,0:T(8,128)S(1)} %get-tuple-element.22.terms, f32[8,128]{1,0:T(8,128)S(1)} %get-tuple-element.23.after), custom_call_target="tpu_custom_call" | custom-call | flops 2000000 | bytes 300000 | tf_op jit(solution)/shard_map/pallas_call | solution.py:550
  50.8 1.3 %collective-permute-start.5 = (f32[5,8,128]{2,1,0:T(8,128)S(1)}, f32[5,8,128]{2,1,0:T(8,128)S(1)}, u32[]{:S(2)}, u32[]{:S(2)}) collective-permute-start(f32[5,8,128]{2,1,0:T(8,128)S(1)} %get-tuple-element.24), channel_id=1, source_target_pairs={{0,1},{1,0},{2,3},{3,2},{4,5},{5,4},{6,7},{7,6},{8,9},{9,8},{10,11... | collective-permute-start | bytes 61448 | tf_op jit(solution)/shard_map/ppermute | solution.py:558
  52.1 1.9 %collective-permute-start.6 = (f32[5,8,128]{2,1,0:T(8,128)S(1)}, f32[5,8,128]{2,1,0:T(8,128)S(1)}, u32[]{:S(2)}, u32[]{:S(2)}) collective-permute-start(f32[5,8,128]{2,1,0:T(8,128)S(1)} %get-tuple-element.25), channel_id=1, source_target_pairs={{1,2},{2,1},{5,6},{6,5},{9,10},{10,9},{13,14},{14,13},{17,18},{18,... | collective-permute-start | bytes 61448 | tf_op jit(solution)/shard_map/ppermute | solution.py:559
  54.0 1.4 %shard_map.101.main = f32[5,64,128]{2,1,0:T(8,128)S(1)} custom-call(f32[1,5,2,5]{3,2,1,0:T(2,128)S(1)} %bitcast.9, f32[64,8,128]{2,1,0:T(8,128)S(1)} %all-to-all-done.1.modes, f32[8,128]{1,0:T(8,128)S(1)} %get-tuple-element.22.terms), custom_call_target="tpu_custom_call" | custom-call | flops 8000000 | bytes 500000 | tf_op jit(solution)/shard_map/pallas_call | solution.py:560
  55.4 0.0 collective-permute-done.5.near
  55.4 2.3 %collective-permute-done.6.far = f32[5,8,128]{2,1,0:T(8,128)S(1)} collective-permute-done((f32[5,8,128]{2,1,0:T(8,128)S(1)}, f32[5,8,128]{2,1,0:T(8,128)S(1)}, u32[]{:S(2)}, u32[]{:S(2)}) %collective-permute-start.6) | collective-permute-done | bytes 20512 | tf_op jit(solution)/shard_map/ppermute | solution.py:559
  57.7 0.9 %shard_map.103 = f32[480,64]{1,0:T(8,128)} custom-call(f32[5,64,128]{2,1,0:T(8,128)S(1)} %shard_map.101.main, f32[5,8,128]{2,1,0:T(8,128)S(1)} %collective-permute-done.5.near, f32[5,8,128]{2,1,0:T(8,128)S(1)} %collective-permute-done.6.far), custom_call_target="tpu_custom_call" | custom-call | flops 1000000 | bytes 800000 | tf_op jit(solution)/shard_map/pallas_call | solution.py:568
  (9 shorter events, 0.0 us)
Async XLA Ops:
  0.6 13.9 %copy-start = (f32[1,5,8,64,128]{4,3,2,1,0:T(8,128)S(1)}, f32[1,5,8,64,128]{4,3,2,1,0:T(8,128)}, u32[]{:S(2)}) copy-start(f32[1,5,8,64,128]{4,3,2,1,0:T(8,128)} %flow.5) | copy-start | bytes 3932164
  2.9 18.6 %copy-start.4 = (s32[2,512,1]{1,2,0:T(1,128)S(1)}, s32[2,512,1]{1,2,0:T(1,128)}, u32[]{:S(2)}) copy-start(s32[2,512,1]{1,2,0:T(1,128)} %param.13) | copy-start | bytes 12292
  2.9 18.6 %copy-start.5 = (s32[2,4,128]{2,1,0:T(4,128)S(1)}, s32[2,4,128]{2,1,0:T(4,128)}, u32[]{:S(2)}) copy-start(s32[2,4,128]{2,1,0:T(4,128)} %modes.1) | copy-start | bytes 12292
  2.9 18.6 %copy-start.6 = (s32[2,8,384]{2,1,0:T(8,128)S(1)}, s32[2,8,384]{2,1,0:T(8,128)}, u32[]{:S(2)}) copy-start(s32[2,8,384]{2,1,0:T(8,128)} %constant.4.clone.codes) | copy-start | bytes 73732
  2.9 25.2 %all-to-all-start = ((f32[64,8,128]{2,1,0:T(8,128)}), f32[64,8,128]{2,1,0:T(8,128)S(1)}, u32[]{:S(2)}, u32[]{:S(2)}) async-start(f32[64,8,128]{2,1,0:T(8,128)} %shard_map.96), calls=%async_computation | async-start | bytes 524288 | tf_op jit(solution)/shard_map/all_to_all | solution.py:474
  15.3 7.7 %collective-permute-start = (f32[64,128]{1,0:T(8,128)S(1)}, f32[64,128]{1,0:T(8,128)S(1)}, u32[]{:S(2)}, u32[]{:S(2)}) collective-permute-start(f32[64,128]{1,0:T(8,128)S(1)} %get-tuple-element.14), channel_id=1, source_target_pairs={{0,4},{4,0},{8,12},{12,8},{16,20},{20,16},{24,28},{28,24},{32,36},... | collective-permute-start | bytes 98312 | tf_op jit(solution)/shard_map/ppermute | solution.py:484
  17.2 8.6 %collective-permute-start.1 = (f32[64,128]{1,0:T(8,128)S(1)}, f32[64,128]{1,0:T(8,128)S(1)}, u32[]{:S(2)}, u32[]{:S(2)}) collective-permute-start(f32[64,128]{1,0:T(8,128)S(1)} %get-tuple-element.15), channel_id=1, source_target_pairs={{4,8},{8,4},{12,16},{16,12},{20,24},{24,20},{28,32},{32,28},{36,40... | collective-permute-start | bytes 98312 | tf_op jit(solution)/shard_map/ppermute | solution.py:485
  29.8 13.5 %copy-start.1 = (f32[1,5,64,128]{3,2,1,0:T(8,128)S(1)}, f32[1,5,64,128]{3,2,1,0:T(8,128)}, u32[]{:S(2)}) copy-start(f32[1,5,64,128]{3,2,1,0:T(8,128)} %inflow.1) | copy-start | bytes 491524
  29.8 13.5 %copy-start.2 = (f32[1,3,5,5]{3,0,2,1:T(1,128)S(1)}, f32[1,3,5,5]{3,0,2,1:T(1,128)}, u32[]{:S(2)}) copy-start(f32[1,3,5,5]{3,0,2,1:T(1,128)} %param.10) | copy-start | bytes 904
  29.8 1.3 %collective-permute-start.2 = (f32[32,384]{1,0:T(8,128)S(1)}, f32[32,384]{1,0:T(8,128)S(1)}, u32[]{:S(2)}, u32[]{:S(2)}) collective-permute-start(f32[32,384]{1,0:T(8,128)S(1)} %shard_map.98), channel_id=1, source_target_pairs={{0,128},{128,0},{1,129},{129,1},{2,130},{130,2},{3,131},{131,3},{4... | collective-permute-start | bytes 147464 | tf_op jit(solution)/shard_map/ppermute | solution.py:513
  32.3 17.6 %copy-start.3 = (f32[1,2,5,5]{3,1,2,0:T(2,128)S(1)}, f32[1,2,5,5]{3,1,2,0:T(2,128)}, u32[]{:S(2)}) copy-start(f32[1,2,5,5]{3,1,2,0:T(2,128)} %param.11) | copy-start | bytes 604
  32.3 17.6 %all-to-all-start.1 = ((f32[64,8,128]{2,1,0:T(8,128)}), f32[64,8,128]{2,1,0:T(8,128)S(1)}, u32[]{:S(2)}, u32[]{:S(2)}) async-start(f32[64,8,128]{2,1,0:T(8,128)} %shard_map.99.after), calls=%async_computation.1 | async-start | bytes 524288 | tf_op jit(solution)/shard_map/all_to_all | solution.py:522
  36.3 3.9 %collective-permute-start.3 = (f32[5,8,128]{2,1,0:T(8,128)S(1)}, f32[5,8,128]{2,1,0:T(8,128)S(1)}, u32[]{:S(2)}, u32[]{:S(2)}) collective-permute-start(f32[5,8,128]{2,1,0:T(8,128)S(1)} %get-tuple-element.19), channel_id=1, source_target_pairs={{0,1},{1,0},{2,3},{3,2},{4,5},{5,4},{6,7},{7,6},{8,9},{9,8},{10,11... | collective-permute-start | bytes 61448 | tf_op jit(solution)/shard_map/ppermute | solution.py:525
  37.6 5.7 %collective-permute-start.4 = (f32[5,8,128]{2,1,0:T(8,128)S(1)}, f32[5,8,128]{2,1,0:T(8,128)S(1)}, u32[]{:S(2)}, u32[]{:S(2)}) collective-permute-start(f32[5,8,128]{2,1,0:T(8,128)S(1)} %get-tuple-element.20), channel_id=1, source_target_pairs={{1,2},{2,1},{5,6},{6,5},{9,10},{10,9},{13,14},{14,13},{17,18},{18,... | collective-permute-start | bytes 61448 | tf_op jit(solution)/shard_map/ppermute | solution.py:526
  50.8 4.6 %collective-permute-start.5 = (f32[5,8,128]{2,1,0:T(8,128)S(1)}, f32[5,8,128]{2,1,0:T(8,128)S(1)}, u32[]{:S(2)}, u32[]{:S(2)}) collective-permute-start(f32[5,8,128]{2,1,0:T(8,128)S(1)} %get-tuple-element.24), channel_id=1, source_target_pairs={{0,1},{1,0},{2,3},{3,2},{4,5},{5,4},{6,7},{7,6},{8,9},{9,8},{10,11... | collective-permute-start | bytes 61448 | tf_op jit(solution)/shard_map/ppermute | solution.py:558
  52.1 5.7 %collective-permute-start.6 = (f32[5,8,128]{2,1,0:T(8,128)S(1)}, f32[5,8,128]{2,1,0:T(8,128)S(1)}, u32[]{:S(2)}, u32[]{:S(2)}) collective-permute-start(f32[5,8,128]{2,1,0:T(8,128)S(1)} %get-tuple-element.25), channel_id=1, source_target_pairs={{1,2},{2,1},{5,6},{6,5},{9,10},{10,9},{13,14},{14,13},{17,18},{18,... | collective-permute-start | bytes 61448 | tf_op jit(solution)/shard_map/ppermute | solution.py:559

commit v3 on v2

--- a/solution.py
+++ b/solution.py
@@ -205,7 +205,7 @@
 
 
 def table_kernel(dest, modes, codes, place, terms):
-    source = 1 - lax.axis_index("row")
+    source = lax.axis_index("row")
     own = jnp.where(source == 0, BLADES, VANES)
     other = jnp.where(source == 0, VANES, BLADES)
     dest_row = dest[source]
@@ -256,8 +256,8 @@
     terms[2:3] = RELAX / (4.0 + sigma * sigma)
 
 
-def transform_kernel(cells, tables, *rest):
-    out, weights, arrived = rest[-3:]
+def spectrum_kernel(cells, tables, place, *rest):
+    out, values, weights, arrived = rest[-4:]
     mine = lax.axis_index("row")
     fetches = [
         pltpu.make_async_copy(tables.at[mine, part], weights.at[part], arrived.at[part])
@@ -324,11 +324,8 @@
             own = (wide >= first) & (wide < first + CLASS_LANES)
             re_lanes = jnp.where(own, re, re_lanes)
             im_lanes = jnp.where(own, im, im_lanes)
-        out[0:16, group * LANES : (group + 1) * LANES] = re_lanes
-        out[16:32, group * LANES : (group + 1) * LANES] = im_lanes
-
-
-def place_kernel(values, place, out):
+        values[0:16, group * LANES : (group + 1) * LANES] = re_lanes
+        values[16:32, group * LANES : (group + 1) * LANES] = im_lanes
     x = values[...]
     high = x.astype(bf16)
     low = (x - high.astype(f32)).astype(bf16)
@@ -389,27 +386,17 @@
     return before, after
 
 
-def edge_kernel(jac, modes, terms, after, near, far):
-    index = iota((32, LANES), 0)
-    inside = domain(jnp.where(index < 16, index - 8, index + RAD - 24))
-    start = []
-    for f in range(F):
-        low, high = beyond(modes, f)
-        start.append(jnp.concatenate([low, modes[0:8, f, :], modes[RAD - 8 :, f, :], high], axis=0))
+def sweep_kernel(jac, modes, terms, after, main, near, far):
+    inside = domain(iota((RAD + 16, LANES), 0) - 8)
     rad_even = lax.rem(lax.axis_index("rad"), 2) == 0
-    for f, w in enumerate(swept(start, inside, jac, terms)):
-        near[f] = jnp.where(rad_even, w[24:], w[:8])
-        far[f] = jnp.where(rad_even, w[:8], w[24:])
-
-
-def sweep_kernel(jac, modes, terms, main):
-    inside = domain(iota((RAD + 16, LANES), 0) - 8)
     start = []
     for f in range(F):
         low, high = beyond(modes, f)
         start.append(jnp.concatenate([low, modes[:, f, :], high], axis=0))
     for f, w in enumerate(swept(start, inside, jac, terms)):
         main[f] = w[8 : 8 + RAD]
+        near[f] = jnp.where(rad_even, w[8 + RAD :], w[:8])
+        far[f] = jnp.where(rad_even, w[:8], w[8 + RAD :])
 
 
 def finish_kernel(main, near, far, out):
@@ -449,10 +436,13 @@
     return pairs
 
 
+def across(pairs):
+    return [(row * N_RAD + i, (1 - row) * N_RAD + j) for row in range(2) for i, j in pairs]
+
+
 def on_device(flow, inflow, flux_jacobian, sweep_jacobian, mode_index, destination):
     weights, codes = fourier_tables()
     flux_jac = jnp.transpose(flux_jacobian, (1, 2, 0, 3))
-    sweep_jac = jnp.transpose(sweep_jacobian, (0, 2, 1, 3))
     near_pitch, far_pitch = swap_pairs(N_PITCH, 0, True), swap_pairs(N_PITCH, 1, True)
     near_rad, far_rad = swap_pairs(N_RAD, 0, False), swap_pairs(N_RAD, 1, False)
 
@@ -481,6 +471,9 @@
         compiler_params=BIG,
         cost_estimate=cost(4_000_000, 1_400_000),
     )(flow)
+    sweep_jac = jnp.transpose(sweep_jacobian, (0, 2, 1, 3))
+    sweep_jac = lax.optimization_barrier((sweep_jac, faces[0]))[0]
+    sweep_jac = lax.ppermute(sweep_jac, "row", [(0, 1), (1, 0)])
     pitch_near = lax.ppermute(faces[0], "pitch", near_pitch)
     pitch_far = lax.ppermute(faces[1], "pitch", far_pitch)
     place, terms = pl.pallas_call(
@@ -492,33 +485,26 @@
         cost_estimate=cost(2 * TABLE * MODES * PACKED, 2_000_000),
     )(jnp.swapaxes(destination, 1, 2), mode_index, codes)
 
-    modes = pl.pallas_call(
-        transform_kernel,
-        out_shape=shape(32, TABLE),
-        in_specs=[VMEM, ANY, ANY, ANY, ANY],
+    placed = pl.pallas_call(
+        spectrum_kernel,
+        out_shape=shape(RAD, 8, LANES),
+        in_specs=[VMEM, ANY, VMEM, ANY, ANY, ANY],
         out_specs=VMEM,
         scratch_shapes=[
+            pltpu.VMEM((32, TABLE), f32),
             pltpu.VMEM((2, 9, LANES, LANES), bf16),
             pltpu.SemaphoreType.DMA((2,)),
         ],
         compiler_params=BIG,
-        cost_estimate=cost(60_000_000, 3_000_000),
+        cost_estimate=cost(200_000_000, 3_000_000),
     )(
         cells,
         pltpu.with_memory_space_constraint(jnp.asarray(weights), pltpu.HBM),
         place,
         pitch_near,
         pitch_far,
+        sweep_jac,
     )
-    modes = lax.ppermute(modes, "row", [(0, 1), (1, 0)])
-    placed = pl.pallas_call(
-        place_kernel,
-        out_shape=shape(RAD, 8, LANES),
-        in_specs=[VMEM, VMEM],
-        out_specs=VMEM,
-        compiler_params=BIG,
-        cost_estimate=cost(150_000_000, 2_000_000),
-    )(modes, place)
     amplitude = lax.all_to_all(placed, "pitch", 0, 0, tiled=True)
 
     rows = lax.optimization_barrier((faces[2], faces[3], placed))[:2]
@@ -547,24 +533,17 @@
         cost_estimate=cost(20_000_000, 3_000_000),
     )(flux_jac, flow, inflow, pitch_near, pitch_far, rad_near, rad_far, placed)
 
-    near, far = pl.pallas_call(
-        edge_kernel,
-        out_shape=(shape(F, 8, LANES), shape(F, 8, LANES)),
+    main, near, far = pl.pallas_call(
+        sweep_kernel,
+        out_shape=(shape(F, RAD, LANES), shape(F, 8, LANES), shape(F, 8, LANES)),
         in_specs=[SMEM, VMEM, VMEM, ANY],
-        out_specs=(VMEM,) * 2,
-        compiler_params=BIG,
-        cost_estimate=cost(2_000_000, 300_000),
+        out_specs=(VMEM,) * 3,
+        compiler_params=BIG,
+        cost_estimate=cost(8_000_000, 500_000),
     )(sweep_jac, amplitude, terms, flux_done)
-    near = lax.ppermute(near, "rad", near_rad)
-    far = lax.ppermute(far, "rad", far_rad)
-    main = pl.pallas_call(
-        sweep_kernel,
-        out_shape=shape(F, RAD, LANES),
-        in_specs=[SMEM, VMEM, VMEM],
-        out_specs=VMEM,
-        compiler_params=BIG,
-        cost_estimate=cost(8_000_000, 500_000),
-    )(sweep_jac, amplitude, terms)
+    near = lax.ppermute(near, ("row", "rad"), across(near_rad))
+    far = lax.ppermute(far, ("row", "rad"), across(far_rad))
+    main = lax.ppermute(main, "row", [(0, 1), (1, 0)])
     response = pl.pallas_call(
         finish_kernel,
         out_shape=shape(CAPACITY * F * 2, RAD),

time: 59 us -> 56.6 us (0.959)
  waiting for transfers between devices: 15.3 us -> 13.7 us
  Pallas kernels: 14.2 us -> 13.2 us
    all_to_all x1, waiting for transfers between devices: 2.9 us -> 1.6 us  [on_device(): amplitude = lax.all_to_all(placed, 'pitch', 0, 0, tiled=True)]
    pallas_call x4 -> x2, Pallas kernels: 5.12 us -> 4.16 us  [the longest x1 2.74 us: on_device(): pl.pallas_call(spectrum_kernel, out_shape=shape(RAD, 8, LANES), in_specs=...]
    ppermute x3 -> x4, waiting for transfers between devices: 3.56 us -> 3.18 us  [the longest x1 3.11 us: on_device(): far = lax.ppermute(far, ('row', 'rad'), across(far_rad))]
    ppermute x3 -> x4, starting transfers between devices: 3.28 us -> 3.32 us  [the longest x1 1.91 us: on_device(): far = lax.ppermute(far, ('row', 'rad'), across(far_rad))]
  transfers between devices with their start and end apart: 9 -> 10, of which waited for: 7 -> 7; matrix products, arithmetic and copies ran while one was open for 0% -> 0% of each run, Pallas kernels for 13% -> 11%
where the time goes in v3:
time: 56.6 us; the launch traced here: 55.9 us
  starting transfers between devices  28.2 us (50%)
  waiting for transfers between devices  13.7 us (24%)
  Pallas kernels  13.2 us (23%)
  between operations  0.77 us (1%)
    all_to_all x1, starting transfers between devices, on_device(): cells = lax.all_to_all(face, 'pitch', 0, 0, tiled=True)  11.6 us
    ppermute x1, starting transfers between devices, on_device(): pitch_far = lax.ppermute(faces[1], 'pitch', far_pitch)  4.26 us
    all_to_all x1, starting transfers between devices, on_device(): amplitude = lax.all_to_all(placed, 'pitch', 0, 0, tiled=True)  3.88 us
    pallas_call x1, Pallas kernels, on_device(): pl.pallas_call(flux_kernel, grid=(AXIAL // DEPTH,), out_shape=(shape(1, F...  3.69 us
    ppermute x1, waiting for transfers between devices, on_device(): far = lax.ppermute(far, ('row', 'rad'), across(far_rad))  3.11 us
    ppermute x1, waiting for transfers between devices, on_device(): rad_far = lax.ppermute(rows[1], 'rad', far_rad)  3.08 us
    pallas_call x1, Pallas kernels, on_device(): pl.pallas_call(spectrum_kernel, out_shape=shape(RAD, 8, LANES), in_specs=...  2.74 us
    ppermute x1, waiting for transfers between devices, on_device(): pitch_far = lax.ppermute(faces[1], 'pitch', far_pitch)  2.68 us
  transfers between devices with their start and end apart: 10, of which 7 were waited for; matrix products, arithmetic and copies ran while one was open for 0% of the time, Pallas kernels for 11%

profile of v3, /device:TPU:4, one launch (start us, length us, event | category | flops | bytes accessed | tf_op | source)
XLA Modules:
  0.0 55.9 jit_solution(8885107729292537990)
XLA Ops:
  0.6 0.0 copy-start
  0.6 2.2 %shard_map.96 = f32[64,8,128]{2,1,0:T(8,128)} custom-call(f32[3,5,1,5]{3,2,1,0:T(1,128)} %bitcast.6, f32[1,5,8,64,128]{4,3,2,1,0:T(8,128)} %flow.5), custom_call_target="tpu_custom_call" | custom-call | flops 4000000 | bytes 600000 | tf_op jit(solution)/shard_map/pallas_call | solution.py:451
  2.9 0.0 copy-start.6
  2.9 0.0 copy-start.3
  2.9 0.0 copy-start.4
  2.9 0.0 copy-start.5
  2.9 11.6 %all-to-all-start = ((f32[64,8,128]{2,1,0:T(8,128)}), f32[64,8,128]{2,1,0:T(8,128)S(1)}, u32[]{:S(2)}, u32[]{:S(2)}) async-start(f32[64,8,128]{2,1,0:T(8,128)} %shard_map.96), calls=%async_computation | async-start | bytes 524288 | tf_op jit(solution)/shard_map/all_to_all | solution.py:464
  14.6 0.7 %shard_map.95 = (f32[64,128]{1,0:T(8,128)S(1)}, f32[64,128]{1,0:T(8,128)S(1)}, f32[5,8,128]{2,1,0:T(8,128)S(1)}, f32[5,8,128]{2,1,0:T(8,128)S(1)}) custom-call(f32[1,5,8,64,128]{4,3,2,1,0:T(8,128)S(1)} %copy-done), custom_call_target="tpu_custom_call" | custom-call | flops 4000000 | bytes 1400000 | tf_op jit(solution)/shard_map/pallas_call | solution.py:466
  15.3 1.9 %collective-permute-start = (f32[64,128]{1,0:T(8,128)S(1)}, f32[64,128]{1,0:T(8,128)S(1)}, u32[]{:S(2)}, u32[]{:S(2)}) collective-permute-start(f32[64,128]{1,0:T(8,128)S(1)} %get-tuple-element.16), channel_id=1, source_target_pairs={{0,4},{4,0},{8,12},{12,8},{16,20},{20,16},{24,28},{28,24},{32,36},... | collective-permute-start | bytes 98312 | tf_op jit(solution)/shard_map/ppermute | solution.py:477
  17.2 0.0 collective-permute-start.2
  17.2 4.3 %collective-permute-start.1 = (f32[64,128]{1,0:T(8,128)S(1)}, f32[64,128]{1,0:T(8,128)S(1)}, u32[]{:S(2)}, u32[]{:S(2)}) collective-permute-start(f32[64,128]{1,0:T(8,128)S(1)} %get-tuple-element.17), channel_id=1, source_target_pairs={{4,8},{8,4},{12,16},{16,12},{20,24},{24,20},{28,32},{32,28},{36,40... | collective-permute-start | bytes 98312 | tf_op jit(solution)/shard_map/ppermute | solution.py:478
  21.5 1.5 %shard_map.97 = (bf16[384,2048]{1,0:T(8,128)(2,1)S(1)}, f32[8,128]{1,0:T(8,128)S(1)}) custom-call(s32[2,1,512]{2,1,0:T(1,128)S(1)} %bitcast.8, s32[2,4,128]{2,1,0:T(4,128)S(1)} %copy-done.4, s32[2,8,384]{2,1,0:T(8,128)S(1)} %copy-done.5), custom_call_target="tpu_custom_call" | custom-call | flops 805306368 | bytes 2000000 | tf_op jit(solution)/shard_map/pallas_call | solution.py:479
  23.0 0.0 collective-permute-done.2.rest_2_.jac
  23.0 2.7 %collective-permute-done.1.rest_1_.pitch_far = f32[64,128]{1,0:T(8,128)S(1)} collective-permute-done((f32[64,128]{1,0:T(8,128)S(1)}, f32[64,128]{1,0:T(8,128)S(1)}, u32[]{:S(2)}, u32[]{:S(2)}) %collective-permute-start.1) | collective-permute-done | bytes 32800 | tf_op jit(solution)/shard_map/ppermute | solution.py:478
  25.7 0.0 collective-permute-done.rest_0_.pitch_near
  25.7 2.5 %all-to-all-done.cells = f32[64,8,128]{2,1,0:T(8,128)S(1)} async-done(((f32[64,8,128]{2,1,0:T(8,128)}), f32[64,8,128]{2,1,0:T(8,128)S(1)}, u32[]{:S(2)}, u32[]{:S(2)}) %all-to-all-start) | async-done | bytes 262176 | tf_op jit(solution)/shard_map/all_to_all | solution.py:464
  28.2 2.7 %shard_map.98.after = f32[64,8,128]{2,1,0:T(8,128)} custom-call(f32[64,8,128]{2,1,0:T(8,128)S(1)} %all-to-all-done.cells, bf16[2,2,9,128,128]{4,3,2,1,0:T(8,128)(2,1)} %constant.5.clone.tables, bf16[384,2048]{1,0:T(8,128)(2,1)S(1)} %get-tuple-element.20.place, f32[64,128]{1,0:T(8,128)S(1)} %collective-permute-done.rest_0_.pitch_near, ...), custom_call_target="tpu_custom_call" | custom-call | flops 200000000 | bytes 3000000 | tf_op jit(solution)/shard_map/pallas_call | solution.py:488
  31.0 3.9 %all-to-all-start.1 = ((f32[64,8,128]{2,1,0:T(8,128)}), f32[64,8,128]{2,1,0:T(8,128)S(1)}, u32[]{:S(2)}, u32[]{:S(2)}) async-start(f32[64,8,128]{2,1,0:T(8,128)} %shard_map.98.after), calls=%async_computation.1 | async-start | bytes 524288 | tf_op jit(solution)/shard_map/all_to_all | solution.py:508
  34.8 1.3 %collective-permute-start.3 = (f32[5,8,128]{2,1,0:T(8,128)S(1)}, f32[5,8,128]{2,1,0:T(8,128)S(1)}, u32[]{:S(2)}, u32[]{:S(2)}) collective-permute-start(f32[5,8,128]{2,1,0:T(8,128)S(1)} %get-tuple-element.22), channel_id=1, source_target_pairs={{0,1},{1,0},{2,3},{3,2},{4,5},{5,4},{6,7},{7,6},{8,9},{9,8},{10,11... | collective-permute-start | bytes 61448 | tf_op jit(solution)/shard_map/ppermute | solution.py:511
  36.1 1.9 %collective-permute-start.4 = (f32[5,8,128]{2,1,0:T(8,128)S(1)}, f32[5,8,128]{2,1,0:T(8,128)S(1)}, u32[]{:S(2)}, u32[]{:S(2)}) collective-permute-start(f32[5,8,128]{2,1,0:T(8,128)S(1)} %get-tuple-element.23), channel_id=1, source_target_pairs={{1,2},{2,1},{5,6},{6,5},{9,10},{10,9},{13,14},{14,13},{17,18},{18,... | collective-permute-start | bytes 61448 | tf_op jit(solution)/shard_map/ppermute | solution.py:512
  38.1 0.7 %collective-permute-done.3.rad_near = f32[5,8,128]{2,1,0:T(8,128)S(1)} collective-permute-done((f32[5,8,128]{2,1,0:T(8,128)S(1)}, f32[5,8,128]{2,1,0:T(8,128)S(1)}, u32[]{:S(2)}, u32[]{:S(2)}) %collective-permute-start.3) | collective-permute-done | bytes 20512 | tf_op jit(solution)/shard_map/ppermute | solution.py:511
  38.7 3.1 %collective-permute-done.4.rad_far = f32[5,8,128]{2,1,0:T(8,128)S(1)} collective-permute-done((f32[5,8,128]{2,1,0:T(8,128)S(1)}, f32[5,8,128]{2,1,0:T(8,128)S(1)}, u32[]{:S(2)}, u32[]{:S(2)}) %collective-permute-start.4) | collective-permute-done | bytes 20512 | tf_op jit(solution)/shard_map/ppermute | solution.py:512
  41.8 3.7 %shard_map.99 = (f32[1,5,8,64,128]{4,3,2,1,0:T(8,128)}, f32[8,128]{1,0:T(8,128)S(1)}) custom-call(f32[3,5,1,5]{3,2,1,0:T(1,128)S(1)} %bitcast.7, f32[1,5,8,64,128]{4,3,2,1,0:T(8,128)S(1)} %copy-done, f32[1,5,64,128]{3,2,1,0:T(8,128)S(1)} %copy-done.1, f32[64,128]{1,0:T(8,128)S(1)} %collective-permute-done.rest_0_.pitch_near, ...), custom_call_target="tpu_custom_call" | custom-call | flops 20000000 | bytes 3000000 | tf_op jit(solution)/shard_map/pallas_call | solution.py:513
  45.5 1.6 %all-to-all-done.1.modes = f32[64,8,128]{2,1,0:T(8,128)S(1)} async-done(((f32[64,8,128]{2,1,0:T(8,128)}), f32[64,8,128]{2,1,0:T(8,128)S(1)}, u32[]{:S(2)}, u32[]{:S(2)}) %all-to-all-start.1) | async-done | bytes 262176 | tf_op jit(solution)/shard_map/all_to_all | solution.py:508
  47.1 1.4 %shard_map.100 = (f32[5,64,128]{2,1,0:T(8,128)S(1)}, f32[5,8,128]{2,1,0:T(8,128)S(1)}, f32[5,8,128]{2,1,0:T(8,128)S(1)}) custom-call(f32[1,5,2,5]{3,2,1,0:T(2,128)S(1)} %collective-permute-done.2.rest_2_.jac, f32[64,8,128]{2,1,0:T(8,128)S(1)} %all-to-all-done.1.modes, f32[8,128]{1,0:T(8,128)S(1)} %get-tuple-element.25.terms, ...), custom_call_target="tpu_custom_call" | custom-call | flops 8000000 | bytes 500000 | tf_op jit(solution)/shard_map/pallas_call | solution.py:536
  48.5 0.1 collective-permute-start.5
  48.6 1.3 %collective-permute-start.6 = (f32[5,8,128]{2,1,0:T(8,128)S(1)}, f32[5,8,128]{2,1,0:T(8,128)S(1)}, u32[]{:S(2)}, u32[]{:S(2)}) collective-permute-start(f32[5,8,128]{2,1,0:T(8,128)S(1)} %get-tuple-element.28), channel_id=1, source_target_pairs={{0,129},{1,128},{2,131},{3,130},{128,1},{129,0},{130,3},{131,2},{4... | collective-permute-start | bytes 61448 | tf_op jit(solution)/shard_map/ppermute | solution.py:544
  49.9 1.9 %collective-permute-start.7 = (f32[5,8,128]{2,1,0:T(8,128)S(1)}, f32[5,8,128]{2,1,0:T(8,128)S(1)}, u32[]{:S(2)}, u32[]{:S(2)}) collective-permute-start(f32[5,8,128]{2,1,0:T(8,128)S(1)} %get-tuple-element.29), channel_id=1, source_target_pairs={{1,130},{2,129},{129,2},{130,1},{5,134},{6,133},{133,6},{134,5},{9... | collective-permute-start | bytes 61448 | tf_op jit(solution)/shard_map/ppermute | solution.py:545
  51.9 0.1 collective-permute-done.6.near
  51.9 3.1 %collective-permute-done.7.far = f32[5,8,128]{2,1,0:T(8,128)S(1)} collective-permute-done((f32[5,8,128]{2,1,0:T(8,128)S(1)}, f32[5,8,128]{2,1,0:T(8,128)S(1)}, u32[]{:S(2)}, u32[]{:S(2)}) %collective-permute-start.7) | collective-permute-done | bytes 20512 | tf_op jit(solution)/shard_map/ppermute | solution.py:545
  55.0 0.0 collective-permute-done.5.main
  55.0 0.9 %shard_map.101 = f32[480,64]{1,0:T(8,128)} custom-call(f32[5,64,128]{2,1,0:T(8,128)S(1)} %collective-permute-done.5.main, f32[5,8,128]{2,1,0:T(8,128)S(1)} %collective-permute-done.6.near, f32[5,8,128]{2,1,0:T(8,128)S(1)} %collective-permute-done.7.far), custom_call_target="tpu_custom_call" | custom-call | flops 1000000 | bytes 800000 | tf_op jit(solution)/shard_map/pallas_call | solution.py:547
  (9 shorter events, 0.0 us)
Async XLA Ops:
  0.6 13.9 %copy-start = (f32[1,5,8,64,128]{4,3,2,1,0:T(8,128)S(1)}, f32[1,5,8,64,128]{4,3,2,1,0:T(8,128)}, u32[]{:S(2)}) copy-start(f32[1,5,8,64,128]{4,3,2,1,0:T(8,128)} %flow.5) | copy-start | bytes 3932164
  2.9 14.3 %copy-start.6 = (f32[1,2,5,5]{3,1,2,0:T(2,128)S(1)}, f32[1,2,5,5]{3,1,2,0:T(2,128)}, u32[]{:S(2)}) copy-start(f32[1,2,5,5]{3,1,2,0:T(2,128)} %param.11) | copy-start | bytes 604
  2.9 18.6 %copy-start.3 = (s32[2,512,1]{1,2,0:T(1,128)S(1)}, s32[2,512,1]{1,2,0:T(1,128)}, u32[]{:S(2)}) copy-start(s32[2,512,1]{1,2,0:T(1,128)} %param.13) | copy-start | bytes 12292
  2.9 18.6 %copy-start.4 = (s32[2,4,128]{2,1,0:T(4,128)S(1)}, s32[2,4,128]{2,1,0:T(4,128)}, u32[]{:S(2)}) copy-start(s32[2,4,128]{2,1,0:T(4,128)} %modes.1) | copy-start | bytes 12292
  2.9 18.6 %copy-start.5 = (s32[2,8,384]{2,1,0:T(8,128)S(1)}, s32[2,8,384]{2,1,0:T(8,128)}, u32[]{:S(2)}) copy-start(s32[2,8,384]{2,1,0:T(8,128)} %constant.4.clone.codes) | copy-start | bytes 73732
  2.9 25.3 %all-to-all-start = ((f32[64,8,128]{2,1,0:T(8,128)}), f32[64,8,128]{2,1,0:T(8,128)S(1)}, u32[]{:S(2)}, u32[]{:S(2)}) async-start(f32[64,8,128]{2,1,0:T(8,128)} %shard_map.96), calls=%async_computation | async-start | bytes 524288 | tf_op jit(solution)/shard_map/all_to_all | solution.py:464
  15.3 10.4 %collective-permute-start = (f32[64,128]{1,0:T(8,128)S(1)}, f32[64,128]{1,0:T(8,128)S(1)}, u32[]{:S(2)}, u32[]{:S(2)}) collective-permute-start(f32[64,128]{1,0:T(8,128)S(1)} %get-tuple-element.16), channel_id=1, source_target_pairs={{0,4},{4,0},{8,12},{12,8},{16,20},{20,16},{24,28},{28,24},{32,36},... | collective-permute-start | bytes 98312 | tf_op jit(solution)/shard_map/ppermute | solution.py:477
  17.2 5.8 %collective-permute-start.2 = (f32[1,5,2,5]{3,2,1,0:T(2,128)S(1)}, f32[1,5,2,5]{3,2,1,0:T(2,128)S(1)}, u32[]{:S(2)}, u32[]{:S(2)}) collective-permute-start(f32[1,5,2,5]{3,2,1,0:T(2,128)S(1)} %bitcast.10), channel_id=1, source_target_pairs={{0,128},{128,0},{1,129},{129,1},{2,130},{130,2},{3,131},{131,3},{4... | collective-permute-start | bytes 608 | tf_op jit(solution)/shard_map/ppermute | solution.py:476
  17.2 8.5 %collective-permute-start.1 = (f32[64,128]{1,0:T(8,128)S(1)}, f32[64,128]{1,0:T(8,128)S(1)}, u32[]{:S(2)}, u32[]{:S(2)}) collective-permute-start(f32[64,128]{1,0:T(8,128)S(1)} %get-tuple-element.17), channel_id=1, source_target_pairs={{4,8},{8,4},{12,16},{16,12},{20,24},{24,20},{28,32},{32,28},{36,40... | collective-permute-start | bytes 98312 | tf_op jit(solution)/shard_map/ppermute | solution.py:478
  28.2 13.6 %copy-start.1 = (f32[1,5,64,128]{3,2,1,0:T(8,128)S(1)}, f32[1,5,64,128]{3,2,1,0:T(8,128)}, u32[]{:S(2)}) copy-start(f32[1,5,64,128]{3,2,1,0:T(8,128)} %inflow.1) | copy-start | bytes 491524
  28.2 13.6 %copy-start.2 = (f32[1,3,5,5]{3,0,2,1:T(1,128)S(1)}, f32[1,3,5,5]{3,0,2,1:T(1,128)}, u32[]{:S(2)}) copy-start(f32[1,3,5,5]{3,0,2,1:T(1,128)} %param.10) | copy-start | bytes 904
  31.0 16.1 %all-to-all-start.1 = ((f32[64,8,128]{2,1,0:T(8,128)}), f32[64,8,128]{2,1,0:T(8,128)S(1)}, u32[]{:S(2)}, u32[]{:S(2)}) async-start(f32[64,8,128]{2,1,0:T(8,128)} %shard_map.98.after), calls=%async_computation.1 | async-start | bytes 524288 | tf_op jit(solution)/shard_map/all_to_all | solution.py:508
  34.8 3.9 %collective-permute-start.3 = (f32[5,8,128]{2,1,0:T(8,128)S(1)}, f32[5,8,128]{2,1,0:T(8,128)S(1)}, u32[]{:S(2)}, u32[]{:S(2)}) collective-permute-start(f32[5,8,128]{2,1,0:T(8,128)S(1)} %get-tuple-element.22), channel_id=1, source_target_pairs={{0,1},{1,0},{2,3},{3,2},{4,5},{5,4},{6,7},{7,6},{8,9},{9,8},{10,11... | collective-permute-start | bytes 61448 | tf_op jit(solution)/shard_map/ppermute | solution.py:511
  36.1 5.7 %collective-permute-start.4 = (f32[5,8,128]{2,1,0:T(8,128)S(1)}, f32[5,8,128]{2,1,0:T(8,128)S(1)}, u32[]{:S(2)}, u32[]{:S(2)}) collective-permute-start(f32[5,8,128]{2,1,0:T(8,128)S(1)} %get-tuple-element.23), channel_id=1, source_target_pairs={{1,2},{2,1},{5,6},{6,5},{9,10},{10,9},{13,14},{14,13},{17,18},{18,... | collective-permute-start | bytes 61448 | tf_op jit(solution)/shard_map/ppermute | solution.py:512
  48.5 6.5 %collective-permute-start.5 = (f32[5,64,128]{2,1,0:T(8,128)S(1)}, f32[5,64,128]{2,1,0:T(8,128)S(1)}, u32[]{:S(2)}, u32[]{:S(2)}) collective-permute-start(f32[5,64,128]{2,1,0:T(8,128)S(1)} %get-tuple-element.27), channel_id=1, source_target_pairs={{0,128},{128,0},{1,129},{129,1},{2,130},{130,2},{3,131},{131,3},{4... | collective-permute-start | bytes 491528 | tf_op jit(solution)/shard_map/ppermute | solution.py:546
  48.6 3.3 %collective-permute-start.6 = (f32[5,8,128]{2,1,0:T(8,128)S(1)}, f32[5,8,128]{2,1,0:T(8,128)S(1)}, u32[]{:S(2)}, u32[]{:S(2)}) collective-permute-start(f32[5,8,128]{2,1,0:T(8,128)S(1)} %get-tuple-element.28), channel_id=1, source_target_pairs={{0,129},{1,128},{2,131},{3,130},{128,1},{129,0},{130,3},{131,2},{4... | collective-permute-start | bytes 61448 | tf_op jit(solution)/shard_map/ppermute | solution.py:544
  49.9 5.1 %collective-permute-start.7 = (f32[5,8,128]{2,1,0:T(8,128)S(1)}, f32[5,8,128]{2,1,0:T(8,128)S(1)}, u32[]{:S(2)}, u32[]{:S(2)}) collective-permute-start(f32[5,8,128]{2,1,0:T(8,128)S(1)} %get-tuple-element.29), channel_id=1, source_target_pairs={{1,130},{2,129},{129,2},{130,1},{5,134},{6,133},{133,6},{134,5},{9... | collective-permute-start | bytes 61448 | tf_op jit(solution)/shard_map/ppermute | solution.py:545

commit v4 on v3

--- a/solution.py
+++ b/solution.py
@@ -27,6 +27,8 @@
 TABLE = GROUPS * LANES
 SLOT_LANES = 64
 PACKED = N_PITCH * SLOT_LANES
+ROWS_EACH = 12
+SENT = N_PITCH * ROWS_EACH
 
 FLUX_PITCH = 0.25
 FLUX_RAD = 0.25
@@ -89,7 +91,7 @@
     return [jac[0, g, k, f] for f in range(F)]
 
 
-def exit_kernel(jacobian, flow, out, planes, jac, arrived):
+def exit_kernel(jacobian, flow, out, planes, jac, fields, edges, arrived):
     copies = [
         pltpu.make_async_copy(flow.at[0, f, pl.ds(AXIAL - 2, 2)], planes.at[f], arrived.at[f])
         for f in range(F)
@@ -104,8 +106,8 @@
     lane = iota((RAD, LANES), 1)
     row = iota((RAD, LANES), 0)
     change = [now[f] - behind[f] for f in range(F)]
-    edges = jnp.zeros((RAD, LANES), f32)
-    out[...] = jnp.zeros(out.shape, f32)
+    edge = jnp.zeros((RAD, LANES), f32)
+    out[pl.ds(11, N_PITCH, ROWS_EACH), :] = jnp.zeros((N_PITCH, LANES), f32)
     for g in range(F):
         pitch = mix([FLUX_PITCH * c for c in flux_row(jac, 0, g)], now)
         radial = mix([FLUX_RAD * c for c in flux_row(jac, 1, g)], now)
@@ -117,12 +119,21 @@
         value = value + jnp.where(lane == 0, 0.0, pltpu.roll(to_high, 1, 1))
         value = value + jnp.where(row == RAD - 1, 0.0, pltpu.roll(inward, RAD - 1, 0))
         value = value + jnp.where(row == 0, 0.0, pltpu.roll(outward, 1, 0))
-        out[:, g, :] = value
-        edges = jnp.where(lane == g, pltpu.roll(to_low, g, 1) if g else to_low, edges)
-        edges = jnp.where(lane == 8 + g, pltpu.roll(to_high, 9 + g, 1), edges)
-        out[g, 6:7, :] = inward[0:1]
-        out[F + g, 6:7, :] = outward[RAD - 1 : RAD]
-    out[:, 5, :] = edges
+        fields[g] = value
+        edge = jnp.where(lane == g, pltpu.roll(to_low, g, 1) if g else to_low, edge)
+        edge = jnp.where(lane == 8 + g, pltpu.roll(to_high, 9 + g, 1), edge)
+        for side in range(2):
+            out[pl.ds(side * F + g, N_PITCH, ROWS_EACH), :] = fields[g, pl.ds(side, N_PITCH, 2), :]
+        out[ROWS_EACH * g + 11 : ROWS_EACH * g + 12, :] = inward[0:1]
+        out[ROWS_EACH * (F + g) + 11 : ROWS_EACH * (F + g) + 12, :] = outward[RAD - 1 : RAD]
+    edges[...] = edge
+    even, odd = edges[pl.ds(0, N_PITCH, 2), :], edges[pl.ds(1, N_PITCH, 2), :]
+    lane = iota((N_PITCH, LANES), 1)
+    both = jnp.where(lane < F, even, 0.0)
+    both = jnp.where((lane >= F) & (lane < 2 * F), pltpu.roll(odd, F, 1), both)
+    both = jnp.where((lane >= 16) & (lane < 16 + F), pltpu.roll(even, 8, 1), both)
+    both = jnp.where((lane >= 16 + F) & (lane < 16 + 2 * F), pltpu.roll(odd, 8 + F, 1), both)
+    out[pl.ds(10, N_PITCH, ROWS_EACH), :] = both
 
 
 def halo_kernel(flow, pitch_near, pitch_far, rad_near, rad_far):
@@ -269,7 +280,8 @@
     sub = iota((8, LANES), 0)
     parts = []
     for half in range(2):
-        x = [cells[2 * p + half] for p in range(N_PITCH)]
+        first = [ROWS_EACH * p + 4 * half for p in range(N_PITCH)]
+        x = [cells[at : at + 8] for at in first]
         z = [x[p] + x[p + 16] for p in range(16)]
         even = [None] + [z[p] + z[16 - p] for p in range(1, 8)]
         odd = [None] + [z[p] - z[16 - p] for p in range(1, 8)]
@@ -281,20 +293,31 @@
                 re = re + math.cos(2.0 * math.pi * ((t * p) % 16) / 16) * even[p]
                 if t % 8:
                     im = im - math.sin(2.0 * math.pi * ((t * p) % 16) / 16) * odd[p]
-
-            def edge(value, offset):
-                spread = jnp.broadcast_to(value[5:6, :], (8, LANES))
-                return jnp.sum(jnp.where(lane == sub + offset, spread, 0.0), axis=1, keepdims=True)
-
+            columns.append((re, im))
+        parts.append(columns)
+
+    def edge(value, half, offset):
+        spread = jnp.broadcast_to(value[6:7, :], (8, LANES))
+        own = lane == sub + (offset + 4 * half)
+        return jnp.sum(jnp.where(own, spread, 0.0), axis=1, keepdims=True)
+
+    closed = []
+    for half in range(2):
+        columns = []
+        for t in range(9):
+            re, im = parts[half][t]
+            edge_re, edge_im = parts[1][t]
             cos, sin = math.cos(2.0 * math.pi * t / 16), math.sin(2.0 * math.pi * t / 16)
-            low_re, high_re = edge(re, 0), edge(re, 8)
-            low_im, high_im = (edge(im, 0), edge(im, 8)) if t % 8 else (0.0, 0.0)
+            low_re, high_re = edge(edge_re, half, 0), edge(edge_re, half, 16)
+            low_im, high_im = 0.0, 0.0
+            if t % 8:
+                low_im, high_im = edge(edge_im, half, 0), edge(edge_im, half, 16)
             re = re + jnp.where(lane == LANES - 1, cos * low_re - sin * low_im, 0.0)
             re = re + jnp.where(lane == 0, cos * high_re + sin * high_im, 0.0)
             im = im + jnp.where(lane == LANES - 1, cos * low_im + sin * low_re, 0.0)
             im = im + jnp.where(lane == 0, cos * high_im - sin * high_re, 0.0)
             columns += [re, im]
-        parts.append(columns)
+        closed.append(columns)
     for fetch in fetches:
         fetch.wait()
     wide = iota((16, LANES), 1)
@@ -306,7 +329,7 @@
         for member in range(3):
             t = group * 3 + member
             left = jnp.concatenate(
-                [parts[0][2 * t], parts[1][2 * t], parts[0][2 * t + 1], parts[1][2 * t + 1]], axis=0
+                [closed[0][2 * t], closed[1][2 * t], closed[0][2 * t + 1], closed[1][2 * t + 1]], axis=0
             )
             high = left.astype(bf16)
             low = (left - high.astype(f32)).astype(bf16)
@@ -338,11 +361,13 @@
         picked = picked[0:32] + picked[32:64]
         for pair in range(2):
             here = picked[:, pair * LANES : (pair + 1) * LANES]
-            at = 8 * block + 4 * pair
+            at = ROWS_EACH * (4 * block + 2 * pair)
             for half in range(2):
                 re, im = here[half * 8 : half * 8 + 8], here[16 + half * 8 : 24 + half * 8]
-                out[at + half] = jnp.where(lane < SLOT_LANES, re, pltpu.roll(im, SLOT_LANES, 1))
-                out[at + 2 + half] = jnp.where(lane < SLOT_LANES, pltpu.roll(re, SLOT_LANES, 1), im)
+                spot = at + 4 * half
+                out[spot : spot + 8] = jnp.where(lane < SLOT_LANES, re, pltpu.roll(im, SLOT_LANES, 1))
+                spot = spot + ROWS_EACH
+                out[spot : spot + 8] = jnp.where(lane < SLOT_LANES, pltpu.roll(re, SLOT_LANES, 1), im)
 
 
 SPAN = RAD + 8
@@ -381,18 +406,21 @@
 
 def beyond(modes, f):
     index = iota((8, LANES), 0)
-    before = jnp.where(index == 7, modes[f, 6:7, :], 0.0)
-    after = jnp.where(index == 0, modes[F + f, 6:7, :], 0.0)
+    at = [ROWS_EACH * d + 11 for d in (f, F + f)]
+    before = jnp.where(index == 7, modes[at[0] : at[0] + 1], 0.0)
+    after = jnp.where(index == 0, modes[at[1] : at[1] + 1], 0.0)
     return before, after
 
 
-def sweep_kernel(jac, modes, terms, after, main, near, far):
+def sweep_kernel(jac, modes, terms, after, main, near, far, body):
     inside = domain(iota((RAD + 16, LANES), 0) - 8)
     rad_even = lax.rem(lax.axis_index("rad"), 2) == 0
     start = []
     for f in range(F):
         low, high = beyond(modes, f)
-        start.append(jnp.concatenate([low, modes[:, f, :], high], axis=0))
+        for side in range(2):
+            body[f, pl.ds(side, N_PITCH, 2), :] = modes[pl.ds(side * F + f, N_PITCH, ROWS_EACH), :]
+        start.append(jnp.concatenate([low, body[f], high], axis=0))
     for f, w in enumerate(swept(start, inside, jac, terms)):
         main[f] = w[8 : 8 + RAD]
         near[f] = jnp.where(rad_even, w[8 + RAD :], w[:8])
@@ -436,6 +464,11 @@
     return pairs
 
 
+def transposed(value):
+    value = value.reshape(SENT // 4, 4, LANES)
+    return lax.all_to_all(value, "pitch", 0, 0, tiled=True).reshape(SENT, LANES)
+
+
 def across(pairs):
     return [(row * N_RAD + i, (1 - row) * N_RAD + j) for row in range(2) for i, j in pairs]
 
@@ -450,18 +483,20 @@
 
     face = pl.pallas_call(
         exit_kernel,
-        out_shape=shape(RAD, 8, LANES),
+        out_shape=shape(SENT, LANES),
         in_specs=[ANY, ANY],
         out_specs=VMEM,
         scratch_shapes=[
             pltpu.VMEM((F, 2, RAD, LANES), f32),
             pltpu.SMEM((3, F, 1, F), f32),
+            pltpu.VMEM((F, RAD, LANES), f32),
+            pltpu.VMEM((RAD, LANES), f32),
             pltpu.SemaphoreType.DMA((F + 1,)),
         ],
         compiler_params=BIG,
         cost_estimate=cost(4_000_000, 600_000),
     )(pltpu.with_memory_space_constraint(flux_jac, pltpu.HBM), pinned)
-    cells = lax.all_to_all(face, "pitch", 0, 0, tiled=True)
+    cells = transposed(face)
 
     faces = pl.pallas_call(
         halo_kernel,
@@ -487,7 +522,7 @@
 
     placed = pl.pallas_call(
         spectrum_kernel,
-        out_shape=shape(RAD, 8, LANES),
+        out_shape=shape(SENT, LANES),
         in_specs=[VMEM, ANY, VMEM, ANY, ANY, ANY],
         out_specs=VMEM,
         scratch_shapes=[
@@ -505,7 +540,7 @@
         pitch_far,
         sweep_jac,
     )
-    amplitude = lax.all_to_all(placed, "pitch", 0, 0, tiled=True)
+    amplitude = transposed(placed)
 
     rows = lax.optimization_barrier((faces[2], faces[3], placed))[:2]
     rad_near = lax.ppermute(rows[0], "rad", near_rad)
@@ -538,6 +573,7 @@
         out_shape=(shape(F, RAD, LANES), shape(F, 8, LANES), shape(F, 8, LANES)),
         in_specs=[SMEM, VMEM, VMEM, ANY],
         out_specs=(VMEM,) * 3,
+        scratch_shapes=[pltpu.VMEM((F, RAD, LANES), f32)],
         compiler_params=BIG,
         cost_estimate=cost(8_000_000, 500_000),
     )(sweep_jac, amplitude, terms, flux_done)

time: 56.6 us -> 55.1 us (0.973)
  waiting for transfers between devices: 13.7 us -> 10.9 us
  starting transfers between devices: 28.2 us -> 29.7 us
    all_to_all x2, waiting for transfers between devices: 4.09 us -> 2.01 us  [transposed(): return lax.all_to_all(value, 'pitch', 0, 0, tiled=True).reshape(SENT, LANES)]
    all_to_all x2, starting transfers between devices: 15.5 us -> 17.1 us  [transposed(): return lax.all_to_all(value, 'pitch', 0, 0, tiled=True).reshape(SENT, LANES)]
    ppermute x1, waiting for transfers between devices: 2.68 us -> 1.98 us  [on_device(): pitch_far = lax.ppermute(faces[1], 'pitch', far_pitch)]
where the time goes in v4:
time: 55.1 us; the launch traced here: 54.5 us
  starting transfers between devices  29.7 us (54%)
  Pallas kernels  13.1 us (24%)
  waiting for transfers between devices  10.9 us (20%)
  between operations  0.77 us (1%)
    all_to_all x2, starting transfers between devices, transposed(): return lax.all_to_all(value, 'pitch', 0, 0, tiled=True).reshape(SENT, LANES)  17.1 us
    ppermute x1, starting transfers between devices, on_device(): pitch_far = lax.ppermute(faces[1], 'pitch', far_pitch)  4.26 us
    pallas_call x1, Pallas kernels, on_device(): pl.pallas_call(flux_kernel, grid=(AXIAL // DEPTH,), out_shape=(shape(1, F...  3.69 us
    ppermute x1, waiting for transfers between devices, on_device(): far = lax.ppermute(far, ('row', 'rad'), across(far_rad))  3.11 us
    ppermute x1, waiting for transfers between devices, on_device(): rad_far = lax.ppermute(rows[1], 'rad', far_rad)  3.07 us
    pallas_call x1, Pallas kernels, on_device(): pl.pallas_call(spectrum_kernel, out_shape=shape(SENT, LANES), in_specs=[V...  2.72 us
    pallas_call x1, Pallas kernels, on_device(): pl.pallas_call(exit_kernel, out_shape=shape(SENT, LANES), in_specs=[ANY,...  2.14 us
    all_to_all x2, waiting for transfers between devices, transposed(): return lax.all_to_all(value, 'pitch', 0, 0, tiled=True).reshape(SENT, LANES)  2.01 us
  transfers between devices with their start and end apart: 10, of which 7 were waited for; matrix products, arithmetic and copies ran while one was open for 0% of the time, Pallas kernels for 11%

profile of v4, /device:TPU:4, one launch (start us, length us, event | category | flops | bytes accessed | tf_op | source)
XLA Modules:
  0.0 54.5 jit_solution(5307605989046842377)
XLA Ops:
  0.6 0.0 copy-start
  0.6 0.0 copy-start.6
  0.7 0.0 copy-start.5
  0.7 2.1 %shard_map.96 = f32[384,128]{1,0:T(8,128)} custom-call(f32[3,5,1,5]{3,2,1,0:T(1,128)} %bitcast.12, f32[1,5,8,64,128]{4,3,2,1,0:T(8,128)} %flow.5), custom_call_target="tpu_custom_call" | custom-call | flops 4000000 | bytes 600000 | tf_op jit(solution)/shard_map/pallas_call | solution.py:484
  2.8 11.5 %all-to-all-start = ((f32[96,4,128]{2,1,0:T(4,128)}), f32[96,4,128]{2,1,0:T(4,128)S(1)}, u32[]{:S(2)}, u32[]{:S(2)}) async-start(f32[96,4,128]{2,1,0:T(4,128)} %bitcast.1), calls=%async_computation | async-start | bytes 393216 | tf_op jit(solution)/shard_map/all_to_all | solution.py:469
  14.3 0.0 copy-done
  14.3 0.7 %shard_map.95 = (f32[64,128]{1,0:T(8,128)S(1)}, f32[64,128]{1,0:T(8,128)S(1)}, f32[5,8,128]{2,1,0:T(8,128)S(1)}, f32[5,8,128]{2,1,0:T(8,128)S(1)}) custom-call(f32[1,5,8,64,128]{4,3,2,1,0:T(8,128)S(1)} %copy-done), custom_call_target="tpu_custom_call" | custom-call | flops 4000000 | bytes 1400000 | tf_op jit(solution)/shard_map/pallas_call | solution.py:501
  15.1 1.9 %collective-permute-start = (f32[64,128]{1,0:T(8,128)S(1)}, f32[64,128]{1,0:T(8,128)S(1)}, u32[]{:S(2)}, u32[]{:S(2)}) collective-permute-start(f32[64,128]{1,0:T(8,128)S(1)} %get-tuple-element.16), channel_id=1, source_target_pairs={{0,4},{4,0},{8,12},{12,8},{16,20},{20,16},{24,28},{28,24},{32,36},... | collective-permute-start | bytes 98312 | tf_op jit(solution)/shard_map/ppermute | solution.py:512
  17.0 0.0 collective-permute-start.2
  17.0 4.3 %collective-permute-start.1 = (f32[64,128]{1,0:T(8,128)S(1)}, f32[64,128]{1,0:T(8,128)S(1)}, u32[]{:S(2)}, u32[]{:S(2)}) collective-permute-start(f32[64,128]{1,0:T(8,128)S(1)} %get-tuple-element.17), channel_id=1, source_target_pairs={{4,8},{8,4},{12,16},{16,12},{20,24},{24,20},{28,32},{32,28},{36,40... | collective-permute-start | bytes 98312 | tf_op jit(solution)/shard_map/ppermute | solution.py:513
  21.3 0.0 copy-done.4
  21.3 1.5 %shard_map.97 = (bf16[384,2048]{1,0:T(8,128)(2,1)S(1)}, f32[8,128]{1,0:T(8,128)S(1)}) custom-call(s32[2,1,512]{2,1,0:T(1,128)S(1)} %bitcast.14, s32[2,4,128]{2,1,0:T(4,128)S(1)} %copy-done.4, s32[2,8,384]{2,1,0:T(8,128)S(1)} %copy-done.5), custom_call_target="tpu_custom_call" | custom-call | flops 805306368 | bytes 2000000 | tf_op jit(solution)/shard_map/pallas_call | solution.py:514
  22.8 0.0 collective-permute-done.2.rest_2_.jac
  22.8 2.0 %collective-permute-done.1.rest_1_.pitch_far = f32[64,128]{1,0:T(8,128)S(1)} collective-permute-done((f32[64,128]{1,0:T(8,128)S(1)}, f32[64,128]{1,0:T(8,128)S(1)}, u32[]{:S(2)}, u32[]{:S(2)}) %collective-permute-start.1) | collective-permute-done | bytes 32800 | tf_op jit(solution)/shard_map/ppermute | solution.py:513
  24.8 0.0 collective-permute-done.rest_0_.pitch_near
  24.8 1.2 %all-to-all-done = f32[96,4,128]{2,1,0:T(4,128)S(1)} async-done(((f32[96,4,128]{2,1,0:T(4,128)}), f32[96,4,128]{2,1,0:T(4,128)S(1)}, u32[]{:S(2)}, u32[]{:S(2)}) %all-to-all-start) | async-done | bytes 196640 | tf_op jit(solution)/shard_map/all_to_all | solution.py:469
  26.0 2.7 %shard_map.98.after = f32[384,128]{1,0:T(8,128)} custom-call(f32[384,128]{1,0:T(8,128)S(1)} %bitcast.10, bf16[2,2,9,128,128]{4,3,2,1,0:T(8,128)(2,1)} %constant.5.clone.tables, bf16[384,2048]{1,0:T(8,128)(2,1)S(1)} %get-tuple-element.20.place, f32[64,128]{1,0:T(8,128)S(1)} %collective-permute-done.rest_0_.pitch_near, ...), custom_call_target="tpu_custom_call" | custom-call | flops 200000000 | bytes 3000000 | tf_op jit(solution)/shard_map/pallas_call | solution.py:523
  28.8 5.6 %all-to-all-start.1 = ((f32[96,4,128]{2,1,0:T(4,128)}), f32[96,4,128]{2,1,0:T(4,128)S(1)}, u32[]{:S(2)}, u32[]{:S(2)}) async-start(f32[96,4,128]{2,1,0:T(4,128)} %bitcast.5), calls=%async_computation.1 | async-start | bytes 393216 | tf_op jit(solution)/shard_map/all_to_all | solution.py:469
  34.3 1.3 %collective-permute-start.3 = (f32[5,8,128]{2,1,0:T(8,128)S(1)}, f32[5,8,128]{2,1,0:T(8,128)S(1)}, u32[]{:S(2)}, u32[]{:S(2)}) collective-permute-start(f32[5,8,128]{2,1,0:T(8,128)S(1)} %get-tuple-element.22), channel_id=1, source_target_pairs={{0,1},{1,0},{2,3},{3,2},{4,5},{5,4},{6,7},{7,6},{8,9},{9,8},{10,11... | collective-permute-start | bytes 61448 | tf_op jit(solution)/shard_map/ppermute | solution.py:546
  35.6 1.9 %collective-permute-start.4 = (f32[5,8,128]{2,1,0:T(8,128)S(1)}, f32[5,8,128]{2,1,0:T(8,128)S(1)}, u32[]{:S(2)}, u32[]{:S(2)}) collective-permute-start(f32[5,8,128]{2,1,0:T(8,128)S(1)} %get-tuple-element.23), channel_id=1, source_target_pairs={{1,2},{2,1},{5,6},{6,5},{9,10},{10,9},{13,14},{14,13},{17,18},{18,... | collective-permute-start | bytes 61448 | tf_op jit(solution)/shard_map/ppermute | solution.py:547
  37.5 0.7 %collective-permute-done.3.rad_near = f32[5,8,128]{2,1,0:T(8,128)S(1)} collective-permute-done((f32[5,8,128]{2,1,0:T(8,128)S(1)}, f32[5,8,128]{2,1,0:T(8,128)S(1)}, u32[]{:S(2)}, u32[]{:S(2)}) %collective-permute-start.3) | collective-permute-done | bytes 20512 | tf_op jit(solution)/shard_map/ppermute | solution.py:546
  38.2 3.1 %collective-permute-done.4.rad_far = f32[5,8,128]{2,1,0:T(8,128)S(1)} collective-permute-done((f32[5,8,128]{2,1,0:T(8,128)S(1)}, f32[5,8,128]{2,1,0:T(8,128)S(1)}, u32[]{:S(2)}, u32[]{:S(2)}) %collective-permute-start.4) | collective-permute-done | bytes 20512 | tf_op jit(solution)/shard_map/ppermute | solution.py:547
  41.3 3.7 %shard_map.99 = (f32[1,5,8,64,128]{4,3,2,1,0:T(8,128)}, f32[8,128]{1,0:T(8,128)S(1)}) custom-call(f32[3,5,1,5]{3,2,1,0:T(1,128)S(1)} %bitcast.13, f32[1,5,8,64,128]{4,3,2,1,0:T(8,128)S(1)} %copy-done, f32[1,5,64,128]{3,2,1,0:T(8,128)S(1)} %copy-done.1, f32[64,128]{1,0:T(8,128)S(1)} %collective-permute-done.rest_0_.pitch_near, ...), custom_call_target="tpu_custom_call" | custom-call | flops 20000000 | bytes 3000000 | tf_op jit(solution)/shard_map/pallas_call | solution.py:548
  45.0 0.8 %all-to-all-done.1 = f32[96,4,128]{2,1,0:T(4,128)S(1)} async-done(((f32[96,4,128]{2,1,0:T(4,128)}), f32[96,4,128]{2,1,0:T(4,128)S(1)}, u32[]{:S(2)}, u32[]{:S(2)}) %all-to-all-start.1) | async-done | bytes 196640 | tf_op jit(solution)/shard_map/all_to_all | solution.py:469
  45.8 1.4 %shard_map.100 = (f32[5,64,128]{2,1,0:T(8,128)S(1)}, f32[5,8,128]{2,1,0:T(8,128)S(1)}, f32[5,8,128]{2,1,0:T(8,128)S(1)}) custom-call(f32[1,5,2,5]{3,2,1,0:T(2,128)S(1)} %collective-permute-done.2.rest_2_.jac, f32[384,128]{1,0:T(8,128)S(1)} %bitcast.11, f32[8,128]{1,0:T(8,128)S(1)} %get-tuple-element.25.terms, f32[8,128]{1,0:T(8,128)S(1)} %get-tuple-element.26.after), custom_call_target="tpu_custom_call" | custom-call | flops 8000000 | bytes 500000 | tf_op jit(solution)/shard_map/pallas_call | solution.py:571
  47.1 0.1 collective-permute-start.5
  47.2 1.3 %collective-permute-start.6 = (f32[5,8,128]{2,1,0:T(8,128)S(1)}, f32[5,8,128]{2,1,0:T(8,128)S(1)}, u32[]{:S(2)}, u32[]{:S(2)}) collective-permute-start(f32[5,8,128]{2,1,0:T(8,128)S(1)} %get-tuple-element.28), channel_id=1, source_target_pairs={{0,129},{1,128},{2,131},{3,130},{128,1},{129,0},{130,3},{131,2},{4... | collective-permute-start | bytes 61448 | tf_op jit(solution)/shard_map/ppermute | solution.py:580
  48.5 1.9 %collective-permute-start.7 = (f32[5,8,128]{2,1,0:T(8,128)S(1)}, f32[5,8,128]{2,1,0:T(8,128)S(1)}, u32[]{:S(2)}, u32[]{:S(2)}) collective-permute-start(f32[5,8,128]{2,1,0:T(8,128)S(1)} %get-tuple-element.29), channel_id=1, source_target_pairs={{1,130},{2,129},{129,2},{130,1},{5,134},{6,133},{133,6},{134,5},{9... | collective-permute-start | bytes 61448 | tf_op jit(solution)/shard_map/ppermute | solution.py:581
  50.5 0.1 collective-permute-done.6.near
  50.5 3.1 %collective-permute-done.7.far = f32[5,8,128]{2,1,0:T(8,128)S(1)} collective-permute-done((f32[5,8,128]{2,1,0:T(8,128)S(1)}, f32[5,8,128]{2,1,0:T(8,128)S(1)}, u32[]{:S(2)}, u32[]{:S(2)}) %collective-permute-start.7) | collective-permute-done | bytes 20512 | tf_op jit(solution)/shard_map/ppermute | solution.py:581
  53.6 0.0 collective-permute-done.5.main
  53.6 0.9 %shard_map.101 = f32[480,64]{1,0:T(8,128)} custom-call(f32[5,64,128]{2,1,0:T(8,128)S(1)} %collective-permute-done.5.main, f32[5,8,128]{2,1,0:T(8,128)S(1)} %collective-permute-done.6.near, f32[5,8,128]{2,1,0:T(8,128)S(1)} %collective-permute-done.7.far), custom_call_target="tpu_custom_call" | custom-call | flops 1000000 | bytes 800000 | tf_op jit(solution)/shard_map/pallas_call | solution.py:583
  (9 shorter events, 0.0 us)
Async XLA Ops:
  0.6 13.7 %copy-start = (f32[1,5,8,64,128]{4,3,2,1,0:T(8,128)S(1)}, f32[1,5,8,64,128]{4,3,2,1,0:T(8,128)}, u32[]{:S(2)}) copy-start(f32[1,5,8,64,128]{4,3,2,1,0:T(8,128)} %flow.5) | copy-start | bytes 3932164
  0.6 16.3 %copy-start.6 = (f32[1,2,5,5]{3,1,2,0:T(2,128)S(1)}, f32[1,2,5,5]{3,1,2,0:T(2,128)}, u32[]{:S(2)}) copy-start(f32[1,2,5,5]{3,1,2,0:T(2,128)} %param.11) | copy-start | bytes 604
  0.7 20.6 %copy-start.3 = (s32[2,512,1]{1,2,0:T(1,128)S(1)}, s32[2,512,1]{1,2,0:T(1,128)}, u32[]{:S(2)}) copy-start(s32[2,512,1]{1,2,0:T(1,128)} %param.13) | copy-start | bytes 12292
  0.7 20.6 %copy-start.4 = (s32[2,4,128]{2,1,0:T(4,128)S(1)}, s32[2,4,128]{2,1,0:T(4,128)}, u32[]{:S(2)}) copy-start(s32[2,4,128]{2,1,0:T(4,128)} %modes.1) | copy-start | bytes 12292
  0.7 20.6 %copy-start.5 = (s32[2,8,384]{2,1,0:T(8,128)S(1)}, s32[2,8,384]{2,1,0:T(8,128)}, u32[]{:S(2)}) copy-start(s32[2,8,384]{2,1,0:T(8,128)} %constant.4.clone.codes) | copy-start | bytes 73732
  2.8 23.2 %all-to-all-start = ((f32[96,4,128]{2,1,0:T(4,128)}), f32[96,4,128]{2,1,0:T(4,128)S(1)}, u32[]{:S(2)}, u32[]{:S(2)}) async-start(f32[96,4,128]{2,1,0:T(4,128)} %bitcast.1), calls=%async_computation | async-start | bytes 393216 | tf_op jit(solution)/shard_map/all_to_all | solution.py:469
  15.1 9.7 %collective-permute-start = (f32[64,128]{1,0:T(8,128)S(1)}, f32[64,128]{1,0:T(8,128)S(1)}, u32[]{:S(2)}, u32[]{:S(2)}) collective-permute-start(f32[64,128]{1,0:T(8,128)S(1)} %get-tuple-element.16), channel_id=1, source_target_pairs={{0,4},{4,0},{8,12},{12,8},{16,20},{20,16},{24,28},{28,24},{32,36},... | collective-permute-start | bytes 98312 | tf_op jit(solution)/shard_map/ppermute | solution.py:512
  17.0 5.8 %collective-permute-start.2 = (f32[1,5,2,5]{3,2,1,0:T(2,128)S(1)}, f32[1,5,2,5]{3,2,1,0:T(2,128)S(1)}, u32[]{:S(2)}, u32[]{:S(2)}) collective-permute-start(f32[1,5,2,5]{3,2,1,0:T(2,128)S(1)} %bitcast.16), channel_id=1, source_target_pairs={{0,128},{128,0},{1,129},{129,1},{2,130},{130,2},{3,131},{131,3},{4... | collective-permute-start | bytes 608 | tf_op jit(solution)/shard_map/ppermute | solution.py:511
  17.0 7.8 %collective-permute-start.1 = (f32[64,128]{1,0:T(8,128)S(1)}, f32[64,128]{1,0:T(8,128)S(1)}, u32[]{:S(2)}, u32[]{:S(2)}) collective-permute-start(f32[64,128]{1,0:T(8,128)S(1)} %get-tuple-element.17), channel_id=1, source_target_pairs={{4,8},{8,4},{12,16},{16,12},{20,24},{24,20},{28,32},{32,28},{36,40... | collective-permute-start | bytes 98312 | tf_op jit(solution)/shard_map/ppermute | solution.py:513
  26.0 15.2 %copy-start.1 = (f32[1,5,64,128]{3,2,1,0:T(8,128)S(1)}, f32[1,5,64,128]{3,2,1,0:T(8,128)}, u32[]{:S(2)}) copy-start(f32[1,5,64,128]{3,2,1,0:T(8,128)} %inflow.1) | copy-start | bytes 491524
  26.0 15.2 %copy-start.2 = (f32[1,3,5,5]{3,0,2,1:T(1,128)S(1)}, f32[1,3,5,5]{3,0,2,1:T(1,128)}, u32[]{:S(2)}) copy-start(f32[1,3,5,5]{3,0,2,1:T(1,128)} %param.10) | copy-start | bytes 904
  28.8 17.0 %all-to-all-start.1 = ((f32[96,4,128]{2,1,0:T(4,128)}), f32[96,4,128]{2,1,0:T(4,128)S(1)}, u32[]{:S(2)}, u32[]{:S(2)}) async-start(f32[96,4,128]{2,1,0:T(4,128)} %bitcast.5), calls=%async_computation.1 | async-start | bytes 393216 | tf_op jit(solution)/shard_map/all_to_all | solution.py:469
  34.3 3.9 %collective-permute-start.3 = (f32[5,8,128]{2,1,0:T(8,128)S(1)}, f32[5,8,128]{2,1,0:T(8,128)S(1)}, u32[]{:S(2)}, u32[]{:S(2)}) collective-permute-start(f32[5,8,128]{2,1,0:T(8,128)S(1)} %get-tuple-element.22), channel_id=1, source_target_pairs={{0,1},{1,0},{2,3},{3,2},{4,5},{5,4},{6,7},{7,6},{8,9},{9,8},{10,11... | collective-permute-start | bytes 61448 | tf_op jit(solution)/shard_map/ppermute | solution.py:546
  35.6 5.7 %collective-permute-start.4 = (f32[5,8,128]{2,1,0:T(8,128)S(1)}, f32[5,8,128]{2,1,0:T(8,128)S(1)}, u32[]{:S(2)}, u32[]{:S(2)}) collective-permute-start(f32[5,8,128]{2,1,0:T(8,128)S(1)} %get-tuple-element.23), channel_id=1, source_target_pairs={{1,2},{2,1},{5,6},{6,5},{9,10},{10,9},{13,14},{14,13},{17,18},{18,... | collective-permute-start | bytes 61448 | tf_op jit(solution)/shard_map/ppermute | solution.py:547
  47.1 6.5 %collective-permute-start.5 = (f32[5,64,128]{2,1,0:T(8,128)S(1)}, f32[5,64,128]{2,1,0:T(8,128)S(1)}, u32[]{:S(2)}, u32[]{:S(2)}) collective-permute-start(f32[5,64,128]{2,1,0:T(8,128)S(1)} %get-tuple-element.27), channel_id=1, source_target_pairs={{0,128},{128,0},{1,129},{129,1},{2,130},{130,2},{3,131},{131,3},{4... | collective-permute-start | bytes 491528 | tf_op jit(solution)/shard_map/ppermute | solution.py:582
  47.2 3.3 %collective-permute-start.6 = (f32[5,8,128]{2,1,0:T(8,128)S(1)}, f32[5,8,128]{2,1,0:T(8,128)S(1)}, u32[]{:S(2)}, u32[]{:S(2)}) collective-permute-start(f32[5,8,128]{2,1,0:T(8,128)S(1)} %get-tuple-element.28), channel_id=1, source_target_pairs={{0,129},{1,128},{2,131},{3,130},{128,1},{129,0},{130,3},{131,2},{4... | collective-permute-start | bytes 61448 | tf_op jit(solution)/shard_map/ppermute | solution.py:580
  48.5 5.1 %collective-permute-start.7 = (f32[5,8,128]{2,1,0:T(8,128)S(1)}, f32[5,8,128]{2,1,0:T(8,128)S(1)}, u32[]{:S(2)}, u32[]{:S(2)}) collective-permute-start(f32[5,8,128]{2,1,0:T(8,128)S(1)} %get-tuple-element.29), channel_id=1, source_target_pairs={{1,130},{2,129},{129,2},{130,1},{5,134},{6,133},{133,6},{134,5},{9... | collective-permute-start | bytes 61448 | tf_op jit(solution)/shard_map/ppermute | solution.py:581

commit v5 on v4

--- a/solution.py
+++ b/solution.py
@@ -215,8 +215,14 @@
     done[...] = jnp.zeros(done.shape, f32)
 
 
-def table_kernel(dest, modes, codes, place, terms):
+def table_kernel(dest, modes, codes, tables, place, terms, weights, arrived):
     source = lax.axis_index("row")
+    fetches = [
+        pltpu.make_async_copy(tables.at[source, part], weights.at[part], arrived.at[part])
+        for part in range(2)
+    ]
+    for fetch in fetches:
+        fetch.start()
     own = jnp.where(source == 0, BLADES, VANES)
     other = jnp.where(source == 0, VANES, BLADES)
     dest_row = dest[source]
@@ -265,17 +271,12 @@
     terms[0:1] = sign * sigma
     terms[1:2] = sign * kappa
     terms[2:3] = RELAX / (4.0 + sigma * sigma)
-
-
-def spectrum_kernel(cells, tables, place, *rest):
-    out, values, weights, arrived = rest[-4:]
-    mine = lax.axis_index("row")
-    fetches = [
-        pltpu.make_async_copy(tables.at[mine, part], weights.at[part], arrived.at[part])
-        for part in range(2)
-    ]
     for fetch in fetches:
-        fetch.start()
+        fetch.wait()
+
+
+def spectrum_kernel(cells, weights, place, *rest):
+    out, values = rest[-2:]
     lane = iota((8, LANES), 1)
     sub = iota((8, LANES), 0)
     parts = []
@@ -318,8 +319,6 @@
             im = im + jnp.where(lane == 0, cos * high_im - sin * high_re, 0.0)
             columns += [re, im]
         closed.append(columns)
-    for fetch in fetches:
-        fetch.wait()
     wide = iota((16, LANES), 1)
     spot = lax.bitwise_and(wide, SLOT_LANES - 1)
     side = jnp.where(spot < HALF_CLASS, 1.0, -1.0)
@@ -506,43 +505,47 @@
         compiler_params=BIG,
         cost_estimate=cost(4_000_000, 1_400_000),
     )(flow)
-    sweep_jac = jnp.transpose(sweep_jacobian, (0, 2, 1, 3))
-    sweep_jac = lax.optimization_barrier((sweep_jac, faces[0]))[0]
-    sweep_jac = lax.ppermute(sweep_jac, "row", [(0, 1), (1, 0)])
     pitch_near = lax.ppermute(faces[0], "pitch", near_pitch)
     pitch_far = lax.ppermute(faces[1], "pitch", far_pitch)
-    place, terms = pl.pallas_call(
+    place, terms, own_weights = pl.pallas_call(
         table_kernel,
-        out_shape=(shape(TABLE, PACKED, dtype=bf16), shape(8, LANES)),
-        in_specs=[VMEM, VMEM, VMEM],
-        out_specs=(VMEM,) * 2,
+        out_shape=(
+            shape(TABLE, PACKED, dtype=bf16),
+            shape(8, LANES),
+            shape(2, 9, LANES, LANES, dtype=bf16),
+        ),
+        in_specs=[VMEM, VMEM, VMEM, ANY],
+        out_specs=(VMEM,) * 3,
+        scratch_shapes=[pltpu.SemaphoreType.DMA((2,))],
         compiler_params=BIG,
         cost_estimate=cost(2 * TABLE * MODES * PACKED, 2_000_000),
-    )(jnp.swapaxes(destination, 1, 2), mode_index, codes)
+    )(
+        jnp.swapaxes(destination, 1, 2),
+        mode_index,
+        codes,
+        pltpu.with_memory_space_constraint(jnp.asarray(weights), pltpu.HBM),
+    )
 
     placed = pl.pallas_call(
         spectrum_kernel,
         out_shape=shape(SENT, LANES),
-        in_specs=[VMEM, ANY, VMEM, ANY, ANY, ANY],
+        in_specs=[VMEM, VMEM, VMEM, ANY, ANY],
         out_specs=VMEM,
-        scratch_shapes=[
-            pltpu.VMEM((32, TABLE), f32),
-            pltpu.VMEM((2, 9, LANES, LANES), bf16),
-            pltpu.SemaphoreType.DMA((2,)),
-        ],
+        scratch_shapes=[pltpu.VMEM((32, TABLE), f32)],
         compiler_params=BIG,
         cost_estimate=cost(200_000_000, 3_000_000),
     )(
         cells,
-        pltpu.with_memory_space_constraint(jnp.asarray(weights), pltpu.HBM),
+        own_weights,
         place,
         pitch_near,
         pitch_far,
-        sweep_jac,
     )
     amplitude = transposed(placed)
 
-    rows = lax.optimization_barrier((faces[2], faces[3], placed))[:2]
+    sweep_jac = jnp.transpose(sweep_jacobian, (0, 2, 1, 3))
+    *rows, sweep_jac = lax.optimization_barrier((faces[2], faces[3], sweep_jac, placed))[:3]
+    sweep_jac = lax.ppermute(sweep_jac, "row", [(0, 1), (1, 0)])
     rad_near = lax.ppermute(rows[0], "rad", near_rad)
     rad_far = lax.ppermute(rows[1], "rad", far_rad)
     next_flow, flux_done = pl.pallas_call(
@@ -566,7 +569,7 @@
         scratch_shapes=[pltpu.VMEM((F, RAD, LANES), f32)],
         compiler_params=BIG,
         cost_estimate=cost(20_000_000, 3_000_000),
-    )(flux_jac, flow, inflow, pitch_near, pitch_far, rad_near, rad_far, placed)
+    )(flux_jac, pinned, inflow, pitch_near, pitch_far, rad_near, rad_far, placed)
 
     main, near, far = pl.pallas_call(
         sweep_kernel,

time: 55.1 us -> 53.8 us (0.976)
    pallas_call x1, Pallas kernels: 2.72 us -> 1.65 us  [on_device(): pl.pallas_call(spectrum_kernel, out_shape=shape(SENT, LANES), in_specs=[V...]
    all_to_all x2, starting transfers between devices: 17.1 us -> 16.4 us  [transposed(): return lax.all_to_all(value, 'pitch', 0, 0, tiled=True).reshape(SENT, LANES)]
  transfers between devices with their start and end apart: 10 -> 10, of which waited for: 7 -> 7; matrix products, arithmetic and copies ran while one was open for 0% -> 0% of each run, Pallas kernels for 11% -> 13%
where the time goes in v5:
time: 53.8 us; the launch traced here: 53.2 us
  starting transfers between devices  29.2 us (54%)
  Pallas kernels  12.7 us (24%)
  waiting for transfers between devices  10.5 us (20%)
  between operations  0.77 us (1%)
    all_to_all x2, starting transfers between devices, transposed(): return lax.all_to_all(value, 'pitch', 0, 0, tiled=True).reshape(SENT, LANES)  16.4 us
    ppermute x1, starting transfers between devices, on_device(): pitch_far = lax.ppermute(faces[1], 'pitch', far_pitch)  4.26 us
    pallas_call x1, Pallas kernels, on_device(): pl.pallas_call(flux_kernel, grid=(AXIAL // DEPTH,), out_shape=(shape(1, F...  4.06 us
    ppermute x1, waiting for transfers between devices, on_device(): far = lax.ppermute(far, ('row', 'rad'), across(far_rad))  3.12 us
    ppermute x1, waiting for transfers between devices, on_device(): rad_far = lax.ppermute(rows[1], 'rad', far_rad)  3.08 us
    all_to_all x2, waiting for transfers between devices, transposed(): return lax.all_to_all(value, 'pitch', 0, 0, tiled=True).reshape(SENT, LANES)  2.26 us
    pallas_call x1, Pallas kernels, on_device(): pl.pallas_call(exit_kernel, out_shape=shape(SENT, LANES), in_specs=[ANY,...  2.14 us
    ppermute x1, starting transfers between devices, on_device(): rad_far = lax.ppermute(rows[1], 'rad', far_rad)  1.91 us
  transfers between devices with their start and end apart: 10, of which 7 were waited for; matrix products, arithmetic and copies ran while one was open for 0% of the time, Pallas kernels for 13%

profile of v5, /device:TPU:4, one launch (start us, length us, event | category | flops | bytes accessed | tf_op | source)
XLA Modules:
  0.0 53.2 jit_solution(11283553992336630577)
XLA Ops:
  0.6 0.0 copy-start
  0.6 0.0 copy-start.3
  0.7 0.0 copy-start.4
  0.7 0.0 copy-start.5
  0.7 2.1 %shard_map.96 = f32[384,128]{1,0:T(8,128)} custom-call(f32[3,5,1,5]{3,2,1,0:T(1,128)} %bitcast.12, f32[1,5,8,64,128]{4,3,2,1,0:T(8,128)} %flow.5), custom_call_target="tpu_custom_call" | custom-call | flops 4000000 | bytes 600000 | tf_op jit(solution)/shard_map/pallas_call | solution.py:483
  2.8 11.5 %all-to-all-start = ((f32[96,4,128]{2,1,0:T(4,128)}), f32[96,4,128]{2,1,0:T(4,128)S(1)}, u32[]{:S(2)}, u32[]{:S(2)}) async-start(f32[96,4,128]{2,1,0:T(4,128)} %bitcast.2), calls=%async_computation | async-start | bytes 393216 | tf_op jit(solution)/shard_map/all_to_all | solution.py:468
  14.3 0.7 %shard_map.95 = (f32[64,128]{1,0:T(8,128)S(1)}, f32[64,128]{1,0:T(8,128)S(1)}, f32[5,8,128]{2,1,0:T(8,128)S(1)}, f32[5,8,128]{2,1,0:T(8,128)S(1)}) custom-call(f32[1,5,8,64,128]{4,3,2,1,0:T(8,128)S(1)} %copy-done), custom_call_target="tpu_custom_call" | custom-call | flops 4000000 | bytes 1400000 | tf_op jit(solution)/shard_map/pallas_call | solution.py:500
  15.1 1.9 %collective-permute-start = (f32[64,128]{1,0:T(8,128)S(1)}, f32[64,128]{1,0:T(8,128)S(1)}, u32[]{:S(2)}, u32[]{:S(2)}) collective-permute-start(f32[64,128]{1,0:T(8,128)S(1)} %get-tuple-element.17), channel_id=1, source_target_pairs={{0,4},{4,0},{8,12},{12,8},{16,20},{20,16},{24,28},{28,24},{32,36},... | collective-permute-start | bytes 98312 | tf_op jit(solution)/shard_map/ppermute | solution.py:508
  17.0 4.3 %collective-permute-start.1 = (f32[64,128]{1,0:T(8,128)S(1)}, f32[64,128]{1,0:T(8,128)S(1)}, u32[]{:S(2)}, u32[]{:S(2)}) collective-permute-start(f32[64,128]{1,0:T(8,128)S(1)} %get-tuple-element.18), channel_id=1, source_target_pairs={{4,8},{8,4},{12,16},{16,12},{20,24},{24,20},{28,32},{32,28},{36,40... | collective-permute-start | bytes 98312 | tf_op jit(solution)/shard_map/ppermute | solution.py:509
  21.2 0.0 copy-done.4
  21.2 1.9 %shard_map.97 = (bf16[384,2048]{1,0:T(8,128)(2,1)S(1)}, f32[8,128]{1,0:T(8,128)S(1)}, bf16[2,9,128,128]{3,2,1,0:T(8,128)(2,1)S(1)}) custom-call(s32[2,1,512]{2,1,0:T(1,128)S(1)} %bitcast.14, s32[2,4,128]{2,1,0:T(4,128)S(1)} %copy-done.4, s32[2,8,384]{2,1,0:T(8,128)S(1)} %copy-done.5, bf16[2,2,9,128,128]{4,3,2,1,0:T(8,128)(2,1)} %constant.4.clone.tables), custom_call_target="tpu_custom_call" | custom-call | flops 805306368 | bytes 2000000 | tf_op jit(solution)/shard_map/pallas_call | solution.py:510
  23.1 0.0 collective-permute-done.rest_0_.pitch_near
  23.1 1.5 %collective-permute-done.1.rest_1_.pitch_far = f32[64,128]{1,0:T(8,128)S(1)} collective-permute-done((f32[64,128]{1,0:T(8,128)S(1)}, f32[64,128]{1,0:T(8,128)S(1)}, u32[]{:S(2)}, u32[]{:S(2)}) %collective-permute-start.1) | collective-permute-done | bytes 32800 | tf_op jit(solution)/shard_map/ppermute | solution.py:509
  24.6 2.1 %all-to-all-done = f32[96,4,128]{2,1,0:T(4,128)S(1)} async-done(((f32[96,4,128]{2,1,0:T(4,128)}), f32[96,4,128]{2,1,0:T(4,128)S(1)}, u32[]{:S(2)}, u32[]{:S(2)}) %all-to-all-start) | async-done | bytes 196640 | tf_op jit(solution)/shard_map/all_to_all | solution.py:468
  26.6 1.6 %shard_map.98.after = f32[384,128]{1,0:T(8,128)} custom-call(f32[384,128]{1,0:T(8,128)S(1)} %bitcast.10, bf16[2,9,128,128]{3,2,1,0:T(8,128)(2,1)S(1)} %get-tuple-element.21.weights, bf16[384,2048]{1,0:T(8,128)(2,1)S(1)} %get-tuple-element.22.place, f32[64,128]{1,0:T(8,128)S(1)} %collective-permute-done.rest_0_.pitch_near, ...), custom_call_target="tpu_custom_call" | custom-call | flops 200000000 | bytes 3000000 | tf_op jit(solution)/shard_map/pallas_call | solution.py:529
  28.3 4.9 %all-to-all-start.1 = ((f32[96,4,128]{2,1,0:T(4,128)}), f32[96,4,128]{2,1,0:T(4,128)S(1)}, u32[]{:S(2)}, u32[]{:S(2)}) async-start(f32[96,4,128]{2,1,0:T(4,128)} %bitcast.5), calls=%async_computation.1 | async-start | bytes 393216 | tf_op jit(solution)/shard_map/all_to_all | solution.py:468
  33.2 1.3 %collective-permute-start.2 = (f32[5,8,128]{2,1,0:T(8,128)S(1)}, f32[5,8,128]{2,1,0:T(8,128)S(1)}, u32[]{:S(2)}, u32[]{:S(2)}) collective-permute-start(f32[5,8,128]{2,1,0:T(8,128)S(1)} %get-tuple-element.23), channel_id=1, source_target_pairs={{0,1},{1,0},{2,3},{3,2},{4,5},{5,4},{6,7},{7,6},{8,9},{9,8},{10,11... | collective-permute-start | bytes 61448 | tf_op jit(solution)/shard_map/ppermute | solution.py:549
  34.5 1.9 %collective-permute-start.3 = (f32[5,8,128]{2,1,0:T(8,128)S(1)}, f32[5,8,128]{2,1,0:T(8,128)S(1)}, u32[]{:S(2)}, u32[]{:S(2)}) collective-permute-start(f32[5,8,128]{2,1,0:T(8,128)S(1)} %get-tuple-element.24), channel_id=1, source_target_pairs={{1,2},{2,1},{5,6},{6,5},{9,10},{10,9},{13,14},{14,13},{17,18},{18,... | collective-permute-start | bytes 61448 | tf_op jit(solution)/shard_map/ppermute | solution.py:550
  36.4 0.1 collective-permute-start.4
  36.5 0.6 %collective-permute-done.2.rad_near = f32[5,8,128]{2,1,0:T(8,128)S(1)} collective-permute-done((f32[5,8,128]{2,1,0:T(8,128)S(1)}, f32[5,8,128]{2,1,0:T(8,128)S(1)}, u32[]{:S(2)}, u32[]{:S(2)}) %collective-permute-start.2) | collective-permute-done | bytes 20512 | tf_op jit(solution)/shard_map/ppermute | solution.py:549
  37.1 3.1 %collective-permute-done.3.rad_far = f32[5,8,128]{2,1,0:T(8,128)S(1)} collective-permute-done((f32[5,8,128]{2,1,0:T(8,128)S(1)}, f32[5,8,128]{2,1,0:T(8,128)S(1)}, u32[]{:S(2)}, u32[]{:S(2)}) %collective-permute-start.3) | collective-permute-done | bytes 20512 | tf_op jit(solution)/shard_map/ppermute | solution.py:550
  40.2 4.1 %shard_map.99 = (f32[1,5,8,64,128]{4,3,2,1,0:T(8,128)}, f32[8,128]{1,0:T(8,128)S(1)}) custom-call(f32[3,5,1,5]{3,2,1,0:T(1,128)S(1)} %bitcast.13, f32[1,5,8,64,128]{4,3,2,1,0:T(8,128)} %flow.5, f32[1,5,64,128]{3,2,1,0:T(8,128)S(1)} %copy-done.1, f32[64,128]{1,0:T(8,128)S(1)} %collective-permute-done.rest_0_.pitch_near, ...), custom_call_target="tpu_custom_call" | custom-call | flops 20000000 | bytes 3000000 | tf_op jit(solution)/shard_map/pallas_call | solution.py:551
  44.2 0.0 collective-permute-done.4.jac
  44.2 0.2 all-to-all-done.1
  44.4 1.4 %shard_map.100 = (f32[5,64,128]{2,1,0:T(8,128)S(1)}, f32[5,8,128]{2,1,0:T(8,128)S(1)}, f32[5,8,128]{2,1,0:T(8,128)S(1)}) custom-call(f32[1,5,2,5]{3,2,1,0:T(2,128)S(1)} %collective-permute-done.4.jac, f32[384,128]{1,0:T(8,128)S(1)} %bitcast.11, f32[8,128]{1,0:T(8,128)S(1)} %get-tuple-element.27.terms, f32[8,128]{1,0:T(8,128)S(1)} %get-tuple-element.28.after), custom_call_target="tpu_custom_call" | custom-call | flops 8000000 | bytes 500000 | tf_op jit(solution)/shard_map/pallas_call | solution.py:574
  45.8 0.1 collective-permute-start.5
  45.9 1.3 %collective-permute-start.6 = (f32[5,8,128]{2,1,0:T(8,128)S(1)}, f32[5,8,128]{2,1,0:T(8,128)S(1)}, u32[]{:S(2)}, u32[]{:S(2)}) collective-permute-start(f32[5,8,128]{2,1,0:T(8,128)S(1)} %get-tuple-element.30), channel_id=1, source_target_pairs={{0,129},{1,128},{2,131},{3,130},{128,1},{129,0},{130,3},{131,2},{4... | collective-permute-start | bytes 61448 | tf_op jit(solution)/shard_map/ppermute | solution.py:583
  47.2 1.9 %collective-permute-start.7 = (f32[5,8,128]{2,1,0:T(8,128)S(1)}, f32[5,8,128]{2,1,0:T(8,128)S(1)}, u32[]{:S(2)}, u32[]{:S(2)}) collective-permute-start(f32[5,8,128]{2,1,0:T(8,128)S(1)} %get-tuple-element.31), channel_id=1, source_target_pairs={{1,130},{2,129},{129,2},{130,1},{5,134},{6,133},{133,6},{134,5},{9... | collective-permute-start | bytes 61448 | tf_op jit(solution)/shard_map/ppermute | solution.py:584
  49.1 0.1 collective-permute-done.6.near
  49.2 3.1 %collective-permute-done.7.far = f32[5,8,128]{2,1,0:T(8,128)S(1)} collective-permute-done((f32[5,8,128]{2,1,0:T(8,128)S(1)}, f32[5,8,128]{2,1,0:T(8,128)S(1)}, u32[]{:S(2)}, u32[]{:S(2)}) %collective-permute-start.7) | collective-permute-done | bytes 20512 | tf_op jit(solution)/shard_map/ppermute | solution.py:584
  52.3 0.0 collective-permute-done.5.main
  52.3 0.9 %shard_map.101 = f32[480,64]{1,0:T(8,128)} custom-call(f32[5,64,128]{2,1,0:T(8,128)S(1)} %collective-permute-done.5.main, f32[5,8,128]{2,1,0:T(8,128)S(1)} %collective-permute-done.6.near, f32[5,8,128]{2,1,0:T(8,128)S(1)} %collective-permute-done.7.far), custom_call_target="tpu_custom_call" | custom-call | flops 1000000 | bytes 800000 | tf_op jit(solution)/shard_map/pallas_call | solution.py:586
  (9 shorter events, 0.0 us)
Async XLA Ops:
  0.6 13.7 %copy-start = (f32[1,5,8,64,128]{4,3,2,1,0:T(8,128)S(1)}, f32[1,5,8,64,128]{4,3,2,1,0:T(8,128)}, u32[]{:S(2)}) copy-start(f32[1,5,8,64,128]{4,3,2,1,0:T(8,128)} %flow.5) | copy-start | bytes 3932164
  0.6 20.6 %copy-start.3 = (s32[2,512,1]{1,2,0:T(1,128)S(1)}, s32[2,512,1]{1,2,0:T(1,128)}, u32[]{:S(2)}) copy-start(s32[2,512,1]{1,2,0:T(1,128)} %param.13) | copy-start | bytes 12292
  0.7 20.6 %copy-start.4 = (s32[2,4,128]{2,1,0:T(4,128)S(1)}, s32[2,4,128]{2,1,0:T(4,128)}, u32[]{:S(2)}) copy-start(s32[2,4,128]{2,1,0:T(4,128)} %modes.1) | copy-start | bytes 12292
  0.7 20.6 %copy-start.5 = (s32[2,8,384]{2,1,0:T(8,128)S(1)}, s32[2,8,384]{2,1,0:T(8,128)}, u32[]{:S(2)}) copy-start(s32[2,8,384]{2,1,0:T(8,128)} %constant.5.clone.codes) | copy-start | bytes 73732
  2.8 23.8 %all-to-all-start = ((f32[96,4,128]{2,1,0:T(4,128)}), f32[96,4,128]{2,1,0:T(4,128)S(1)}, u32[]{:S(2)}, u32[]{:S(2)}) async-start(f32[96,4,128]{2,1,0:T(4,128)} %bitcast.2), calls=%async_computation | async-start | bytes 393216 | tf_op jit(solution)/shard_map/all_to_all | solution.py:468
  15.1 8.0 %collective-permute-start = (f32[64,128]{1,0:T(8,128)S(1)}, f32[64,128]{1,0:T(8,128)S(1)}, u32[]{:S(2)}, u32[]{:S(2)}) collective-permute-start(f32[64,128]{1,0:T(8,128)S(1)} %get-tuple-element.17), channel_id=1, source_target_pairs={{0,4},{4,0},{8,12},{12,8},{16,20},{20,16},{24,28},{28,24},{32,36},... | collective-permute-start | bytes 98312 | tf_op jit(solution)/shard_map/ppermute | solution.py:508
  17.0 7.6 %collective-permute-start.1 = (f32[64,128]{1,0:T(8,128)S(1)}, f32[64,128]{1,0:T(8,128)S(1)}, u32[]{:S(2)}, u32[]{:S(2)}) collective-permute-start(f32[64,128]{1,0:T(8,128)S(1)} %get-tuple-element.18), channel_id=1, source_target_pairs={{4,8},{8,4},{12,16},{16,12},{20,24},{24,20},{28,32},{32,28},{36,40... | collective-permute-start | bytes 98312 | tf_op jit(solution)/shard_map/ppermute | solution.py:509
  26.6 9.8 %copy-start.6 = (f32[1,2,5,5]{3,1,2,0:T(2,128)S(1)}, f32[1,2,5,5]{3,1,2,0:T(2,128)}, u32[]{:S(2)}) copy-start(f32[1,2,5,5]{3,1,2,0:T(2,128)} %param.11) | copy-start | bytes 604
  26.6 13.5 %copy-start.1 = (f32[1,5,64,128]{3,2,1,0:T(8,128)S(1)}, f32[1,5,64,128]{3,2,1,0:T(8,128)}, u32[]{:S(2)}) copy-start(f32[1,5,64,128]{3,2,1,0:T(8,128)} %inflow.1) | copy-start | bytes 491524
  26.6 13.5 %copy-start.2 = (f32[1,3,5,5]{3,0,2,1:T(1,128)S(1)}, f32[1,3,5,5]{3,0,2,1:T(1,128)}, u32[]{:S(2)}) copy-start(f32[1,3,5,5]{3,0,2,1:T(1,128)} %param.10) | copy-start | bytes 904
  28.3 16.2 %all-to-all-start.1 = ((f32[96,4,128]{2,1,0:T(4,128)}), f32[96,4,128]{2,1,0:T(4,128)S(1)}, u32[]{:S(2)}, u32[]{:S(2)}) async-start(f32[96,4,128]{2,1,0:T(4,128)} %bitcast.5), calls=%async_computation.1 | async-start | bytes 393216 | tf_op jit(solution)/shard_map/all_to_all | solution.py:468
  33.2 3.9 %collective-permute-start.2 = (f32[5,8,128]{2,1,0:T(8,128)S(1)}, f32[5,8,128]{2,1,0:T(8,128)S(1)}, u32[]{:S(2)}, u32[]{:S(2)}) collective-permute-start(f32[5,8,128]{2,1,0:T(8,128)S(1)} %get-tuple-element.23), channel_id=1, source_target_pairs={{0,1},{1,0},{2,3},{3,2},{4,5},{5,4},{6,7},{7,6},{8,9},{9,8},{10,11... | collective-permute-start | bytes 61448 | tf_op jit(solution)/shard_map/ppermute | solution.py:549
  34.5 5.7 %collective-permute-start.3 = (f32[5,8,128]{2,1,0:T(8,128)S(1)}, f32[5,8,128]{2,1,0:T(8,128)S(1)}, u32[]{:S(2)}, u32[]{:S(2)}) collective-permute-start(f32[5,8,128]{2,1,0:T(8,128)S(1)} %get-tuple-element.24), channel_id=1, source_target_pairs={{1,2},{2,1},{5,6},{6,5},{9,10},{10,9},{13,14},{14,13},{17,18},{18,... | collective-permute-start | bytes 61448 | tf_op jit(solution)/shard_map/ppermute | solution.py:550
  36.4 7.8 %collective-permute-start.4 = (f32[1,5,2,5]{3,2,1,0:T(2,128)S(1)}, f32[1,5,2,5]{3,2,1,0:T(2,128)S(1)}, u32[]{:S(2)}, u32[]{:S(2)}) collective-permute-start(f32[1,5,2,5]{3,2,1,0:T(2,128)S(1)} %bitcast.16), channel_id=1, source_target_pairs={{0,128},{128,0},{1,129},{129,1},{2,130},{130,2},{3,131},{131,3},{4... | collective-permute-start | bytes 608 | tf_op jit(solution)/shard_map/ppermute | solution.py:548
  45.8 6.5 %collective-permute-start.5 = (f32[5,64,128]{2,1,0:T(8,128)S(1)}, f32[5,64,128]{2,1,0:T(8,128)S(1)}, u32[]{:S(2)}, u32[]{:S(2)}) collective-permute-start(f32[5,64,128]{2,1,0:T(8,128)S(1)} %get-tuple-element.29), channel_id=1, source_target_pairs={{0,128},{128,0},{1,129},{129,1},{2,130},{130,2},{3,131},{131,3},{4... | collective-permute-start | bytes 491528 | tf_op jit(solution)/shard_map/ppermute | solution.py:585
  45.9 3.3 %collective-permute-start.6 = (f32[5,8,128]{2,1,0:T(8,128)S(1)}, f32[5,8,128]{2,1,0:T(8,128)S(1)}, u32[]{:S(2)}, u32[]{:S(2)}) collective-permute-start(f32[5,8,128]{2,1,0:T(8,128)S(1)} %get-tuple-element.30), channel_id=1, source_target_pairs={{0,129},{1,128},{2,131},{3,130},{128,1},{129,0},{130,3},{131,2},{4... | collective-permute-start | bytes 61448 | tf_op jit(solution)/shard_map/ppermute | solution.py:583
  47.2 5.1 %collective-permute-start.7 = (f32[5,8,128]{2,1,0:T(8,128)S(1)}, f32[5,8,128]{2,1,0:T(8,128)S(1)}, u32[]{:S(2)}, u32[]{:S(2)}) collective-permute-start(f32[5,8,128]{2,1,0:T(8,128)S(1)} %get-tuple-element.31), channel_id=1, source_target_pairs={{1,130},{2,129},{129,2},{130,1},{5,134},{6,133},{133,6},{134,5},{9... | collective-permute-start | bytes 61448 | tf_op jit(solution)/shard_map/ppermute | solution.py:584

commit v6 on v5

--- a/solution.py
+++ b/solution.py
@@ -155,7 +155,7 @@
     pitch_far[...] = jnp.where(pitch_even, low, high)
 
 
-DEPTH = 4
+DEPTH = 2
 ROWS = 16
 
 
@@ -251,7 +251,7 @@
             before = before + same.astype(f32)
         rank = jnp.sum(before, axis=1, keepdims=True).astype(jnp.int32)
         slot = dest_col * SLOT_LANES + rank
-        hits.append((slot[:, :1] == spread).astype(f32).astype(bf16))
+        hits.append(jnp.where(slot[:, :1] == spread, 1.0, 0.0).astype(bf16))
         mine = jnp.where(slot == target, column(code_row, block), 0)
         slot_code = slot_code + jnp.sum(mine, axis=0, keepdims=True)
     hit = jnp.concatenate(hits, axis=0)

time: 53.8 us -> 53.8 us (level)
  transfers between devices with their start and end apart: 10 -> 10, of which waited for: 7 -> 6; matrix products, arithmetic and copies ran while one was open for 0% -> 0% of each run, Pallas kernels for 13% -> 13%
where the time goes in v6:
time: 53.8 us; the launch traced here: 53.2 us
  starting transfers between devices  28.9 us (54%)
  Pallas kernels  13.1 us (24%)
  waiting for transfers between devices  10.3 us (19%)
  between operations  0.78 us (1%)
    all_to_all x2, starting transfers between devices, transposed(): return lax.all_to_all(value, 'pitch', 0, 0, tiled=True).reshape(SENT, LANES)  16.4 us
    pallas_call x1, Pallas kernels, on_device(): pl.pallas_call(flux_kernel, grid=(AXIAL // DEPTH,), out_shape=(shape(1, F...  4.52 us
    ppermute x1, starting transfers between devices, on_device(): pitch_far = lax.ppermute(faces[1], 'pitch', far_pitch)  4.26 us
    ppermute x1, waiting for transfers between devices, on_device(): rad_far = lax.ppermute(rows[1], 'rad', far_rad)  3.08 us
    ppermute x1, waiting for transfers between devices, on_device(): far = lax.ppermute(far, ('row', 'rad'), across(far_rad))  2.86 us
    pallas_call x1, Pallas kernels, on_device(): pl.pallas_call(exit_kernel, out_shape=shape(SENT, LANES), in_specs=[ANY,...  2.14 us
    all_to_all x2, waiting for transfers between devices, transposed(): return lax.all_to_all(value, 'pitch', 0, 0, tiled=True).reshape(SENT, LANES)  2.06 us
    ppermute x1, starting transfers between devices, on_device(): rad_far = lax.ppermute(rows[1], 'rad', far_rad)  1.91 us
  transfers between devices with their start and end apart: 10, of which 6 were waited for; matrix products, arithmetic and copies ran while one was open for 0% of the time, Pallas kernels for 13%

profile of v6, /device:TPU:4, one launch (start us, length us, event | category | flops | bytes accessed | tf_op | source)
XLA Modules:
  0.0 53.2 jit_solution(14175323489597557077)
XLA Ops:
  0.6 0.0 copy-start
  0.6 0.0 copy-start.3
  0.7 0.0 copy-start.4
  0.7 0.0 copy-start.5
  0.7 2.1 %shard_map.96 = f32[384,128]{1,0:T(8,128)} custom-call(f32[3,5,1,5]{3,2,1,0:T(1,128)} %bitcast.12, f32[1,5,8,64,128]{4,3,2,1,0:T(8,128)} %flow.5), custom_call_target="tpu_custom_call" | custom-call | flops 4000000 | bytes 600000 | tf_op jit(solution)/shard_map/pallas_call | solution.py:483
  2.8 11.5 %all-to-all-start = ((f32[96,4,128]{2,1,0:T(4,128)}), f32[96,4,128]{2,1,0:T(4,128)S(1)}, u32[]{:S(2)}, u32[]{:S(2)}) async-start(f32[96,4,128]{2,1,0:T(4,128)} %bitcast.2), calls=%async_computation | async-start | bytes 393216 | tf_op jit(solution)/shard_map/all_to_all | solution.py:468
  14.3 0.7 %shard_map.95 = (f32[64,128]{1,0:T(8,128)S(1)}, f32[64,128]{1,0:T(8,128)S(1)}, f32[5,8,128]{2,1,0:T(8,128)S(1)}, f32[5,8,128]{2,1,0:T(8,128)S(1)}) custom-call(f32[1,5,8,64,128]{4,3,2,1,0:T(8,128)S(1)} %copy-done), custom_call_target="tpu_custom_call" | custom-call | flops 4000000 | bytes 1400000 | tf_op jit(solution)/shard_map/pallas_call | solution.py:500
  15.1 1.9 %collective-permute-start = (f32[64,128]{1,0:T(8,128)S(1)}, f32[64,128]{1,0:T(8,128)S(1)}, u32[]{:S(2)}, u32[]{:S(2)}) collective-permute-start(f32[64,128]{1,0:T(8,128)S(1)} %get-tuple-element.17), channel_id=1, source_target_pairs={{0,4},{4,0},{8,12},{12,8},{16,20},{20,16},{24,28},{28,24},{32,36},... | collective-permute-start | bytes 98312 | tf_op jit(solution)/shard_map/ppermute | solution.py:508
  17.0 4.3 %collective-permute-start.1 = (f32[64,128]{1,0:T(8,128)S(1)}, f32[64,128]{1,0:T(8,128)S(1)}, u32[]{:S(2)}, u32[]{:S(2)}) collective-permute-start(f32[64,128]{1,0:T(8,128)S(1)} %get-tuple-element.18), channel_id=1, source_target_pairs={{4,8},{8,4},{12,16},{16,12},{20,24},{24,20},{28,32},{32,28},{36,40... | collective-permute-start | bytes 98312 | tf_op jit(solution)/shard_map/ppermute | solution.py:509
  21.2 1.9 %shard_map.97 = (bf16[384,2048]{1,0:T(8,128)(2,1)S(1)}, f32[8,128]{1,0:T(8,128)S(1)}, bf16[2,9,128,128]{3,2,1,0:T(8,128)(2,1)S(1)}) custom-call(s32[2,1,512]{2,1,0:T(1,128)S(1)} %bitcast.14, s32[2,4,128]{2,1,0:T(4,128)S(1)} %copy-done.4, s32[2,8,384]{2,1,0:T(8,128)S(1)} %copy-done.5, bf16[2,2,9,128,128]{4,3,2,1,0:T(8,128)(2,1)} %constant.4.clone.tables), custom_call_target="tpu_custom_call" | custom-call | flops 805306368 | bytes 2000000 | tf_op jit(solution)/shard_map/pallas_call | solution.py:510
  23.1 0.0 collective-permute-done.rest_0_.pitch_near
  23.1 1.5 %collective-permute-done.1.rest_1_.pitch_far = f32[64,128]{1,0:T(8,128)S(1)} collective-permute-done((f32[64,128]{1,0:T(8,128)S(1)}, f32[64,128]{1,0:T(8,128)S(1)}, u32[]{:S(2)}, u32[]{:S(2)}) %collective-permute-start.1) | collective-permute-done | bytes 32800 | tf_op jit(solution)/shard_map/ppermute | solution.py:509
  24.6 2.1 %all-to-all-done = f32[96,4,128]{2,1,0:T(4,128)S(1)} async-done(((f32[96,4,128]{2,1,0:T(4,128)}), f32[96,4,128]{2,1,0:T(4,128)S(1)}, u32[]{:S(2)}, u32[]{:S(2)}) %all-to-all-start) | async-done | bytes 196640 | tf_op jit(solution)/shard_map/all_to_all | solution.py:468
  26.6 1.6 %shard_map.98.after = f32[384,128]{1,0:T(8,128)} custom-call(f32[384,128]{1,0:T(8,128)S(1)} %bitcast.10, bf16[2,9,128,128]{3,2,1,0:T(8,128)(2,1)S(1)} %get-tuple-element.21.weights, bf16[384,2048]{1,0:T(8,128)(2,1)S(1)} %get-tuple-element.22.place, f32[64,128]{1,0:T(8,128)S(1)} %collective-permute-done.rest_0_.pitch_near, ...), custom_call_target="tpu_custom_call" | custom-call | flops 200000000 | bytes 3000000 | tf_op jit(solution)/shard_map/pallas_call | solution.py:529
  28.3 4.9 %all-to-all-start.1 = ((f32[96,4,128]{2,1,0:T(4,128)}), f32[96,4,128]{2,1,0:T(4,128)S(1)}, u32[]{:S(2)}, u32[]{:S(2)}) async-start(f32[96,4,128]{2,1,0:T(4,128)} %bitcast.5), calls=%async_computation.1 | async-start | bytes 393216 | tf_op jit(solution)/shard_map/all_to_all | solution.py:468
  33.2 1.3 %collective-permute-start.2 = (f32[5,8,128]{2,1,0:T(8,128)S(1)}, f32[5,8,128]{2,1,0:T(8,128)S(1)}, u32[]{:S(2)}, u32[]{:S(2)}) collective-permute-start(f32[5,8,128]{2,1,0:T(8,128)S(1)} %get-tuple-element.23), channel_id=1, source_target_pairs={{0,1},{1,0},{2,3},{3,2},{4,5},{5,4},{6,7},{7,6},{8,9},{9,8},{10,11... | collective-permute-start | bytes 61448 | tf_op jit(solution)/shard_map/ppermute | solution.py:549
  34.5 1.9 %collective-permute-start.3 = (f32[5,8,128]{2,1,0:T(8,128)S(1)}, f32[5,8,128]{2,1,0:T(8,128)S(1)}, u32[]{:S(2)}, u32[]{:S(2)}) collective-permute-start(f32[5,8,128]{2,1,0:T(8,128)S(1)} %get-tuple-element.24), channel_id=1, source_target_pairs={{1,2},{2,1},{5,6},{6,5},{9,10},{10,9},{13,14},{14,13},{17,18},{18,... | collective-permute-start | bytes 61448 | tf_op jit(solution)/shard_map/ppermute | solution.py:550
  36.4 0.0 copy-done.6
  36.4 0.1 collective-permute-start.4
  36.5 0.6 %collective-permute-done.2.rad_near = f32[5,8,128]{2,1,0:T(8,128)S(1)} collective-permute-done((f32[5,8,128]{2,1,0:T(8,128)S(1)}, f32[5,8,128]{2,1,0:T(8,128)S(1)}, u32[]{:S(2)}, u32[]{:S(2)}) %collective-permute-start.2) | collective-permute-done | bytes 20512 | tf_op jit(solution)/shard_map/ppermute | solution.py:549
  37.1 3.1 %collective-permute-done.3.rad_far = f32[5,8,128]{2,1,0:T(8,128)S(1)} collective-permute-done((f32[5,8,128]{2,1,0:T(8,128)S(1)}, f32[5,8,128]{2,1,0:T(8,128)S(1)}, u32[]{:S(2)}, u32[]{:S(2)}) %collective-permute-start.3) | collective-permute-done | bytes 20512 | tf_op jit(solution)/shard_map/ppermute | solution.py:550
  40.2 4.5 %shard_map.99 = (f32[1,5,8,64,128]{4,3,2,1,0:T(8,128)}, f32[8,128]{1,0:T(8,128)S(1)}) custom-call(f32[3,5,1,5]{3,2,1,0:T(1,128)S(1)} %bitcast.13, f32[1,5,8,64,128]{4,3,2,1,0:T(8,128)} %flow.5, f32[1,5,64,128]{3,2,1,0:T(8,128)S(1)} %copy-done.1, f32[64,128]{1,0:T(8,128)S(1)} %collective-permute-done.rest_0_.pitch_near, ...), custom_call_target="tpu_custom_call" | custom-call | flops 20000000 | bytes 3000000 | tf_op jit(solution)/shard_map/pallas_call | solution.py:551
  44.7 0.0 collective-permute-done.4.jac
  44.7 0.0 all-to-all-done.1
  44.7 1.4 %shard_map.100 = (f32[5,64,128]{2,1,0:T(8,128)S(1)}, f32[5,8,128]{2,1,0:T(8,128)S(1)}, f32[5,8,128]{2,1,0:T(8,128)S(1)}) custom-call(f32[1,5,2,5]{3,2,1,0:T(2,128)S(1)} %collective-permute-done.4.jac, f32[384,128]{1,0:T(8,128)S(1)} %bitcast.11, f32[8,128]{1,0:T(8,128)S(1)} %get-tuple-element.27.terms, f32[8,128]{1,0:T(8,128)S(1)} %get-tuple-element.28.after), custom_call_target="tpu_custom_call" | custom-call | flops 8000000 | bytes 500000 | tf_op jit(solution)/shard_map/pallas_call | solution.py:574
  46.1 0.1 collective-permute-start.5
  46.2 1.1 %collective-permute-start.6 = (f32[5,8,128]{2,1,0:T(8,128)S(1)}, f32[5,8,128]{2,1,0:T(8,128)S(1)}, u32[]{:S(2)}, u32[]{:S(2)}) collective-permute-start(f32[5,8,128]{2,1,0:T(8,128)S(1)} %get-tuple-element.30), channel_id=1, source_target_pairs={{0,129},{1,128},{2,131},{3,130},{128,1},{129,0},{130,3},{131,2},{4... | collective-permute-start | bytes 61448 | tf_op jit(solution)/shard_map/ppermute | solution.py:583
  47.2 1.9 %collective-permute-start.7 = (f32[5,8,128]{2,1,0:T(8,128)S(1)}, f32[5,8,128]{2,1,0:T(8,128)S(1)}, u32[]{:S(2)}, u32[]{:S(2)}) collective-permute-start(f32[5,8,128]{2,1,0:T(8,128)S(1)} %get-tuple-element.31), channel_id=1, source_target_pairs={{1,130},{2,129},{129,2},{130,1},{5,134},{6,133},{133,6},{134,5},{9... | collective-permute-start | bytes 61448 | tf_op jit(solution)/shard_map/ppermute | solution.py:584
  49.1 0.3 collective-permute-done.6.near
  49.5 2.9 %collective-permute-done.7.far = f32[5,8,128]{2,1,0:T(8,128)S(1)} collective-permute-done((f32[5,8,128]{2,1,0:T(8,128)S(1)}, f32[5,8,128]{2,1,0:T(8,128)S(1)}, u32[]{:S(2)}, u32[]{:S(2)}) %collective-permute-start.7) | collective-permute-done | bytes 20512 | tf_op jit(solution)/shard_map/ppermute | solution.py:584
  52.3 0.0 collective-permute-done.5.main
  52.3 0.9 %shard_map.101 = f32[480,64]{1,0:T(8,128)} custom-call(f32[5,64,128]{2,1,0:T(8,128)S(1)} %collective-permute-done.5.main, f32[5,8,128]{2,1,0:T(8,128)S(1)} %collective-permute-done.6.near, f32[5,8,128]{2,1,0:T(8,128)S(1)} %collective-permute-done.7.far), custom_call_target="tpu_custom_call" | custom-call | flops 1000000 | bytes 800000 | tf_op jit(solution)/shard_map/pallas_call | solution.py:586
  (9 shorter events, 0.0 us)
Async XLA Ops:
  0.6 13.7 %copy-start = (f32[1,5,8,64,128]{4,3,2,1,0:T(8,128)S(1)}, f32[1,5,8,64,128]{4,3,2,1,0:T(8,128)}, u32[]{:S(2)}) copy-start(f32[1,5,8,64,128]{4,3,2,1,0:T(8,128)} %flow.5) | copy-start | bytes 3932164
  0.6 20.6 %copy-start.3 = (s32[2,512,1]{1,2,0:T(1,128)S(1)}, s32[2,512,1]{1,2,0:T(1,128)}, u32[]{:S(2)}) copy-start(s32[2,512,1]{1,2,0:T(1,128)} %param.13) | copy-start | bytes 12292
  0.7 20.6 %copy-start.4 = (s32[2,4,128]{2,1,0:T(4,128)S(1)}, s32[2,4,128]{2,1,0:T(4,128)}, u32[]{:S(2)}) copy-start(s32[2,4,128]{2,1,0:T(4,128)} %modes.1) | copy-start | bytes 12292
  0.7 20.6 %copy-start.5 = (s32[2,8,384]{2,1,0:T(8,128)S(1)}, s32[2,8,384]{2,1,0:T(8,128)}, u32[]{:S(2)}) copy-start(s32[2,8,384]{2,1,0:T(8,128)} %constant.5.clone.codes) | copy-start | bytes 73732
  2.8 23.8 %all-to-all-start = ((f32[96,4,128]{2,1,0:T(4,128)}), f32[96,4,128]{2,1,0:T(4,128)S(1)}, u32[]{:S(2)}, u32[]{:S(2)}) async-start(f32[96,4,128]{2,1,0:T(4,128)} %bitcast.2), calls=%async_computation | async-start | bytes 393216 | tf_op jit(solution)/shard_map/all_to_all | solution.py:468
  15.1 8.0 %collective-permute-start = (f32[64,128]{1,0:T(8,128)S(1)}, f32[64,128]{1,0:T(8,128)S(1)}, u32[]{:S(2)}, u32[]{:S(2)}) collective-permute-start(f32[64,128]{1,0:T(8,128)S(1)} %get-tuple-element.17), channel_id=1, source_target_pairs={{0,4},{4,0},{8,12},{12,8},{16,20},{20,16},{24,28},{28,24},{32,36},... | collective-permute-start | bytes 98312 | tf_op jit(solution)/shard_map/ppermute | solution.py:508
  17.0 7.6 %collective-permute-start.1 = (f32[64,128]{1,0:T(8,128)S(1)}, f32[64,128]{1,0:T(8,128)S(1)}, u32[]{:S(2)}, u32[]{:S(2)}) collective-permute-start(f32[64,128]{1,0:T(8,128)S(1)} %get-tuple-element.18), channel_id=1, source_target_pairs={{4,8},{8,4},{12,16},{16,12},{20,24},{24,20},{28,32},{32,28},{36,40... | collective-permute-start | bytes 98312 | tf_op jit(solution)/shard_map/ppermute | solution.py:509
  26.6 9.8 %copy-start.6 = (f32[1,2,5,5]{3,1,2,0:T(2,128)S(1)}, f32[1,2,5,5]{3,1,2,0:T(2,128)}, u32[]{:S(2)}) copy-start(f32[1,2,5,5]{3,1,2,0:T(2,128)} %param.11) | copy-start | bytes 604
  26.6 13.5 %copy-start.1 = (f32[1,5,64,128]{3,2,1,0:T(8,128)S(1)}, f32[1,5,64,128]{3,2,1,0:T(8,128)}, u32[]{:S(2)}) copy-start(f32[1,5,64,128]{3,2,1,0:T(8,128)} %inflow.1) | copy-start | bytes 491524
  26.6 13.5 %copy-start.2 = (f32[1,3,5,5]{3,0,2,1:T(1,128)S(1)}, f32[1,3,5,5]{3,0,2,1:T(1,128)}, u32[]{:S(2)}) copy-start(f32[1,3,5,5]{3,0,2,1:T(1,128)} %param.10) | copy-start | bytes 904
  28.3 16.4 %all-to-all-start.1 = ((f32[96,4,128]{2,1,0:T(4,128)}), f32[96,4,128]{2,1,0:T(4,128)S(1)}, u32[]{:S(2)}, u32[]{:S(2)}) async-start(f32[96,4,128]{2,1,0:T(4,128)} %bitcast.5), calls=%async_computation.1 | async-start | bytes 393216 | tf_op jit(solution)/shard_map/all_to_all | solution.py:468
  33.2 3.9 %collective-permute-start.2 = (f32[5,8,128]{2,1,0:T(8,128)S(1)}, f32[5,8,128]{2,1,0:T(8,128)S(1)}, u32[]{:S(2)}, u32[]{:S(2)}) collective-permute-start(f32[5,8,128]{2,1,0:T(8,128)S(1)} %get-tuple-element.23), channel_id=1, source_target_pairs={{0,1},{1,0},{2,3},{3,2},{4,5},{5,4},{6,7},{7,6},{8,9},{9,8},{10,11... | collective-permute-start | bytes 61448 | tf_op jit(solution)/shard_map/ppermute | solution.py:549
  34.5 5.7 %collective-permute-start.3 = (f32[5,8,128]{2,1,0:T(8,128)S(1)}, f32[5,8,128]{2,1,0:T(8,128)S(1)}, u32[]{:S(2)}, u32[]{:S(2)}) collective-permute-start(f32[5,8,128]{2,1,0:T(8,128)S(1)} %get-tuple-element.24), channel_id=1, source_target_pairs={{1,2},{2,1},{5,6},{6,5},{9,10},{10,9},{13,14},{14,13},{17,18},{18,... | collective-permute-start | bytes 61448 | tf_op jit(solution)/shard_map/ppermute | solution.py:550
  36.4 8.3 %collective-permute-start.4 = (f32[1,5,2,5]{3,2,1,0:T(2,128)S(1)}, f32[1,5,2,5]{3,2,1,0:T(2,128)S(1)}, u32[]{:S(2)}, u32[]{:S(2)}) collective-permute-start(f32[1,5,2,5]{3,2,1,0:T(2,128)S(1)} %bitcast.16), channel_id=1, source_target_pairs={{0,128},{128,0},{1,129},{129,1},{2,130},{130,2},{3,131},{131,3},{4... | collective-permute-start | bytes 608 | tf_op jit(solution)/shard_map/ppermute | solution.py:548
  46.1 6.3 %collective-permute-start.5 = (f32[5,64,128]{2,1,0:T(8,128)S(1)}, f32[5,64,128]{2,1,0:T(8,128)S(1)}, u32[]{:S(2)}, u32[]{:S(2)}) collective-permute-start(f32[5,64,128]{2,1,0:T(8,128)S(1)} %get-tuple-element.29), channel_id=1, source_target_pairs={{0,128},{128,0},{1,129},{129,1},{2,130},{130,2},{3,131},{131,3},{4... | collective-permute-start | bytes 491528 | tf_op jit(solution)/shard_map/ppermute | solution.py:585
  46.2 3.3 %collective-permute-start.6 = (f32[5,8,128]{2,1,0:T(8,128)S(1)}, f32[5,8,128]{2,1,0:T(8,128)S(1)}, u32[]{:S(2)}, u32[]{:S(2)}) collective-permute-start(f32[5,8,128]{2,1,0:T(8,128)S(1)} %get-tuple-element.30), channel_id=1, source_target_pairs={{0,129},{1,128},{2,131},{3,130},{128,1},{129,0},{130,3},{131,2},{4... | collective-permute-start | bytes 61448 | tf_op jit(solution)/shard_map/ppermute | solution.py:583
  47.2 5.1 %collective-permute-start.7 = (f32[5,8,128]{2,1,0:T(8,128)S(1)}, f32[5,8,128]{2,1,0:T(8,128)S(1)}, u32[]{:S(2)}, u32[]{:S(2)}) collective-permute-start(f32[5,8,128]{2,1,0:T(8,128)S(1)} %get-tuple-element.31), channel_id=1, source_target_pairs={{1,130},{2,129},{129,2},{130,1},{5,134},{6,133},{133,6},{134,5},{9... | collective-permute-start | bytes 61448 | tf_op jit(solution)/shard_map/ppermute | solution.py:584
